TPU v7x, 32 devices: a whole 2x2x4 slice. The times are simulated.
32 devices in a mesh: seq: 8 (over z, y), head: 4 (over x, core).
Axes of the slice: x: 2, y: 2, z: 4, core: 2. Of those that a mesh axis runs over, the one named last changes fastest.
Arguments:
- queries: bfloat16 [1280, 3072], P('seq', 'head'), may hold values from -240 to 240
- latent_rope: bfloat16 [1280, 576], P('seq'), may hold values from -4 to 4
- w_uk: bfloat16 [512, 2048], P(None, 'head'), may hold values from -0.25 to 0.25
- w_uv: bfloat16 [512, 2048], P(None, 'head'), may hold values from -0.25 to 0.25
- d_out: bfloat16 [1280, 2048], P('seq', 'head'), may hold values from -6 to 6
- block_order: int32 [16], replicated, may hold values from 0 to 15, as said below
- block_doc: int32 [16], replicated, may hold values from 0 to 2, never falling along the last dimension, each value on 1 to 8 neighbouring positions
Outputs:
- d_queries: bfloat16 [1280, 3072], P('seq', 'head')
- d_latent: float32 [1280, 576], P('seq')
- d_w_uk: float32 [512, 2048], P(None, 'head')
- d_w_uv: float32 [512, 2048], P(None, 'head')
Inputs may be any that keep to these rules, and one draw needn't show every extreme that they name: block_order holds every sequence block once, and block_order[2 s] + block_order[2 s + 1] = 15 for every s. `block_doc`: never falls along the sequence blocks.
All inputs are finite; a program needn't handle non-finite values.
Results may differ from a plain program's by a relative error of at most 0.017.
Values may be sent and summed in bfloat16 or wider, within the bound.
No kernel may reach another device: no remote copies, remote signals or barrier semaphores. Data moves between devices by JAX's collectives and lax.ppermute only.
A program may use at most 128 MiB of HBM per device.

v0:
```python
import jax
import jax.numpy as jnp
from jax import lax
from jax.sharding import PartitionSpec as P

D_LAT = 512
ROPE = 64
NOPE = 128
VDIM = 128


NEG_FILL = -1e30


def locate(row_index, half_rows, block_order, block_doc):
    slot_index = row_index // half_rows
    catalog = jnp.arange(block_order.shape[0], dtype=jnp.int32)
    picked = (slot_index[:, None] == catalog[None, :]).astype(jnp.int32)
    seq_block = jnp.sum(picked * block_order[None, :], axis=1)
    owning = (seq_block[:, None] == catalog[None, :]).astype(jnp.int32)
    document = jnp.sum(owning * block_doc[None, :], axis=1)
    return (seq_block * half_rows + row_index % half_rows, document)


def shards(queries, latent_rope, w_uk, w_uv, d_out, block_order, block_doc):
    local_rows = queries.shape[0]
    head_here = w_uk.shape[1] // NOPE
    width_query = NOPE + ROPE
    score_scale = width_query ** (-0.5)
    all_rows = local_rows * lax.axis_size("seq")
    half_rows = local_rows // 2
    first_query = lax.axis_index("seq") * local_rows
    query_pos, query_doc = locate(
        first_query + jnp.arange(local_rows, dtype=jnp.int32), half_rows, block_order, block_doc
    )
    query_heads = queries.reshape(local_rows, head_here, width_query)
    query_nope = query_heads[:, :, :NOPE]
    query_rope = query_heads[:, :, NOPE:]
    grad_out = d_out.reshape(local_rows, head_here, VDIM)
    key_width = head_here * NOPE
    piece_rows = lax.all_gather(latent_rope, "seq", axis=0, tiled=True)
    latent_part = piece_rows[:, :D_LAT]
    keys_up = jnp.dot(latent_part, w_uk, preferred_element_type=jnp.float32).astype(jnp.bfloat16)
    values_up = jnp.dot(latent_part, w_uv, preferred_element_type=jnp.float32).astype(jnp.bfloat16)
    gathered = jnp.concatenate([piece_rows, keys_up, values_up], axis=1)
    if all_rows % 512 == 0:
        block_rows = 512
    else:
        block_rows = 256
    block_total = all_rows // block_rows
    stacked = gathered.reshape(block_total, block_rows, gathered.shape[1])
    numbers = jnp.arange(block_total, dtype=jnp.int32)

    def unpack(packed, number):
        latent_part = packed[:, :D_LAT]
        key_rope = packed[:, D_LAT : D_LAT + ROPE]
        key_nope = packed[:, D_LAT + ROPE : D_LAT + ROPE + key_width].reshape(
            block_rows, head_here, NOPE
        )
        value_heads = packed[:, D_LAT + ROPE + key_width :].reshape(block_rows, head_here, VDIM)
        key_index = number * block_rows + jnp.arange(block_rows, dtype=jnp.int32)
        key_pos, key_doc = locate(key_index, half_rows, block_order, block_doc)
        visible = (query_pos[:, None] >= key_pos[None, :]) & (
            query_doc[:, None] == key_doc[None, :]
        )
        scores = jnp.einsum(
            "qhd,khd->hqk", query_nope, key_nope, preferred_element_type=jnp.float32
        )
        scores = scores + jnp.einsum(
            "qhd,kd->hqk", query_rope, key_rope, preferred_element_type=jnp.float32
        )
        scores = jnp.where(visible[None], scores * score_scale, NEG_FILL)
        return (latent_part, key_rope, key_nope, value_heads, visible, scores)

    def forward_step(carry, inputs):
        row_max, row_total, weighted = carry
        packed, number = inputs
        latent_part, key_rope, key_nope, value_heads, visible, scores = unpack(packed, number)
        new_max = jnp.maximum(row_max, jnp.max(scores, axis=2))
        expo = jnp.where(visible[None], jnp.exp(scores - new_max[:, :, None]), 0.0)
        shrink = jnp.exp(row_max - new_max)
        row_total = row_total * shrink + jnp.sum(expo, axis=2)
        update = jnp.einsum(
            "hqk,khd->hqd",
            expo.astype(jnp.bfloat16),
            value_heads,
            preferred_element_type=jnp.float32,
        )
        weighted = weighted * shrink[:, :, None] + update
        return ((new_max, row_total, weighted), None)

    start_forward = (
        jnp.full((head_here, local_rows), NEG_FILL, jnp.float32),
        jnp.zeros((head_here, local_rows), jnp.float32),
        jnp.zeros((head_here, local_rows, VDIM), jnp.float32),
    )
    (row_max, row_total, weighted), _ = lax.scan(forward_step, start_forward, (stacked, numbers))
    log_total = row_max + jnp.log(row_total)
    attended = weighted / row_total[:, :, None]
    delta = jnp.einsum("qhd,hqd->hq", grad_out.astype(jnp.float32), attended)

    def backward_step(carry, inputs):
        grad_nope, grad_rope, grad_wk, grad_wv = carry
        packed, number = inputs
        latent_part, key_rope, key_nope, value_heads, visible, scores = unpack(packed, number)
        attention = jnp.where(visible[None], jnp.exp(scores - log_total[:, :, None]), 0.0)
        grad_probs = jnp.einsum(
            "qhd,khd->hqk", grad_out, value_heads, preferred_element_type=jnp.float32
        )
        grad_scores = (attention * (grad_probs - delta[:, :, None]) * score_scale).astype(
            jnp.bfloat16
        )
        attention_low = attention.astype(jnp.bfloat16)
        grad_nope = grad_nope + jnp.einsum(
            "hqk,khd->qhd", grad_scores, key_nope, preferred_element_type=jnp.float32
        )
        grad_rope = grad_rope + jnp.einsum(
            "hqk,kd->qhd", grad_scores, key_rope, preferred_element_type=jnp.float32
        )
        key_grad_nope = jnp.einsum(
            "hqk,qhd->khd", grad_scores, query_nope, preferred_element_type=jnp.float32
        )
        key_grad_nope = key_grad_nope.astype(jnp.bfloat16).reshape(block_rows, key_width)
        key_grad_rope = jnp.einsum(
            "hqk,qhd->kd", grad_scores, query_rope, preferred_element_type=jnp.float32
        )
        value_grad = jnp.einsum(
            "hqk,qhd->khd", attention_low, grad_out, preferred_element_type=jnp.float32
        )
        value_grad = value_grad.astype(jnp.bfloat16).reshape(block_rows, head_here * VDIM)
        by_columns = (((1,), (1,)), ((), ()))
        by_rows = (((0,), (0,)), ((), ()))
        latent_grad = lax.dot_general(
            key_grad_nope, w_uk, by_columns, preferred_element_type=jnp.float32
        )
        latent_grad = latent_grad + lax.dot_general(
            value_grad, w_uv, by_columns, preferred_element_type=jnp.float32
        )
        grad_wk = grad_wk + lax.dot_general(
            latent_part, key_grad_nope, by_rows, preferred_element_type=jnp.float32
        )
        grad_wv = grad_wv + lax.dot_general(
            latent_part, value_grad, by_rows, preferred_element_type=jnp.float32
        )
        return (
            (grad_nope, grad_rope, grad_wk, grad_wv),
            jnp.concatenate([latent_grad, key_grad_rope], axis=1),
        )

    start_backward = (
        jnp.zeros((local_rows, head_here, NOPE), jnp.float32),
        jnp.zeros((local_rows, head_here, ROPE), jnp.float32),
        jnp.zeros((D_LAT, key_width), jnp.float32),
        jnp.zeros((D_LAT, head_here * VDIM), jnp.float32),
    )
    (grad_nope, grad_rope, grad_wk, grad_wv), pieces = lax.scan(
        backward_step, start_backward, (stacked, numbers)
    )
    d_queries = jnp.concatenate([grad_nope, grad_rope], axis=2).reshape(
        local_rows, head_here * width_query
    )
    d_queries = d_queries.astype(jnp.bfloat16)
    latent_terms = pieces.reshape(all_rows, D_LAT + ROPE)
    shares = lax.psum_scatter(
        latent_terms.astype(jnp.bfloat16), "seq", scatter_dimension=0, tiled=True
    )
    d_latent = lax.psum(shares, "head").astype(jnp.float32)
    d_w_uk, d_w_uv = (
        lax.psum(grad_wk.astype(jnp.bfloat16), "seq").astype(jnp.float32),
        lax.psum(grad_wv.astype(jnp.bfloat16), "seq").astype(jnp.float32),
    )
    return (d_queries, d_latent, d_w_uk, d_w_uv)


def solution(mesh):
    return jax.shard_map(
        shards,
        mesh=mesh,
        in_specs=(
            P("seq", "head"),
            P("seq", None),
            P(None, "head"),
            P(None, "head"),
            P("seq", "head"),
            P(),
            P(),
        ),
        out_specs=(P("seq", "head"), P("seq", None), P(None, "head"), P(None, "head")),
        check_vma=False,
    )
```

profile of v0, /device:TPU:0, one launch (start us, length us, event | category | flops | bytes accessed | tf_op | source)
XLA Modules:
  0.0 333.6 jit_solution(13051993929053484380)
XLA Ops:
  7.3 0.7 all-gather.2.cloned.1.call-update
  8.0 1.1 copy.45
  9.2 0.7 slice.69
  9.9 0.7 reshape.253
  10.6 1.1 copy.49
  12.0 0.9 copy_bitcast_fusion
  12.9 44.6 %all-gather.2.cloned.1.call-done = bf16[1280,576]{1,0:T(8,128)(2,1)} async-done(((bf16[160,576]{1,0:T(8,128)(2,1)}), bf16[1280,576]{1,0:T(8,128)(2,1)}) %all-gather.2.cloned.1.call-update) | async-done | bytes 1474576 | tf_op jit(solution)/shard_map/all_gather | solution.py:41
  57.5 3.3 convolution_convert_fusion.2
  60.8 2.4 copy.44
  63.2 3.4 %convolution_convert_fusion.3 = bf16[1280,512]{0,1:T(8,128)(2,1)} fusion(bf16[512,512]{1,0:T(8,128)(2,1)} %param.13, bf16[1280,576]{1,0:T(8,128)(2,1)} %all-gather.2.cloned.1.call-done), kind=kOutput, calls=%fused_computation.73 | convolution fusion | flops 671744000 | bytes 3145728 | tf_op jit(solution)/shard_map/dot_general | solution.py:43
  66.6 2.4 copy.43
  69.0 8.3 %concatenate.13 = bf16[1280,1600]{1,0:T(8,128)(2,1)} concatenate(bf16[1280,576]{1,0:T(8,128)(2,1)} %all-gather.2.cloned.1.call-done, bf16[1280,512]{1,0:T(8,128)(2,1)} %copy.43, bf16[1280,512]{1,0:T(8,128)(2,1)} %copy.44), dimensions={1} | concatenate | bytes 8192000 | tf_op jit(solution)/shard_map/concatenate | solution.py:45
  77.4 6.9 %copy.48 = bf16[5,256,1600]{1,2,0:T(8,128)(2,1)} copy(bf16[5,256,1600]{2,1,0:T(8,128)(2,1)} %bitcast.203) | data formatting | bytes 8192000
  84.3 21.5 %while.38 = (s32[]{:T(128)}, f32[4,160]{1,0:T(4,128)S(1)}, f32[4,160]{1,0:T(4,128)S(1)}, f32[4,160,128]{2,1,0:T(8,128)S(1)}, s32[160]{0:T(256)S(1)}, /*index=5*/...) while((s32[]{:T(128)}, f32[4,160]{1,0:T(4,128)S(1)}, ...), condition=%wide.region_7.8_spmd.clone, body=%wide.region_2.7_spmd.clone.sunk | while | flops 106896512 | bytes 7686725 | solution.py:97
  84.3 0.6 dynamic_slice.37
  85.9 1.2 dynamic-slice_bitcast_fusion.4
  87.4 0.4 fusion.115
  88.6 0.6 dynamic_slice.37
  90.2 1.2 dynamic-slice_bitcast_fusion.4
  91.7 0.4 fusion.115
  92.9 0.6 dynamic_slice.37
  94.5 1.2 dynamic-slice_bitcast_fusion.4
  96.1 0.4 fusion.115
  97.2 0.6 dynamic_slice.37
  98.8 1.2 dynamic-slice_bitcast_fusion.4
  100.4 0.4 fusion.115
  101.6 0.6 dynamic_slice.37
  103.1 1.2 dynamic-slice_bitcast_fusion.4
  106.0 1.2 multiply_reduce_fusion
  107.4 38.8 %while.39 = (s32[]{:T(128)}, f32[160,4,128]{2,0,1:T(8,128)}, f32[160,4,64]{0,2,1:T(8,128)}, f32[512,512]{1,0:T(8,128)S(1)}, f32[512,512]{1,0:T(8,128)S(1)}, /*in...) while((s32[]{:T(128)}, f32[160,4,128]{2,0,1:T(8,128)}, ...), condition=%wide.region_11.12_spmd.clone, body=%wide.region_8.11_spmd.clone.sunk | while | flops 813699072 | bytes 25837324 | solution.py:156
  107.4 0.6 dynamic_slice.39
  109.0 1.2 dynamic-slice_bitcast_fusion.5
  113.4 0.5 convolution_add_fusion.10
  113.9 0.5 convolution_add_fusion.9
  114.4 0.8 fusion.147
  115.2 0.6 dynamic_slice.39
  116.7 1.2 dynamic-slice_bitcast_fusion.5
  121.2 0.5 convolution_add_fusion.10
  121.7 0.5 convolution_add_fusion.9
  122.1 0.8 fusion.147
  122.9 0.6 dynamic_slice.39
  124.5 1.2 dynamic-slice_bitcast_fusion.5
  129.0 0.5 convolution_add_fusion.10
  129.4 0.5 convolution_add_fusion.9
  129.9 0.8 fusion.147
  130.7 0.6 dynamic_slice.39
  132.3 1.2 dynamic-slice_bitcast_fusion.5
  136.7 0.5 convolution_add_fusion.10
  137.2 0.5 convolution_add_fusion.9
  137.7 0.8 fusion.147
  138.5 0.6 dynamic_slice.39
  140.0 1.2 dynamic-slice_bitcast_fusion.5
  144.5 0.5 convolution_add_fusion.10
  145.0 0.5 convolution_add_fusion.9
  145.4 0.8 fusion.147
  146.3 0.9 convert_element_type.80
  147.1 0.9 convert_element_type.82
  148.4 62.2 %reduce-scatter.2.cloned.1.call-done = bf16[160,576]{1,0:T(8,128)(2,1)} async-done(((bf16[1280,576]{1,0:T(8,128)(2,1)}), bf16[160,576]{1,0:T(8,128)(2,1)}) %reduce-scatter.2.cloned.1.call-update) | async-done | bytes 184336 | tf_op jit(solution)/shard_map/reduce_scatter | solution.py:164
  210.9 1.0 convert_element_type.76
  211.9 80.7 %all-reduce.6.cloned.1.call-done = (bf16[512,512]{1,0:T(8,128)(2,1)}, bf16[512,512]{1,0:T(8,128)(2,1)}) async-done(((bf16[512,512]{1,0:T(8,128)(2,1)}, bf16[512,512]{1,0:T(8,128)(2,1)}), (bf16[512,512]{1,0:T(8,128)(2,1)}, bf16[512,512]{1,0:T(8,128)(2,1)})) %all-reduce.6.cloned.1.call-update) | async-done | bytes 1048592 | tf_op jit(solution)/shard_map/psum | solution.py:169
  292.6 2.2 convert_element_type.81
  294.9 1.1 convert_element_type.83
  296.0 29.4 %all-reduce.4.cloned.1.call-done = bf16[160,576]{1,0:T(8,128)(2,1)} async-done(((bf16[160,576]{1,0:T(8,128)(2,1)}), bf16[160,576]{1,0:T(8,128)(2,1)}) %all-reduce.4.cloned.1.call-update) | async-done | bytes 184336 | tf_op jit(solution)/shard_map/psum | solution.py:167
  325.4 1.7 convert_element_type.79
  (235 shorter events, 26.0 us)
Async XLA Ops:
  7.2 2.7 copy-start.8
  7.2 4.6 %copy-start.10 = (s32[16]{0:T(128)S(1)}, s32[16]{0:T(128)}, u32[]{:S(2)}) copy-start(s32[16]{0:T(128)} %param.16) | copy-start | bytes 196
  7.2 4.7 %copy-start.11 = (s32[16]{0:T(128)S(1)}, s32[16]{0:T(128)}, u32[]{:S(2)}) copy-start(s32[16]{0:T(128)} %param.17) | copy-start | bytes 196
  7.2 50.3 %copy-start = (bf16[512,512]{1,0:T(8,128)(2,1)S(1)}, bf16[512,512]{1,0:T(8,128)(2,1)}, u32[]{:S(2)}) copy-start(bf16[512,512]{1,0:T(8,128)(2,1)} %param.14) | copy-start | bytes 1572868
  7.2 50.3 %all-gather.2.cloned.1.call-start = ((), (), s32[]{:S(2)}) async-start(), calls=%async_computation.1 | async-start | bytes 1843200 | tf_op jit(solution)/shard_map/all_gather | solution.py:41
  7.9 202.6 %reduce-scatter.2.cloned.1.call-start = ((), (), s32[]{:S(2)}) async-start(), calls=%async_computation.2 | async-start | bytes 1843200 | tf_op jit(solution)/shard_map/reduce_scatter | solution.py:164
  110.8 1.0 copy-start.2
  111.1 1.3 copy-start.5
  111.4 1.3 copy-start.1
  112.1 1.3 copy-start.3
  112.7 1.2 copy-start.6
  118.6 1.0 copy-start.2
  118.9 1.3 copy-start.5
  119.2 1.3 copy-start.1
  119.9 1.3 copy-start.3
  120.5 1.2 copy-start.6
  126.4 1.0 copy-start.2
  126.6 1.3 copy-start.5
  126.9 1.3 copy-start.1
  127.7 1.3 copy-start.3
  128.2 1.2 copy-start.6
  134.1 1.0 copy-start.2
  134.4 1.3 copy-start.5
  134.7 1.3 copy-start.1
  135.4 1.3 copy-start.3
  136.0 1.2 copy-start.6
  141.9 1.0 copy-start.2
  142.2 1.3 copy-start.5
  142.5 1.3 copy-start.1
  143.2 1.3 copy-start.3
  143.8 1.2 copy-start.6
  146.2 146.4 %all-reduce.6.cloned.1.call-start = ((), (), s32[]{:S(2)}) async-start(), calls=%async_computation.4 | async-start | bytes 2097152 | tf_op jit(solution)/shard_map/psum | solution.py:169
  147.1 0.9 copy-start.7
  147.1 1.2 copy-start.4
  148.0 177.3 %all-reduce.4.cloned.1.call-start = ((), (), s32[]{:S(2)}) async-start(), calls=%async_computation.3 | async-start | bytes 409600 | tf_op jit(solution)/shard_map/psum | solution.py:167
  292.6 2.2 copy-start.9
Sparse Core Ops, SparseCore 0:
  10.2 47.2 all-gather.1
  146.4 64.1 reduce-scatter.1
  215.1 77.4 all-reduce.5
  294.8 30.4 all-reduce.3
where the time goes:
time: 335 us; the launch traced here: 334 us
  waiting for transfers between devices  218 us (65%)
  local copies, waits for them, and re-layouts  45.1 us (13%)
  matrix products  31.5 us (9%)
  other arithmetic  17.5 us (5%)
  between operations  14 us (4%)
  loops' own time  7.75 us (2%)
    psum x1, waiting for transfers between devices, shards(): lax.psum(grad_wk.astype(jnp.bfloat16), 'seq').astype(jnp.float32)  80.7 us
    reduce_scatter x1, waiting for transfers between devices, shards(): lax.psum_scatter(latent_terms.astype(jnp.bfloat16), 'seq', scatter_dimens...  62.2 us
    all_gather x1, waiting for transfers between devices, shards(): piece_rows = lax.all_gather(latent_rope, 'seq', axis=0, tiled=True)  44.6 us
    psum x1, waiting for transfers between devices, shards(): d_latent = lax.psum(shares, 'head').astype(jnp.float32)  29.4 us
    squeeze x10, local copies, waits for them, and re-layouts, shards(): lax.scan(forward_step, start_forward, (stacked, numbers))  12 us
    unnamed x18, local copies, waits for them, and re-layouts  10.2 us
    concatenate x1, local copies, waits for them, and re-layouts, shards(): gathered = jnp.concatenate([piece_rows, keys_up, values_up], axis=1)  8.35 us
  transfers between devices with their start and end apart: 4, of which 4 were waited for; matrix products, arithmetic and copies ran while one was open for 3% of the time, Pallas kernels for 0%

commit v1 on v0

v1 whole, which is shorter than its diff:
```python
import functools
import math

import jax
import jax.numpy as jnp
from jax import lax
from jax.experimental import pallas as pl
from jax.experimental.pallas import tpu as pltpu
from jax.sharding import PartitionSpec as P

D_LAT = 512
ROPE = 64
NOPE = 128
VDIM = 128
WIDTH = NOPE + ROPE
SCALE = WIDTH ** (-0.5)
SCALE_LOG2 = SCALE * math.log2(math.e)
NEG_FILL = -1e30
TILE = 256
VMEM_BYTES = 60 * 1024 * 1024
BY_COLUMNS = (((1,), (1,)), ((), ()))
BY_ROWS = (((1,), (0,)), ((), ()))
SMEM = pl.BlockSpec(memory_space=pltpu.SMEM)
VMEM = pl.BlockSpec(memory_space=pltpu.VMEM)
HBM = pl.BlockSpec(memory_space=pl.ANY)


def dot(a, b, dims):
    return lax.dot_general(a, b, dims, preferred_element_type=jnp.float32)


def head_queries(x_ref, rows, head, nope_at, rope_at):
    nope = x_ref[rows, nope_at + head * NOPE : nope_at + (head + 1) * NOPE]
    rope = x_ref[rows, rope_at + head * ROPE : rope_at + (head + 1) * ROPE]
    return jnp.concatenate([nope, rope], axis=1)


def project_kernel(
    masks, half, heads, order_ref, low_ref, where_ref, mine_ref, other_ref, wk_ref, wv_ref, x_ref,
    keys_ref, values_ref, turned_ref, dq_ref, latent, sem,
):
    blocks = 2 * len(masks)
    total = blocks * half
    me, core = where_ref[0], where_ref[1]
    copies = []
    for number, mask in enumerate(masks):
        for side, source in enumerate((mine_ref, other_ref)):
            block = order_ref[2 * (me ^ mask) + (core ^ side)]
            target = latent.at[pl.ds(pl.multiple_of(block * half, 16), half), :]
            copy = pltpu.make_async_copy(
                source.at[pl.ds(number * half, half), :], target, sem.at[2 * number + side]
            )
            copy.start()
            copies.append(copy)
    for copy in copies:
        copy.wait()
    for first in range(0, total, TILE):
        rows = pl.ds(first, TILE)
        part = latent[rows, :D_LAT]
        rope = latent[rows, D_LAT:]
        up_keys = dot(part, wk_ref[...], BY_ROWS).astype(jnp.bfloat16)
        for head in range(heads):
            keys_ref[head, rows, :] = jnp.concatenate(
                [up_keys[:, head * NOPE : (head + 1) * NOPE], rope], axis=1
            )
        values_ref[rows, :] = dot(part, wv_ref[...], BY_ROWS).astype(jnp.bfloat16)
        turned_ref[:, first : first + TILE] = part.T
    span = (blocks // 2) * half
    rope_at = heads * NOPE
    grad_at = heads * WIDTH
    for side in range(2):
        block = order_ref[2 * me + side]
        start = pl.multiple_of(jnp.maximum(block - (blocks // 2 - 1), 0) * half, 16)
        window = pl.ds(start, span)
        key_pos = start + lax.broadcasted_iota(jnp.int32, (half, span), 1)
        query_pos = block * half + lax.broadcasted_iota(jnp.int32, (half, span), 0)
        seen = (key_pos <= query_pos) & (key_pos >= low_ref[block] * half)
        bias = jnp.where(seen, 0.0, NEG_FILL)
        rows = pl.ds(side * half, half)
        outs = []
        for head in range(heads):
            query = head_queries(x_ref, rows, head, 0, rope_at)
            grad = x_ref[rows, grad_at + head * VDIM : grad_at + (head + 1) * VDIM]
            keys = keys_ref[head, window, :]
            values = values_ref[window, head * VDIM : (head + 1) * VDIM]
            scores = dot(query, keys, BY_COLUMNS) * SCALE_LOG2 + bias
            expo = jnp.exp2(scores - jnp.max(scores, axis=1, keepdims=True))
            probs = expo * (1.0 / jnp.sum(expo, axis=1, keepdims=True))
            grad_probs = dot(grad, values, BY_COLUMNS)
            delta = jnp.sum(probs * grad_probs, axis=1, keepdims=True)
            grad_scores = (probs * (grad_probs - delta) * SCALE).astype(jnp.bfloat16)
            outs.append(dot(grad_scores, keys, BY_ROWS).astype(jnp.bfloat16))
        dq_ref[rows, :] = jnp.concatenate(outs, axis=1)


def key_kernel(masks, half, heads, first_head, here, order_ref, where_ref, *refs):
    count = len(masks)
    x_refs = refs[:count]
    low_ref, keys_ref, values_ref, wk_ref, wv_ref = refs[count : count + 5]
    dk_ref, dv_ref, dlat_ref = refs[count + 5 : count + 8]
    x_all, sum_nope, sum_value, sum_rope, sem = refs[count + 8 :]
    blocks = 2 * count
    total = blocks * half
    me = where_ref[0]
    rope_at = here * NOPE
    grad_at = rope_at + heads * ROPE
    if here == heads:
        columns = ((0, 0, heads * (WIDTH + VDIM)),)
    else:
        columns = (
            (first_head * NOPE, 0, here * NOPE),
            (heads * NOPE, rope_at, heads * ROPE),
            (heads * WIDTH + first_head * VDIM, grad_at, here * VDIM),
        )
    copies = []
    for number, mask in enumerate(masks):
        for side in range(2):
            block = order_ref[2 * (me ^ mask) + side]
            rows = pl.ds(pl.multiple_of(block * half, 16), half)
            for piece, (source, target, wide) in enumerate(columns):
                copy = pltpu.make_async_copy(
                    x_refs[number].at[pl.ds(side * half, half), pl.ds(source, wide)],
                    x_all.at[rows, pl.ds(target, wide)],
                    sem.at[(2 * number + side) * len(columns) + piece],
                )
                copy.start()
                copies.append(copy)
    sum_nope[...] = jnp.zeros_like(sum_nope)
    sum_value[...] = jnp.zeros_like(sum_value)
    sum_rope[...] = jnp.zeros_like(sum_rope)
    for copy in copies:
        copy.wait()

    def tile(first, start, span):
        window = pl.ds(start, span)
        rows = pl.ds(first, TILE)
        key_pos = start + lax.broadcasted_iota(jnp.int32, (span, TILE), 0)
        query_pos = first + lax.broadcasted_iota(jnp.int32, (span, TILE), 1)
        seen = (key_pos <= query_pos) & (key_pos >= low_ref[:, rows])
        bias = jnp.where(seen, 0.0, NEG_FILL)
        for head in range(here):
            lanes = slice(head * NOPE, (head + 1) * NOPE)
            query = jnp.concatenate(
                [
                    x_all[rows, lanes],
                    x_all[rows, rope_at + (first_head + head) * ROPE : rope_at + (first_head + head + 1) * ROPE],
                ],
                axis=1,
            )
            grad = x_all[rows, grad_at + head * VDIM : grad_at + (head + 1) * VDIM]
            keys = keys_ref[head, window, :]
            values = values_ref[window, lanes]
            scores = dot(keys, query, BY_COLUMNS) * SCALE_LOG2 + bias
            expo = jnp.exp2(scores - jnp.max(scores, axis=0, keepdims=True))
            probs = expo * (1.0 / jnp.sum(expo, axis=0, keepdims=True))
            grad_probs = dot(values, grad, BY_COLUMNS)
            delta = jnp.sum(probs * grad_probs, axis=0, keepdims=True)
            grad_scores = (probs * (grad_probs - delta) * SCALE).astype(jnp.bfloat16)
            sum_value[window, lanes] += dot(probs.astype(jnp.bfloat16), grad, BY_ROWS)
            key_grad = dot(grad_scores, query, BY_ROWS)
            sum_nope[window, lanes] += key_grad[:, :NOPE]
            sum_rope[window, :] += key_grad[:, NOPE:]

    reach = (blocks // 2 - 1) * half
    if total <= 8 * TILE:
        for first in range(0, total, TILE):
            start = max(first // half * half - reach, 0)
            tile(first, start, first + TILE - start)
    else:
        span = -(-(reach + half + TILE) // 16) * 16

        def step(number, carry):
            first = pl.multiple_of(number * TILE, TILE)
            start = jnp.clip(first + TILE - span, 0, total - span)
            tile(first, pl.multiple_of(start, 16), span)
            return carry

        lax.fori_loop(0, total // TILE, step, 0)
    dk_ref[...] = sum_nope[...].astype(jnp.bfloat16)
    dv_ref[...] = sum_value[...].astype(jnp.bfloat16)
    for side in range(2):
        block = order_ref[2 * me + side]
        rows = pl.ds(pl.multiple_of(block * half, 16), half)
        out = dot(dk_ref[rows, :], wk_ref[...], BY_COLUMNS)
        out = out + dot(dv_ref[rows, :], wv_ref[...], BY_COLUMNS)
        dlat_ref[pl.ds(side * half, half), :] = jnp.concatenate([out, sum_rope[rows, :]], axis=1)


def swap(array, axis, mask):
    size = lax.axis_size(axis)
    return lax.ppermute(array, axis, [(i, i ^ mask) for i in range(size)])


def shards(queries, latent_rope, w_uk, w_uv, d_out, block_order, block_doc):
    local_rows = queries.shape[0]
    heads = w_uk.shape[1] // NOPE
    devices = lax.axis_size("seq")
    half = local_rows // 2
    total = local_rows * devices
    me = lax.axis_index("seq")
    core = lax.axis_index("head") % 2
    where = jnp.stack([me, core]).astype(jnp.int32)
    low = jnp.sum((block_doc[None, :] < block_doc[:, None]).astype(jnp.int32), axis=1)
    low_rows = jnp.repeat(low * half, half).reshape(1, total)

    latent_masks = [0]
    mine = lax.dynamic_slice_in_dim(latent_rope, core * half, half, axis=0)
    step = devices // 2
    while step:
        mine = jnp.concatenate([mine, swap(mine, "seq", step)], axis=0)
        latent_masks = latent_masks + [m ^ step for m in latent_masks]
        step //= 2
    other = swap(mine, "head", 1)

    by_head = queries.reshape(local_rows, heads, WIDTH)
    packed = jnp.concatenate(
        [
            by_head[:, :, :NOPE].reshape(local_rows, heads * NOPE),
            by_head[:, :, NOPE:].reshape(local_rows, heads * ROPE),
            d_out,
        ],
        axis=1,
    )
    far = [packed] + [swap(packed, "seq", m) for m in range(2, devices, 2)]
    near = [swap(x, "seq", 1) for x in far]
    pieces = far + near
    masks = list(range(0, devices, 2)) + list(range(1, devices, 2))

    bf16 = jnp.bfloat16
    params = pltpu.CompilerParams(vmem_limit_bytes=VMEM_BYTES)
    keys, values, turned, d_queries = pl.pallas_call(
        functools.partial(project_kernel, latent_masks, half, heads),
        out_shape=(
            jax.ShapeDtypeStruct((heads, total, WIDTH), bf16),
            jax.ShapeDtypeStruct((total, heads * VDIM), bf16),
            jax.ShapeDtypeStruct((D_LAT, total), bf16),
            jax.ShapeDtypeStruct((local_rows, heads * WIDTH), bf16),
        ),
        in_specs=[SMEM, SMEM, SMEM, HBM, HBM, VMEM, VMEM, VMEM],
        out_specs=(VMEM, VMEM, VMEM, VMEM),
        scratch_shapes=[
            pltpu.VMEM((total, D_LAT + ROPE), bf16),
            pltpu.SemaphoreType.DMA((2 * devices,)),
        ],
        compiler_params=params,
        name="project",
    )(block_order, low, where, mine, other, w_uk, w_uv, packed)

    here = heads if total <= 8 * TILE else 1
    parts = 1 if here == heads else 3
    dks, dvs, dlat = [], [], 0.0
    for first_head in range(0, heads, here):
        lanes = slice(first_head * NOPE, (first_head + here) * NOPE)
        dk, dv, share = pl.pallas_call(
            functools.partial(key_kernel, masks, half, heads, first_head, here),
            out_shape=(
                jax.ShapeDtypeStruct((total, here * NOPE), bf16),
                jax.ShapeDtypeStruct((total, here * VDIM), bf16),
                jax.ShapeDtypeStruct((local_rows, D_LAT + ROPE), jnp.float32),
            ),
            in_specs=[SMEM, SMEM] + [HBM] * devices + [VMEM] * 5,
            out_specs=(VMEM, VMEM, VMEM),
            scratch_shapes=[
                pltpu.VMEM((total, here * (NOPE + VDIM) + heads * ROPE), bf16),
                pltpu.VMEM((total, here * NOPE), jnp.float32),
                pltpu.VMEM((total, here * VDIM), jnp.float32),
                pltpu.VMEM((total, ROPE), jnp.float32),
                pltpu.SemaphoreType.DMA((2 * devices * parts,)),
            ],
            compiler_params=params,
            name="keys",
        )(
            block_order, where, *pieces, low_rows,
            keys[first_head : first_head + here], values[:, lanes], w_uk[:, lanes], w_uv[:, lanes],
        )
        dks.append(dk)
        dvs.append(dv)
        dlat = dlat + share
    dk = jnp.concatenate(dks, axis=1)
    dv = jnp.concatenate(dvs, axis=1)
    step = 1
    while step < lax.axis_size("head"):
        sent = dlat.astype(bf16)
        dlat = sent.astype(jnp.float32) + swap(sent, "head", step).astype(jnp.float32)
        step *= 2
    return (d_queries, dlat, dot(turned, dk, BY_ROWS), dot(turned, dv, BY_ROWS))


def solution(mesh):
    return jax.shard_map(
        shards,
        mesh=mesh,
        in_specs=(
            P("seq", "head"),
            P("seq", None),
            P(None, "head"),
            P(None, "head"),
            P("seq", "head"),
            P(),
            P(),
        ),
        out_specs=(P("seq", "head"), P("seq", None), P(None, "head"), P(None, "head")),
        check_vma=False,
    )
```

time: 335 us -> 111 us (0.33)
  waiting for transfers between devices: 218 us -> 50.8 us
  local copies, waits for them, and re-layouts: 45.1 us -> 4 us
  Pallas kernels: 0 us -> 30.3 us
  matrix products: 31.5 us -> 5.06 us
  starting transfers between devices: 0.16 us -> 17.1 us
  other arithmetic: 17.5 us -> 2.83 us
  between operations: 14 us -> 0.9 us
  loops' own time: 7.75 us -> 0 us
    psum x2 -> x0, waiting for transfers between devices: 110 us -> none  [the longest x1 80.7 us: shards(): lax.psum(grad_wk.astype(jnp.bfloat16), 'seq').astype(jnp.float32)]
    reduce_scatter x1 -> x0, waiting for transfers between devices: 62.2 us -> none  [shards(): lax.psum_scatter(latent_terms.astype(jnp.bfloat16), 'seq', scatter_dimens...]
    ppermute x0 -> x13, waiting for transfers between devices: none -> 50.8 us  [swap(): return lax.ppermute(array, axis, [(i, i ^ mask) for i in range(size)])]
    all_gather x1 -> x0, waiting for transfers between devices: 44.6 us -> none  [shards(): piece_rows = lax.all_gather(latent_rope, 'seq', axis=0, tiled=True)]
    pallas_call x0 -> x2, Pallas kernels: none -> 30.3 us  [the longest x1 20.7 us: shards(): pl.pallas_call(functools.partial(key_kernel, masks, half, heads, first_he...]
    dot_general x77 -> x2, matrix products: 31.5 us -> 5.06 us  [dot(): return lax.dot_general(a, b, dims, preferred_element_type=jnp.float32)]
    ppermute x0 -> x13, starting transfers between devices: none -> 17.1 us  [swap(): return lax.ppermute(array, axis, [(i, i ^ mask) for i in range(size)])]
    squeeze x10 -> x0, local copies, waits for them, and re-layouts: 12 us -> none  [shards(): lax.scan(forward_step, start_forward, (stacked, numbers))]
  transfers between devices with their start and end apart: 4 -> 13, of which waited for: 4 -> 7; matrix products, arithmetic and copies ran while one was open for 3% -> 8% of each run, Pallas kernels for 0% -> 9%
where the time goes in v1:
time: 111 us
  waiting for transfers between devices  50.8 us (46%)
  Pallas kernels  30.3 us (27%)
  starting transfers between devices  17.1 us (15%)
  matrix products  5.06 us (5%)
  local copies, waits for them, and re-layouts  4 us (4%)
  other arithmetic  2.83 us (3%)
    ppermute x13, waiting for transfers between devices, swap(): return lax.ppermute(array, axis, [(i, i ^ mask) for i in range(size)])  50.8 us
    pallas_call x1, Pallas kernels, shards(): pl.pallas_call(functools.partial(key_kernel, masks, half, heads, first_he...  20.7 us
    ppermute x13, starting transfers between devices, swap(): return lax.ppermute(array, axis, [(i, i ^ mask) for i in range(size)])  17.1 us
    pallas_call x1, Pallas kernels, shards(): pl.pallas_call(functools.partial(project_kernel, latent_masks, half, head...  9.66 us
    dot_general x2, matrix products, dot(): return lax.dot_general(a, b, dims, preferred_element_type=jnp.float32)  5.06 us
  transfers between devices with their start and end apart: 13, of which 7 were waited for; matrix products, arithmetic and copies ran while one was open for 8% of the time, Pallas kernels for 9%

profile of v1, /device:TPU:0, one launch (start us, length us, event | category | flops | bytes accessed | tf_op | source)
XLA Modules:
  0.0 111.0 jit_solution(11076083584558521575)
XLA Ops:
  0.6 0.0 copy-start
  0.6 0.0 copy-start.5
  0.7 0.9 copy-done
  1.6 4.1 %collective-permute-start = (bf16[80,576]{1,0:T(8,128)(2,1)S(1)}, bf16[80,576]{1,0:T(8,128)(2,1)S(1)}, u32[]{:S(2)}, u32[]{:S(2)}) collective-permute-start(bf16[80,576]{1,0:T(8,128)(2,1)S(1)} %constant_dynamic-slice_fusion), channel_id=1, source_target_pairs={{0,16},{4,20},{8,24},{12,28},{16,0},{20,4},{24,8},{28,12},{1,17},{... | collective-permute-start | bytes 276488 | tf_op jit(solution)/shard_map/ppermute | solution.py:191
  5.7 5.1 %collective-permute-done = bf16[80,576]{1,0:T(8,128)(2,1)S(1)} collective-permute-done((bf16[80,576]{1,0:T(8,128)(2,1)S(1)}, bf16[80,576]{1,0:T(8,128)(2,1)S(1)}, u32[]{:S(2)}, u32[]{:S(2)}) %collective-permute-start) | collective-permute-done | bytes 92192 | tf_op jit(solution)/shard_map/ppermute | solution.py:191
  10.8 0.0 copy-start.6
  10.8 0.8 collective-permute-start.1
  11.6 5.5 %collective-permute-done.1 = bf16[160,576]{1,0:T(8,128)(2,1)S(1)} collective-permute-done((bf16[160,576]{1,0:T(8,128)(2,1)S(1)}, bf16[160,576]{1,0:T(8,128)(2,1)S(1)}, u32[]{:S(2)}, u32[]{:S(2)}) %collective-permute-start.1) | collective-permute-done | bytes 184352 | tf_op jit(solution)/shard_map/ppermute | solution.py:191
  17.2 1.3 %collective-permute-start.2 = (bf16[320,576]{1,0:T(8,128)(2,1)S(1)}, bf16[320,576]{1,0:T(8,128)(2,1)S(1)}, u32[]{:S(2)}, u32[]{:S(2)}) collective-permute-start(bf16[320,576]{1,0:T(8,128)(2,1)S(1)} %pad_maximum_fusion.1), channel_id=1, source_target_pairs={{0,4},{4,0},{8,12},{12,8},{16,20},{20,16},{24,28},{28,24},{1,5},{5... | collective-permute-start | bytes 1105928 | tf_op jit(solution)/shard_map/ppermute | solution.py:191
  18.5 0.0 copy-done.5
  18.5 0.3 reshape.19
  18.8 0.1 slice.9
  18.8 0.1 slice.8
  18.9 0.1 copy.21
  19.1 0.1 copy.19
  19.2 0.0 copy-done.6
  19.3 0.0 copy-start.2
  19.3 0.0 copy-start.10
  19.3 4.6 %collective-permute-start.6 = (bf16[160,1280]{1,0:T(8,128)(2,1)S(1)}, bf16[160,1280]{1,0:T(8,128)(2,1)S(1)}, u32[]{:S(2)}, u32[]{:S(2)}) collective-permute-start(bf16[160,1280]{1,0:T(8,128)(2,1)S(1)} %pad_maximum_fusion.2.x_ref.refs_0_), channel_id=1, source_target_pairs={{0,24},{4,28},{8,16},{12,20},{16,8},{20,12},{24,0},{28,4},{1,25},{... | collective-permute-start | bytes 1228808 | tf_op jit(solution)/shard_map/ppermute | solution.py:191
  23.9 0.0 collective-permute-start.5
  23.9 0.6 collective-permute-start.4
  24.5 2.4 %collective-permute-done.2 = bf16[320,576]{1,0:T(8,128)(2,1)S(1)} collective-permute-done((bf16[320,576]{1,0:T(8,128)(2,1)S(1)}, bf16[320,576]{1,0:T(8,128)(2,1)S(1)}, u32[]{:S(2)}, u32[]{:S(2)}) %collective-permute-start.2) | collective-permute-done | bytes 368672 | tf_op jit(solution)/shard_map/ppermute | solution.py:191
  27.0 0.1 pad_maximum_fusion.mine_ref
  27.0 0.0 copy-start.1
  27.1 0.4 copy.17
  27.4 0.1 collective-permute-start.3
  27.5 0.0 copy-done.2
  27.5 1.4 %collective-permute-start.7 = (bf16[160,1280]{1,0:T(8,128)(2,1)S(1)}, bf16[160,1280]{1,0:T(8,128)(2,1)}, u32[]{:S(2)}, u32[]{:S(2)}) collective-permute-start(bf16[160,1280]{1,0:T(8,128)(2,1)S(1)} %pad_maximum_fusion.2.x_ref.refs_0_), channel_id=1, source_target_pairs={{0,4},{4,0},{8,12},{12,8},{16,20},{20,16},{24,28},{28,24},{1,5},{5... | collective-permute-start | bytes 1228808 | tf_op jit(solution)/shard_map/ppermute | solution.py:191
  28.9 5.5 %collective-permute-done.6.refs_3_ = bf16[160,1280]{1,0:T(8,128)(2,1)S(1)} collective-permute-done((bf16[160,1280]{1,0:T(8,128)(2,1)S(1)}, bf16[160,1280]{1,0:T(8,128)(2,1)S(1)}, u32[]{:S(2)}, u32[]{:S(2)}) %collective-permute-start.6) | collective-permute-done | bytes 409632 | tf_op jit(solution)/shard_map/ppermute | solution.py:191
  34.4 0.0 copy-start.4
  34.4 0.5 collective-permute-start.10
  34.9 23.1 %collective-permute-done.5.refs_2_ = bf16[160,1280]{1,0:T(8,128)(2,1)} collective-permute-done((bf16[160,1280]{1,0:T(8,128)(2,1)S(1)}, bf16[160,1280]{1,0:T(8,128)(2,1)}, u32[]{:S(2)}, u32[]{:S(2)}) %collective-permute-start.5) | collective-permute-done | bytes 409632 | tf_op jit(solution)/shard_map/ppermute | solution.py:191
  58.0 0.5 collective-permute-start.9
  58.5 0.0 collective-permute-done.4.refs_1_
  58.5 1.5 %collective-permute-start.8 = (bf16[160,1280]{1,0:T(8,128)(2,1)}, bf16[160,1280]{1,0:T(8,128)(2,1)}, u32[]{:S(2)}, u32[]{:S(2)}) collective-permute-start(bf16[160,1280]{1,0:T(8,128)(2,1)} %collective-permute-done.4.refs_1_), channel_id=1, source_target_pairs={{0,4},{4,0},{8,12},{12,8},{16,20},{20,16},{24,28},{28,24},{1,5},{5... | collective-permute-start | bytes 1228808 | tf_op jit(solution)/shard_map/ppermute | solution.py:191
  60.0 0.0 copy-done.10
  60.0 0.2 convert_reduce_fusion.low_ref
  60.2 0.1 broadcast_in_dim.2
  60.3 0.7 reshape_reshape.3.refs_8_
  61.0 0.6 pad_add_fusion.where_ref
  61.6 0.0 collective-permute-done.3
  61.6 1.2 %copy.20.other_ref = bf16[640,576]{1,0:T(8,128)(2,1)} copy(bf16[640,576]{0,1:T(8,128)(2,1)S(1)} %collective-permute-done.3) | data formatting | bytes 1474560 | tf_op jit(solution)/shard_map/ppermute | solution.py:191
  62.8 0.0 copy-done.1
  62.8 0.0 copy-done.7
  62.8 9.7 %project.1 = (bf16[4,1280,192]{2,1,0:T(8,128)(2,1)}, bf16[1280,512]{1,0:T(8,128)(2,1)}, bf16[512,1280]{1,0:T(8,128)(2,1)}, bf16[160,768]{1,0:T(8,128)(2,1)}) custom-call(s32[16]{0:T(128)} %order_ref.3, s32[16]{0:T(128)} %copy-done.7, s32[2]{0:T(128)} %pad_add_fusion.where_ref, bf16[640,576]{1,0:T(8,128)(2,1)} %copy-done.1, bf16[640,576]{1,0:T(8,128)(2,1)} %copy.20.other_ref, ...), custom_call_target="tpu_custom_call" | custom-call | tf_op jit(solution)/shard_map/project/pallas_call | solution.py:231
  72.5 0.0 copy-done.4
  72.5 0.0 collective-permute-done.7.refs_4_
  72.5 0.0 collective-permute-done.10.refs_7_
  72.5 0.0 collective-permute-done.9.refs_6_
  72.5 5.0 %collective-permute-done.8.refs_5_ = bf16[160,1280]{1,0:T(8,128)(2,1)} collective-permute-done((bf16[160,1280]{1,0:T(8,128)(2,1)}, bf16[160,1280]{1,0:T(8,128)(2,1)}, u32[]{:S(2)}, u32[]{:S(2)}) %collective-permute-start.8) | collective-permute-done | bytes 409632 | tf_op jit(solution)/shard_map/ppermute | solution.py:191
  77.6 20.7 %keys.1 = (bf16[1280,512]{1,0:T(8,128)(2,1)}, bf16[1280,512]{1,0:T(8,128)(2,1)}, f32[160,576]{1,0:T(8,128)}) custom-call(s32[16]{0:T(128)} %order_ref.3, s32[2]{0:T(128)} %pad_add_fusion.where_ref, bf16[160,1280]{1,0:T(8,128)(2,1)} %copy-done.2, bf16[160,1280]{1,0:T(8,128)(2,1)} %collective-permute-done.4.refs_1_, ...), custom_call_target="tpu_custom_call" | custom-call | tf_op jit(solution)/shard_map/keys/pallas_call | solution.py:254
  98.3 1.0 convert_element_type.22
  99.3 0.1 collective-permute-start.11
  99.4 0.0 copy-done.8
  99.4 0.0 copy-start.3
  99.4 0.0 copy-start.9
  99.4 3.3 %fusion = f32[512,512]{1,0:T(8,128)} fusion(bf16[512,1280]{1,0:T(8,128)(2,1)S(1)} %copy-done.8, bf16[1280,512]{1,0:T(8,128)(2,1)} %get-tuple-element.16), kind=kOutput, calls=%fused_computation.11 | convolution fusion | flops 671088640 | bytes 3670016 | tf_op jit(solution)/shard_map/dot_general | solution.py:29
  102.6 0.0 collective-permute-done.11
  102.7 0.0 copy-done.3
  102.7 1.6 %collective-permute-start.12 = (bf16[160,576]{1,0:T(8,128)(2,1)S(1)}, bf16[160,576]{1,0:T(8,128)(2,1)S(1)}, u32[]{:S(2)}, u32[]{:S(2)}) collective-permute-start(bf16[160,576]{1,0:T(8,128)(2,1)S(1)} %add_convert_fusion), channel_id=1, source_target_pairs={{0,2},{1,3},{2,0},{3,1},{4,6},{5,7},{6,4},{7,5},{8,10},{9,11},{10,... | collective-permute-start | bytes 552968 | tf_op jit(solution)/shard_map/ppermute | solution.py:191
  104.3 0.0 copy-done.9
  104.3 1.8 %fusion.1 = f32[512,512]{1,0:T(8,128)} fusion(bf16[512,1280]{1,0:T(8,128)(2,1)S(1)} %copy-done.8, bf16[1280,512]{1,0:T(8,128)(2,1)S(1)} %copy-done.9), kind=kOutput, calls=%fused_computation.12 | convolution fusion | flops 671088640 | bytes 3670016 | tf_op jit(solution)/shard_map/dot_general | solution.py:29
  106.1 4.2 %collective-permute-done.12 = bf16[160,576]{1,0:T(8,128)(2,1)S(1)} collective-permute-done((bf16[160,576]{1,0:T(8,128)(2,1)S(1)}, bf16[160,576]{1,0:T(8,128)(2,1)S(1)}, u32[]{:S(2)}, u32[]{:S(2)}) %collective-permute-start.12) | collective-permute-done | bytes 184352 | tf_op jit(solution)/shard_map/ppermute | solution.py:191
  110.2 0.8 convert_add_fusion
  (9 shorter events, 0.2 us)
Async XLA Ops:
  0.6 0.9 copy-start
  0.6 17.8 %copy-start.5 = (bf16[160,768]{1,0:T(8,128)(2,1)S(1)}, bf16[160,768]{1,0:T(8,128)(2,1)}, u32[]{:S(2)}) copy-start(bf16[160,768]{1,0:T(8,128)(2,1)} %param.7) | copy-start | bytes 737284
  1.6 9.2 %collective-permute-start = (bf16[80,576]{1,0:T(8,128)(2,1)S(1)}, bf16[80,576]{1,0:T(8,128)(2,1)S(1)}, u32[]{:S(2)}, u32[]{:S(2)}) collective-permute-start(bf16[80,576]{1,0:T(8,128)(2,1)S(1)} %constant_dynamic-slice_fusion), channel_id=1, source_target_pairs={{0,16},{4,20},{8,24},{12,28},{16,0},{20,4},{24,8},{28,12},{1,17},{... | collective-permute-start | bytes 276488 | tf_op jit(solution)/shard_map/ppermute | solution.py:191
  10.8 8.4 %copy-start.6 = (bf16[160,512]{1,0:T(8,128)(2,1)S(1)}, bf16[160,512]{1,0:T(8,128)(2,1)}, u32[]{:S(2)}) copy-start(bf16[160,512]{1,0:T(8,128)(2,1)} %param.11) | copy-start | bytes 491524
  10.8 6.3 %collective-permute-start.1 = (bf16[160,576]{1,0:T(8,128)(2,1)S(1)}, bf16[160,576]{1,0:T(8,128)(2,1)S(1)}, u32[]{:S(2)}, u32[]{:S(2)}) collective-permute-start(bf16[160,576]{1,0:T(8,128)(2,1)S(1)} %pad_maximum_fusion.3), channel_id=1, source_target_pairs={{0,8},{4,12},{8,0},{12,4},{16,24},{20,28},{24,16},{28,20},{1,9},{5... | collective-permute-start | bytes 552968 | tf_op jit(solution)/shard_map/ppermute | solution.py:191
  17.2 9.8 %collective-permute-start.2 = (bf16[320,576]{1,0:T(8,128)(2,1)S(1)}, bf16[320,576]{1,0:T(8,128)(2,1)S(1)}, u32[]{:S(2)}, u32[]{:S(2)}) collective-permute-start(bf16[320,576]{1,0:T(8,128)(2,1)S(1)} %pad_maximum_fusion.1), channel_id=1, source_target_pairs={{0,4},{4,0},{8,12},{12,8},{16,20},{20,16},{24,28},{28,24},{1,5},{5... | collective-permute-start | bytes 1105928 | tf_op jit(solution)/shard_map/ppermute | solution.py:191
  19.3 8.3 %copy-start.2 = (bf16[160,1280]{1,0:T(8,128)(2,1)}, bf16[160,1280]{1,0:T(8,128)(2,1)S(1)}, u32[]{:S(2)}) copy-start(bf16[160,1280]{1,0:T(8,128)(2,1)S(1)} %pad_maximum_fusion.2.x_ref.refs_0_) | copy-start | bytes 1228804
  19.3 40.8 %copy-start.10 = (s32[16]{0:T(128)S(1)}, s32[16]{0:T(128)}, u32[]{:S(2)}) copy-start(s32[16]{0:T(128)} %param.13) | copy-start | bytes 196
  19.3 15.1 %collective-permute-start.6 = (bf16[160,1280]{1,0:T(8,128)(2,1)S(1)}, bf16[160,1280]{1,0:T(8,128)(2,1)S(1)}, u32[]{:S(2)}, u32[]{:S(2)}) collective-permute-start(bf16[160,1280]{1,0:T(8,128)(2,1)S(1)} %pad_maximum_fusion.2.x_ref.refs_0_), channel_id=1, source_target_pairs={{0,24},{4,28},{8,16},{12,20},{16,8},{20,12},{24,0},{28,4},{1,25},{... | collective-permute-start | bytes 1228808 | tf_op jit(solution)/shard_map/ppermute | solution.py:191
  23.9 34.1 %collective-permute-start.5 = (bf16[160,1280]{1,0:T(8,128)(2,1)S(1)}, bf16[160,1280]{1,0:T(8,128)(2,1)}, u32[]{:S(2)}, u32[]{:S(2)}) collective-permute-start(bf16[160,1280]{1,0:T(8,128)(2,1)S(1)} %pad_maximum_fusion.2.x_ref.refs_0_), channel_id=1, source_target_pairs={{0,16},{4,20},{8,24},{12,28},{16,0},{20,4},{24,8},{28,12},{1,17},{... | collective-permute-start | bytes 1228808 | tf_op jit(solution)/shard_map/ppermute | solution.py:191
  23.9 34.6 %collective-permute-start.4 = (bf16[160,1280]{1,0:T(8,128)(2,1)S(1)}, bf16[160,1280]{1,0:T(8,128)(2,1)}, u32[]{:S(2)}, u32[]{:S(2)}) collective-permute-start(bf16[160,1280]{1,0:T(8,128)(2,1)S(1)} %pad_maximum_fusion.2.x_ref.refs_0_), channel_id=1, source_target_pairs={{0,8},{4,12},{8,0},{12,4},{16,24},{20,28},{24,16},{28,20},{1,9},{5... | collective-permute-start | bytes 1228808 | tf_op jit(solution)/shard_map/ppermute | solution.py:191
  27.0 35.8 %copy-start.1 = (bf16[640,576]{1,0:T(8,128)(2,1)}, bf16[640,576]{1,0:T(8,128)(2,1)S(1)}, u32[]{:S(2)}) copy-start(bf16[640,576]{1,0:T(8,128)(2,1)S(1)} %pad_maximum_fusion.mine_ref) | copy-start | bytes 2211844
  27.4 34.2 %collective-permute-start.3 = (bf16[640,576]{0,1:T(8,128)(2,1)S(1)}, bf16[640,576]{0,1:T(8,128)(2,1)S(1)}, u32[]{:S(2)}, u32[]{:S(2)}) collective-permute-start(bf16[640,576]{0,1:T(8,128)(2,1)S(1)} %copy.17), channel_id=1, source_target_pairs={{0,1},{1,0},{2,3},{3,2},{4,5},{5,4},{6,7},{7,6},{8,9},{9,8},{10,11... | collective-permute-start | bytes 2211848 | tf_op jit(solution)/shard_map/ppermute | solution.py:191
  27.5 45.0 %collective-permute-start.7 = (bf16[160,1280]{1,0:T(8,128)(2,1)S(1)}, bf16[160,1280]{1,0:T(8,128)(2,1)}, u32[]{:S(2)}, u32[]{:S(2)}) collective-permute-start(bf16[160,1280]{1,0:T(8,128)(2,1)S(1)} %pad_maximum_fusion.2.x_ref.refs_0_), channel_id=1, source_target_pairs={{0,4},{4,0},{8,12},{12,8},{16,20},{20,16},{24,28},{28,24},{1,5},{5... | collective-permute-start | bytes 1228808 | tf_op jit(solution)/shard_map/ppermute | solution.py:191
  34.4 38.1 %copy-start.4 = (bf16[160,1280]{1,0:T(8,128)(2,1)}, bf16[160,1280]{1,0:T(8,128)(2,1)S(1)}, u32[]{:S(2)}) copy-start(bf16[160,1280]{1,0:T(8,128)(2,1)S(1)} %collective-permute-done.6.refs_3_) | copy-start | bytes 1228804
  34.4 38.1 %collective-permute-start.10 = (bf16[160,1280]{1,0:T(8,128)(2,1)S(1)}, bf16[160,1280]{1,0:T(8,128)(2,1)}, u32[]{:S(2)}, u32[]{:S(2)}) collective-permute-start(bf16[160,1280]{1,0:T(8,128)(2,1)S(1)} %collective-permute-done.6.refs_3_), channel_id=1, source_target_pairs={{0,4},{4,0},{8,12},{12,8},{16,20},{20,16},{24,28},{28,24},{1,5},{5... | collective-permute-start | bytes 1228808 | tf_op jit(solution)/shard_map/ppermute | solution.py:191
  58.0 14.5 %collective-permute-start.9 = (bf16[160,1280]{1,0:T(8,128)(2,1)}, bf16[160,1280]{1,0:T(8,128)(2,1)}, u32[]{:S(2)}, u32[]{:S(2)}) collective-permute-start(bf16[160,1280]{1,0:T(8,128)(2,1)} %collective-permute-done.5.refs_2_), channel_id=1, source_target_pairs={{0,4},{4,0},{8,12},{12,8},{16,20},{20,16},{24,28},{28,24},{1,5},{5... | collective-permute-start | bytes 1228808 | tf_op jit(solution)/shard_map/ppermute | solution.py:191
  58.5 19.0 %collective-permute-start.8 = (bf16[160,1280]{1,0:T(8,128)(2,1)}, bf16[160,1280]{1,0:T(8,128)(2,1)}, u32[]{:S(2)}, u32[]{:S(2)}) collective-permute-start(bf16[160,1280]{1,0:T(8,128)(2,1)} %collective-permute-done.4.refs_1_), channel_id=1, source_target_pairs={{0,4},{4,0},{8,12},{12,8},{16,20},{20,16},{24,28},{28,24},{1,5},{5... | collective-permute-start | bytes 1228808 | tf_op jit(solution)/shard_map/ppermute | solution.py:191
  60.2 2.6 %copy-start.7 = (s32[16]{0:T(128)}, s32[16]{0:T(128)S(1)}, u32[]{:S(2)}) copy-start(s32[16]{0:T(128)S(1)} %convert_reduce_fusion.low_ref) | copy-start | bytes 196
  77.6 21.8 %copy-start.8 = (bf16[512,1280]{1,0:T(8,128)(2,1)S(1)}, bf16[512,1280]{1,0:T(8,128)(2,1)}, u32[]{:S(2)}) copy-start(bf16[512,1280]{1,0:T(8,128)(2,1)} %get-tuple-element.15) | copy-start | bytes 3932164
  99.3 3.4 %collective-permute-start.11 = (bf16[160,576]{1,0:T(8,128)(2,1)S(1)}, bf16[160,576]{1,0:T(8,128)(2,1)S(1)}, u32[]{:S(2)}, u32[]{:S(2)}) collective-permute-start(bf16[160,576]{1,0:T(8,128)(2,1)S(1)} %convert_element_type.22), channel_id=1, source_target_pairs={{0,1},{1,0},{2,3},{3,2},{4,5},{5,4},{6,7},{7,6},{8,9},{9,8},{10,11... | collective-permute-start | bytes 552968 | tf_op jit(solution)/shard_map/ppermute | solution.py:191
  99.4 3.3 %copy-start.3 = (f32[160,576]{1,0:T(8,128)S(1)}, f32[160,576]{1,0:T(8,128)}, u32[]{:S(2)}) copy-start(f32[160,576]{1,0:T(8,128)} %get-tuple-element.14) | copy-start | bytes 1105924
  99.4 4.9 %copy-start.9 = (bf16[1280,512]{1,0:T(8,128)(2,1)S(1)}, bf16[1280,512]{1,0:T(8,128)(2,1)}, u32[]{:S(2)}) copy-start(bf16[1280,512]{1,0:T(8,128)(2,1)} %get-tuple-element.17) | copy-start | bytes 3932164
  102.7 7.5 %collective-permute-start.12 = (bf16[160,576]{1,0:T(8,128)(2,1)S(1)}, bf16[160,576]{1,0:T(8,128)(2,1)S(1)}, u32[]{:S(2)}, u32[]{:S(2)}) collective-permute-start(bf16[160,576]{1,0:T(8,128)(2,1)S(1)} %add_convert_fusion), channel_id=1, source_target_pairs={{0,2},{1,3},{2,0},{3,1},{4,6},{5,7},{6,4},{7,5},{8,10},{9,11},{10,... | collective-permute-start | bytes 552968 | tf_op jit(solution)/shard_map/ppermute | solution.py:191

commit v2 on v1

v2 whole, which is shorter than its diff:
```python
import functools
import math

import jax
import jax.numpy as jnp
from jax import lax
from jax.experimental import pallas as pl
from jax.experimental.pallas import tpu as pltpu
from jax.sharding import PartitionSpec as P

D_LAT = 512
ROPE = 64
NOPE = 128
VDIM = 128
WIDTH = NOPE + ROPE
SCALE = WIDTH ** (-0.5)
SCALE_LOG2 = SCALE * math.log2(math.e)
NEG_FILL = -1e30
TILE = 256
GRAIN = 128
LAT_LANES = 640
BY_COLUMNS = (((1,), (1,)), ((), ()))
BY_ROWS = (((1,), (0,)), ((), ()))
SMEM = pl.BlockSpec(memory_space=pltpu.SMEM)
VMEM = pl.BlockSpec(memory_space=pltpu.VMEM)
HBM = pl.BlockSpec(memory_space=pl.ANY)


def dot(a, b, dims):
    return lax.dot_general(a, b, dims, preferred_element_type=jnp.float32)


def project_kernel(
    devices, half, heads, pair, order_ref, low_ref, where_ref, mine_ref, other_ref, wk_in, wv_in, *refs
):
    x_refs = refs[: heads // pair]
    keys_ref, values_ref, turned_ref, dq_ref, latent, wk_ref, wv_ref, sem, weight_sem = refs[heads // pair :]
    blocks = 2 * devices
    total = blocks * half
    me, core = where_ref[0], where_ref[1]
    copies = [
        pltpu.make_async_copy(wk_in, wk_ref, weight_sem.at[0]),
        pltpu.make_async_copy(wv_in, wv_ref, weight_sem.at[1]),
    ]
    for copy in copies:
        copy.start()
    masks = [0]
    for bit in reversed(range(devices.bit_length() - 1)):
        masks = masks + [m ^ (1 << bit) for m in masks]
    for number, mask in enumerate(masks):
        for side, source in enumerate((mine_ref, other_ref)):
            block = order_ref[2 * (me ^ mask) + (core ^ side)]
            copy = pltpu.make_async_copy(
                source.at[pl.ds(number * half, half), :],
                latent.at[pl.ds(pl.multiple_of(block * half, 16), half), :],
                sem.at[2 * number + side],
            )
            copy.start()
            copies.append(copy)
    for copy in copies:
        copy.wait()
    for first in range(0, total, TILE):
        rows = pl.ds(first, TILE)
        part = latent[rows, :D_LAT]
        rope = latent[rows, D_LAT : D_LAT + ROPE]
        up_keys = dot(part, wk_ref[...], BY_ROWS).astype(jnp.bfloat16)
        for head in range(heads):
            keys_ref[head, rows, :] = jnp.concatenate(
                [up_keys[:, head * NOPE : (head + 1) * NOPE], rope], axis=1
            )
        values_ref[rows, :] = dot(part, wv_ref[...], BY_ROWS).astype(jnp.bfloat16)
        turned_ref[:, first : first + TILE] = part.T
    span = (blocks // 2) * half
    grad_at = pair * WIDTH
    for side in range(2):
        block = order_ref[2 * me + side]
        start = pl.multiple_of(jnp.maximum(block - (blocks // 2 - 1), 0) * half, 16)
        window = pl.ds(start, span)
        key_pos = start + lax.broadcasted_iota(jnp.int32, (half, span), 1)
        query_pos = block * half + lax.broadcasted_iota(jnp.int32, (half, span), 0)
        seen = (key_pos <= query_pos) & (key_pos >= low_ref[block] * half)
        bias = jnp.where(seen, 0.0, NEG_FILL)
        rows = pl.ds(side * half, half)
        outs = []
        for head in range(heads):
            x_ref, at = x_refs[head // pair], head % pair
            query = x_ref[rows, at * WIDTH : (at + 1) * WIDTH]
            grad = x_ref[rows, grad_at + at * VDIM : grad_at + (at + 1) * VDIM]
            keys = keys_ref[head, window, :]
            values = values_ref[window, head * VDIM : (head + 1) * VDIM]
            scores = dot(query, keys, BY_COLUMNS) * SCALE_LOG2 + bias
            expo = jnp.exp2(scores - jnp.max(scores, axis=1, keepdims=True))
            probs = expo * (1.0 / jnp.sum(expo, axis=1, keepdims=True))
            grad_probs = dot(grad, values, BY_COLUMNS)
            delta = jnp.sum(probs * grad_probs, axis=1, keepdims=True)
            grad_scores = (probs * (grad_probs - delta) * SCALE).astype(jnp.bfloat16)
            outs.append(dot(grad_scores, keys, BY_ROWS).astype(jnp.bfloat16))
        dq_ref[rows, :] = jnp.concatenate(outs, axis=1)


def key_kernel(devices, half, here, begun, low_ref, order_ref, source_ref, *refs):
    x_refs = refs[:devices]
    low_rows_ref, *sources = refs[devices : devices + 5]
    dk_ref, dv_ref, dlat_ref = refs[devices + 5 + begun : devices + 8 + begun]
    x_all, sum_nope, sum_value, sum_rope, sem = refs[devices + 8 + begun : devices + 13 + begun]
    *held, held_sem = refs[devices + 13 + begun :]
    keys_ref, values_ref, wk_ref, wv_ref = held
    loads = [
        pltpu.make_async_copy(source, target, held_sem.at[number])
        for number, (source, target) in enumerate(zip(sources, held))
    ]
    for copy in loads:
        copy.start()
    blocks = 2 * devices
    total = blocks * half
    grad_at = here * WIDTH
    copies = []
    for number in range(devices):
        for side in range(2):
            block = order_ref[2 * source_ref[number] + side]
            rows = pl.ds(pl.multiple_of(block * half, 16), half)
            copy = pltpu.make_async_copy(
                x_refs[number].at[pl.ds(side * half, half), :],
                x_all.at[rows, :],
                sem.at[2 * number + side],
            )
            copy.start()
            copies.append(copy)
    sum_nope[...] = jnp.zeros_like(sum_nope)
    sum_value[...] = jnp.zeros_like(sum_value)
    sum_rope[...] = jnp.zeros_like(sum_rope)
    for copy in loads[:2] + copies:
        copy.wait()

    def tile(first, start, span):
        window = pl.ds(start, span)
        rows = pl.ds(first, TILE)
        key_pos = start + lax.broadcasted_iota(jnp.int32, (span, TILE), 0)
        query_pos = first + lax.broadcasted_iota(jnp.int32, (span, TILE), 1)
        seen = (key_pos <= query_pos) & (key_pos >= low_rows_ref[:, rows])
        bias = jnp.where(seen, 0.0, NEG_FILL)
        def begin(head):
            lanes = slice(head * NOPE, (head + 1) * NOPE)
            query = x_all[rows, head * WIDTH : (head + 1) * WIDTH]
            grad = x_all[rows, grad_at + head * VDIM : grad_at + (head + 1) * VDIM]
            scores = dot(keys_ref[head, window, :], query, BY_COLUMNS)
            return lanes, query, grad, scores, dot(values_ref[window, lanes], grad, BY_COLUMNS)

        def middle(lanes, query, grad, scores, grad_probs):
            scores = scores * SCALE_LOG2 + bias
            expo = jnp.exp2(scores - jnp.max(scores, axis=0, keepdims=True))
            inverse = 1.0 / jnp.sum(expo, axis=0, keepdims=True)
            delta = jnp.sum(expo * grad_probs, axis=0, keepdims=True) * inverse
            probs = expo * inverse
            grad_scores = (probs * (grad_probs - delta)).astype(jnp.bfloat16)
            return lanes, query, grad, probs.astype(jnp.bfloat16), grad_scores

        def end(lanes, query, grad, probs, grad_scores):
            sum_value[window, lanes] += dot(probs, grad, BY_ROWS)
            key_grad = dot(grad_scores, query, BY_ROWS)
            sum_nope[window, lanes] += key_grad[:, :NOPE]
            return key_grad[:, NOPE:]

        rope = 0.0
        begun_heads = [begin(0)]
        for head in range(here):
            if head + 1 < here:
                begun_heads.append(begin(head + 1))
            rope = rope + end(*middle(*begun_heads[head]))
        sum_rope[window, :] += rope

    def step(number, carry):
        first = pl.multiple_of(number * TILE, TILE)
        oldest = low_ref[first // half] * half
        need = (first + TILE - oldest + GRAIN - 1) // GRAIN
        for size in sizes:
            below = sizes[sizes.index(size) - 1] if size != sizes[0] else 0

            @pl.when((need <= size) & (need > below))
            def _(size=size):
                start = jnp.maximum(first + TILE - size * GRAIN, 0)
                tile(first, pl.multiple_of(start, 16), size * GRAIN)

        return carry

    most = -(-(devices * half + TILE) // GRAIN)
    sizes = list(range(TILE // GRAIN, most + 1, max(1, most // 8)))
    if sizes[-1] != most:
        sizes.append(most)
    lax.fori_loop(0, total // TILE, step, 0)
    dk_ref[...] = (sum_nope[...] * SCALE).astype(jnp.bfloat16)
    dv_ref[...] = sum_value[...].astype(jnp.bfloat16)
    for copy in loads[2:]:
        copy.wait()
    for side in range(2):
        block = order_ref[2 * source_ref[0] + side]
        rows = pl.ds(pl.multiple_of(block * half, 16), half)
        out = dot(dk_ref[rows, :], wk_ref[...], BY_COLUMNS)
        out = out + dot(dv_ref[rows, :], wv_ref[...], BY_COLUMNS)
        rope = sum_rope[rows, :] * SCALE
        here_rows = pl.ds(side * half, half)
        out = jnp.concatenate([out, rope], axis=1)
        if begun:
            out = out + refs[devices + 5][here_rows, :]
        dlat_ref[here_rows, :] = out.astype(dlat_ref.dtype)


def swap(array, axis, mask):
    size = lax.axis_size(axis)
    return lax.ppermute(array, axis, [(i, i ^ mask) for i in range(size)])


def gather(own, devices):
    far = [own] + [swap(own, "seq", m) for m in range(2, devices, 2)]
    return far + [swap(x, "seq", 1) for x in far]


def join(array, axis, mask):
    return jnp.concatenate([array, swap(array, axis, mask)], axis=0)


def gather_latent(mine, devices):
    step = devices // 2
    while step:
        mine = join(mine, "seq", step)
        step //= 2
    return mine


def gather_by_line(own, mine, me):
    def along(array, pairs):
        return lax.ppermute(
            array, "seq", [(2 * a + y, 2 * b + y) for a, b in pairs for y in range(2)]
        )

    hold = lax.optimization_barrier
    middle = [(1, 2), (2, 1)]
    outward = [(1, 0), (2, 3)]
    place = me // 2
    inner = (place == 1) | (place == 2)
    piece = mine.shape[0]
    mine = join(mine, "seq", 4)
    mine = join(mine, "seq", 2)
    near = swap(own, "seq", 2)
    third = along(own, middle)
    y_own = swap(own, "seq", 1)
    near, third, y_own, mine = hold((near, third, y_own, mine))
    fourth = along(near, middle)
    handed = along(third, outward)
    y_near = swap(near, "seq", 1)
    mine = join(mine, "seq", 1)
    fourth, handed, y_near, mine = hold((fourth, handed, y_near, mine))
    third = jnp.where(inner, third, handed)
    last = along(fourth, outward)
    y_third = swap(third, "seq", 1)
    theirs = swap(mine, "head", 2)
    last, y_third, mine, theirs = hold((last, y_third, mine, theirs))
    fourth = jnp.where(inner, fourth, last)
    fourth, mine, theirs = hold((fourth, mine, theirs))
    y_fourth = swap(fourth, "seq", 1)
    first = lax.axis_index("head") < 2
    mine, theirs = (x.reshape(8, piece, mine.shape[1]) for x in (mine, theirs))
    mine = jnp.concatenate(
        [jnp.where(first, mine, theirs), jnp.where(first, theirs, mine)], axis=1
    ).reshape(16 * piece, mine.shape[2])
    left = place < 2
    places = [place, place ^ 1, jnp.where(left, 2, 1), jnp.where(left, 3, 0)]
    y = me % 2
    sources = [2 * p + y for p in places] + [2 * p + 1 - y for p in places]
    return [own, near, third, fourth, y_own, y_near, y_third, y_fourth], jnp.stack(sources), mine


def shards(queries, latent_rope, w_uk, w_uv, d_out, block_order, block_doc):
    local_rows = queries.shape[0]
    heads = w_uk.shape[1] // NOPE
    devices = lax.axis_size("seq")
    half = local_rows // 2
    total = local_rows * devices
    me = lax.axis_index("seq")
    low = jnp.sum((block_doc[None, :] < block_doc[:, None]).astype(jnp.int32), axis=1)
    low_rows = jnp.repeat(low * half, half).reshape(1, total)

    small = total <= 8 * TILE
    pair = heads if small else 2
    packed = [
        jnp.concatenate(
            [
                queries[:, first * WIDTH : (first + pair) * WIDTH],
                d_out[:, first * VDIM : (first + pair) * VDIM],
            ],
            axis=1,
        )
        for first in range(0, heads, pair)
    ]
    core = lax.axis_index("head") % 2
    where = jnp.stack([me, core]).astype(jnp.int32)
    latent = jnp.pad(latent_rope, ((0, 0), (0, LAT_LANES - D_LAT - ROPE)))
    mine = lax.dynamic_slice_in_dim(latent, core * half, half, axis=0)
    by_line = small and devices == 8 and lax.axis_size("head") == 4
    if by_line:
        mine = lax.dynamic_slice_in_dim(
            mine, lax.axis_index("head") // 2 * (half // 2), half // 2, axis=0
        )
        pieces, sources, mine = gather_by_line(packed[0], mine, me)
        gathered = [pieces]
    else:
        mine = gather_latent(mine, devices)
        gathered = [gather(x, devices) for x in packed]
        order = list(range(0, devices, 2)) + list(range(1, devices, 2))
        sources = jnp.stack([me ^ m for m in order])
    other = swap(mine, "head", 1)

    bf16 = jnp.bfloat16
    mebi = 1024 * 1024

    def params(size):
        return pltpu.CompilerParams(vmem_limit_bytes=(size if small else 60) * mebi)

    keys, values, turned, d_queries = pl.pallas_call(
        functools.partial(project_kernel, devices, half, heads, pair),
        out_shape=(
            jax.ShapeDtypeStruct((heads, total, WIDTH), bf16),
            jax.ShapeDtypeStruct((total, heads * VDIM), bf16),
            jax.ShapeDtypeStruct((D_LAT, total), bf16),
            jax.ShapeDtypeStruct((local_rows, heads * WIDTH), bf16),
        ),
        in_specs=[SMEM, SMEM, SMEM, HBM, HBM, HBM, HBM] + [VMEM] * len(packed),
        out_specs=(VMEM, VMEM, VMEM, VMEM),
        scratch_shapes=[
            pltpu.VMEM((total, LAT_LANES), bf16),
            pltpu.VMEM(w_uk.shape, bf16),
            pltpu.VMEM(w_uv.shape, bf16),
            pltpu.SemaphoreType.DMA((2 * devices,)),
            pltpu.SemaphoreType.DMA((2,)),
        ],
        compiler_params=params(20),
        cost_estimate=pl.CostEstimate(
            flops=20 * 2**30, bytes_accessed=16 * mebi, transcendentals=0
        ),
        name="project",
    )(block_order, low, where, mine, other, w_uk, w_uv, *packed)

    dks, dvs = [], []
    shares = []
    for first in range(0, heads, pair):
        lanes = slice(first * NOPE, (first + pair) * NOPE)
        pieces = gathered[first // pair]
        last = first + pair == heads
        dk, dv, *shares = pl.pallas_call(
            functools.partial(key_kernel, devices, half, pair, len(shares)),
            out_shape=(
                jax.ShapeDtypeStruct((total, pair * NOPE), bf16),
                jax.ShapeDtypeStruct((total, pair * VDIM), bf16),
                jax.ShapeDtypeStruct((local_rows, D_LAT + ROPE), bf16 if last else jnp.float32),
            ),
            in_specs=[SMEM, SMEM, SMEM] + [HBM] * devices + [VMEM] + [HBM] * 4 + [VMEM] * len(shares),
            out_specs=(VMEM, VMEM, VMEM),
            scratch_shapes=[
                pltpu.VMEM((total, pair * (WIDTH + VDIM)), bf16),
                pltpu.VMEM((total, pair * NOPE), jnp.float32),
                pltpu.VMEM((total, pair * VDIM), jnp.float32),
                pltpu.VMEM((total, ROPE), jnp.float32),
                pltpu.SemaphoreType.DMA((2 * devices,)),
                pltpu.VMEM((pair, total, WIDTH), bf16),
                pltpu.VMEM((total, pair * VDIM), bf16),
                pltpu.VMEM((D_LAT, pair * NOPE), bf16),
                pltpu.VMEM((D_LAT, pair * VDIM), bf16),
                pltpu.SemaphoreType.DMA((4,)),
            ],
            compiler_params=params(28),
            cost_estimate=pl.CostEstimate(
                flops=20 * 2**30, bytes_accessed=16 * mebi, transcendentals=0
            ),
            name="keys",
        )(
            low, block_order, sources, *pieces, low_rows,
            keys[first : first + pair], values[:, lanes], w_uk[:, lanes], w_uv[:, lanes], *shares,
        )
        dks.append(dk)
        dvs.append(dv)
    dk = jnp.concatenate(dks, axis=1)
    dv = jnp.concatenate(dvs, axis=1)
    sent = shares[0]
    dlat = sent.astype(jnp.float32) + swap(sent, "head", 1).astype(jnp.float32)
    dlat, dk, dv = lax.optimization_barrier((dlat, dk, dv))
    step = 2
    while step < lax.axis_size("head"):
        sent = dlat.astype(bf16)
        dlat = sent.astype(jnp.float32) + swap(sent, "head", step).astype(jnp.float32)
        step *= 2
    return (d_queries, dlat, dot(turned, dk, BY_ROWS), dot(turned, dv, BY_ROWS))


def solution(mesh):
    return jax.shard_map(
        shards,
        mesh=mesh,
        in_specs=(
            P("seq", "head"),
            P("seq", None),
            P(None, "head"),
            P(None, "head"),
            P("seq", "head"),
            P(),
            P(),
        ),
        out_specs=(P("seq", "head"), P("seq", None), P(None, "head"), P(None, "head")),
        check_vma=False,
    )
```

time: 111 us -> 94.3 us (0.85)
  waiting for transfers between devices: 50.8 us -> 32.4 us
  starting transfers between devices: 17.1 us -> 20.5 us
  Pallas kernels: 30.3 us -> 27.5 us
  local copies, waits for them, and re-layouts: 4 us -> 5.6 us
  matrix products: 5.06 us -> 3.62 us
    ppermute x13 -> x12, waiting for transfers between devices: 50.8 us -> 30.7 us  [swap(): return lax.ppermute(array, axis, [(i, i ^ mask) for i in range(size)])]
    ppermute x0 -> x4, starting transfers between devices: none -> 3.92 us  [along(): lax.ppermute(array, 'seq', [(2 * a + y, 2 * b + y) for a, b in pairs for...]
    pallas_call x2, Pallas kernels: 30.3 us -> 27.5 us  [the longest x1 18.2 us: shards(): pl.pallas_call(functools.partial(key_kernel, devices, half, pair, len(sha...]
    unnamed x24 -> x27, local copies, waits for them, and re-layouts: 1.12 us -> 3.57 us
    select_n x0 -> x3, other arithmetic: none -> 2.23 us  [the longest x1 1.14 us: gather_by_line(): jnp.where(first, mine, theirs)]
    ppermute x0 -> x4, waiting for transfers between devices: none -> 1.79 us  [along(): lax.ppermute(array, 'seq', [(2 * a + y, 2 * b + y) for a, b in pairs for...]
    dot_general x2, matrix products: 5.06 us -> 3.62 us  [dot(): return lax.dot_general(a, b, dims, preferred_element_type=jnp.float32)]
    ppermute x1 -> x0, local copies, waits for them, and re-layouts: 1.22 us -> none  [swap(): return lax.ppermute(array, axis, [(i, i ^ mask) for i in range(size)])]
  transfers between devices with their start and end apart: 13 -> 16, of which waited for: 7 -> 8; matrix products, arithmetic and copies ran while one was open for 8% -> 5% of each run, Pallas kernels for 9% -> 10%
where the time goes in v2:
time: 94.3 us; the launch traced here: 94.2 us
  waiting for transfers between devices  32.4 us (34%)
  Pallas kernels  27.5 us (29%)
  starting transfers between devices  20.5 us (22%)
  local copies, waits for them, and re-layouts  5.6 us (6%)
  matrix products  3.62 us (4%)
  other arithmetic  3.48 us (4%)
  between operations  0.96 us (1%)
    ppermute x12, waiting for transfers between devices, swap(): return lax.ppermute(array, axis, [(i, i ^ mask) for i in range(size)])  30.7 us
    pallas_call x1, Pallas kernels, shards(): pl.pallas_call(functools.partial(key_kernel, devices, half, pair, len(sha...  18.2 us
    ppermute x12, starting transfers between devices, swap(): return lax.ppermute(array, axis, [(i, i ^ mask) for i in range(size)])  16.6 us
    pallas_call x1, Pallas kernels, shards(): pl.pallas_call(functools.partial(project_kernel, devices, half, heads, pa...  9.37 us
    ppermute x4, starting transfers between devices, along(): lax.ppermute(array, 'seq', [(2 * a + y, 2 * b + y) for a, b in pairs for...  3.92 us
    dot_general x2, matrix products, dot(): return lax.dot_general(a, b, dims, preferred_element_type=jnp.float32)  3.62 us
    unnamed x27, local copies, waits for them, and re-layouts  3.57 us
  transfers between devices with their start and end apart: 16, of which 8 were waited for; matrix products, arithmetic and copies ran while one was open for 5% of the time, Pallas kernels for 10%

profile of v2, /device:TPU:0, one launch (start us, length us, event | category | flops | bytes accessed | tf_op | source)
XLA Modules:
  0.0 94.2 jit_solution(294313077533481436)
XLA Ops:
  0.6 1.0 %constant_dynamic-update-slice_fusion.1 = bf16[160,1280]{1,0:T(8,128)(2,1)S(1)} fusion(bf16[160,768]{1,0:T(8,128)(2,1)} %param.7), kind=kLoop, calls=%fused_computation.13 | loop fusion | bytes 491520
  1.6 0.9 constant_dynamic-update-slice_fusion.refs_0_
  2.5 3.0 %collective-permute-start.2 = (bf16[160,1280]{1,0:T(8,128)(2,1)S(1)}, bf16[160,1280]{1,0:T(8,128)(2,1)S(1)}, u32[]{:S(2)}, u32[]{:S(2)}) collective-permute-start(bf16[160,1280]{1,0:T(8,128)(2,1)S(1)} %constant_dynamic-update-slice_fusion.refs_0_), channel_id=1, source_target_pairs={{0,4},{4,0},{8,12},{12,8},{16,20},{20,16},{24,28},{28,24},{1,5},{5... | collective-permute-start | bytes 1228808 | tf_op jit(solution)/shard_map/ppermute | solution.py:210
  5.6 0.7 collective-permute-start.1
  6.2 4.4 %collective-permute-start = (bf16[160,1280]{1,0:T(8,128)(2,1)S(1)}, bf16[160,1280]{1,0:T(8,128)(2,1)S(1)}, u32[]{:S(2)}, u32[]{:S(2)}) collective-permute-start(bf16[160,1280]{1,0:T(8,128)(2,1)S(1)} %constant_dynamic-update-slice_fusion.refs_0_), channel_id=1, source_target_pairs={{0,8},{4,12},{8,0},{12,4},{16,24},{20,28},{24,16},{28,20},{1,9},{5... | collective-permute-start | bytes 1228808 | tf_op jit(solution)/shard_map/ppermute | solution.py:210
  10.7 0.8 pad_dynamic-slice_fusion
  11.5 0.1 collective-permute-start.3
  11.6 9.4 %collective-permute-done.3 = bf16[40,640]{1,0:T(8,128)(2,1)S(1)} collective-permute-done((bf16[40,640]{1,0:T(8,128)(2,1)S(1)}, bf16[40,640]{1,0:T(8,128)(2,1)S(1)}, u32[]{:S(2)}, u32[]{:S(2)}) %collective-permute-start.3) | collective-permute-done | bytes 51232 | tf_op jit(solution)/shard_map/ppermute | solution.py:210
  21.0 1.4 %collective-permute-start.4 = (bf16[80,640]{1,0:T(8,128)(2,1)S(1)}, bf16[80,640]{1,0:T(8,128)(2,1)S(1)}, u32[]{:S(2)}, u32[]{:S(2)}) collective-permute-start(bf16[80,640]{1,0:T(8,128)(2,1)S(1)} %pad_maximum_fusion.3), channel_id=1, source_target_pairs={{0,8},{4,12},{8,0},{12,4},{16,24},{20,28},{24,16},{28,20},{1,9},{5... | collective-permute-start | bytes 307208 | tf_op jit(solution)/shard_map/ppermute | solution.py:210
  22.4 3.4 %collective-permute-done.4 = bf16[80,640]{1,0:T(8,128)(2,1)S(1)} collective-permute-done((bf16[80,640]{1,0:T(8,128)(2,1)S(1)}, bf16[80,640]{1,0:T(8,128)(2,1)S(1)}, u32[]{:S(2)}, u32[]{:S(2)}) %collective-permute-start.4) | collective-permute-done | bytes 102432 | tf_op jit(solution)/shard_map/ppermute | solution.py:210
  25.8 0.0 collective-permute-done.2.refs_4_
  25.8 0.0 copy-start.3
  25.8 0.0 collective-permute-done.1
  25.8 0.0 collective-permute-done.refs_1_
  25.8 0.0 copy-start.5
  25.8 1.3 %collective-permute-start.6 = (bf16[160,1280]{1,0:T(8,128)(2,1)S(1)}, bf16[160,1280]{1,0:T(8,128)(2,1)}, u32[]{:S(2)}, u32[]{:S(2)}) collective-permute-start(bf16[160,1280]{1,0:T(8,128)(2,1)S(1)} %collective-permute-done.1), channel_id=1, source_target_pairs={{8,0},{12,4},{16,24},{20,28},{9,1},{13,5},{17,25},{21,29},{10,2},{... | collective-permute-start | bytes 1228808 | tf_op jit(solution)/shard_map/ppermute | solution.py:232
  27.1 0.6 collective-permute-start.7
  27.7 0.7 collective-permute-start.5
  28.4 1.6 %collective-permute-start.8 = (bf16[160,640]{1,0:T(8,128)(2,1)S(1)}, bf16[160,640]{1,0:T(8,128)(2,1)S(1)}, u32[]{:S(2)}, u32[]{:S(2)}) collective-permute-start(bf16[160,640]{1,0:T(8,128)(2,1)S(1)} %pad_maximum_fusion.2), channel_id=1, source_target_pairs={{0,4},{4,0},{8,12},{12,8},{16,20},{20,16},{24,28},{28,24},{1,5},{5... | collective-permute-start | bytes 614408 | tf_op jit(solution)/shard_map/ppermute | solution.py:210
  30.0 9.8 %collective-permute-done.8 = bf16[160,640]{1,0:T(8,128)(2,1)S(1)} collective-permute-done((bf16[160,640]{1,0:T(8,128)(2,1)S(1)}, bf16[160,640]{1,0:T(8,128)(2,1)S(1)}, u32[]{:S(2)}, u32[]{:S(2)}) %collective-permute-start.8) | collective-permute-done | bytes 204832 | tf_op jit(solution)/shard_map/ppermute | solution.py:210
  39.8 0.0 collective-permute-done.6
  39.8 0.0 collective-permute-done.7.refs_5_
  39.8 0.0 copy-start.7
  39.8 0.7 copy-done.7
  40.6 0.0 collective-permute-done.5
  40.6 1.0 %broadcast_select_fusion.1.refs_2_ = bf16[160,1280]{1,0:T(8,128)(2,1)S(1)} fusion(bf16[160,1280]{1,0:T(8,128)(2,1)S(1)} %collective-permute-done.1, bf16[160,1280]{1,0:T(8,128)(2,1)} %collective-permute-done.6, pred[]{:T(512)S(6)} %or.3), kind=kLoop, calls=%fused_computation.5 | loop fusion | flops 204800 | bytes 1228801 | tf_op jit(solution)/shard_map/jit(_where)/select_n | solution.py:253
  41.6 0.6 collective-permute-start.10
  42.2 1.3 %collective-permute-start.9 = (bf16[160,1280]{1,0:T(8,128)(2,1)S(1)}, bf16[160,1280]{1,0:T(8,128)(2,1)S(1)}, u32[]{:S(2)}, u32[]{:S(2)}) collective-permute-start(bf16[160,1280]{1,0:T(8,128)(2,1)S(1)} %collective-permute-done.5), channel_id=1, source_target_pairs={{8,0},{12,4},{16,24},{20,28},{9,1},{13,5},{17,25},{21,29},{10,2},{... | collective-permute-start | bytes 1228808 | tf_op jit(solution)/shard_map/ppermute | solution.py:232
  43.5 1.6 %collective-permute-start.11 = (bf16[320,640]{1,0:T(8,128)(2,1)S(1)}, bf16[320,640]{1,0:T(8,128)(2,1)}, u32[]{:S(2)}, u32[]{:S(2)}) collective-permute-start(bf16[320,640]{1,0:T(8,128)(2,1)S(1)} %pad_maximum_fusion.1), channel_id=1, source_target_pairs={{0,2},{1,3},{2,0},{3,1},{4,6},{5,7},{6,4},{7,5},{8,10},{9,11},{10,... | collective-permute-start | bytes 1228808 | tf_op jit(solution)/shard_map/ppermute | solution.py:210
  45.0 4.6 %collective-permute-done.10.refs_6_ = bf16[160,1280]{1,0:T(8,128)(2,1)S(1)} collective-permute-done((bf16[160,1280]{1,0:T(8,128)(2,1)S(1)}, bf16[160,1280]{1,0:T(8,128)(2,1)S(1)}, u32[]{:S(2)}, u32[]{:S(2)}) %collective-permute-start.10) | collective-permute-done | bytes 409632 | tf_op jit(solution)/shard_map/ppermute | solution.py:210
  49.6 0.8 copy-done.9
  50.4 1.8 %collective-permute-done.9 = bf16[160,1280]{1,0:T(8,128)(2,1)S(1)} collective-permute-done((bf16[160,1280]{1,0:T(8,128)(2,1)S(1)}, bf16[160,1280]{1,0:T(8,128)(2,1)S(1)}, u32[]{:S(2)}, u32[]{:S(2)}) %collective-permute-start.9) | collective-permute-done | bytes 409632 | tf_op jit(solution)/shard_map/ppermute | solution.py:232
  52.2 0.0 collective-permute-done.11
  52.2 0.0 copy-done.3
  52.2 0.0 copy-done.5
  52.3 0.0 copy-start.12
  52.3 0.0 copy-start
  52.3 0.0 copy-start.11
  52.3 1.1 %broadcast_select_fusion.3 = (bf16[320,640]{1,0:T(8,128)(2,1)S(1)}, bf16[320,640]{1,0:T(8,128)(2,1)S(1)}) fusion(bf16[320,640]{1,0:T(8,128)(2,1)S(1)} %pad_maximum_fusion.1, bf16[320,640]{1,0:T(8,128)(2,1)} %collective-permute-done.11, pred[]{:T(512)S(6)} %lt.39), kind=kLoop, calls=%fused_computation.7 | loop fusion | flops 409600 | bytes 1638401 | tf_op jit(solution)/shard_map/jit(_where)/select_n | solution.py:264
  53.4 0.1 pad_maximum_fusion
  53.5 0.1 collective-permute-start.12
  53.6 0.0 copy-done.12
  53.6 0.2 convert_reduce_fusion.low_ref
  53.8 0.1 broadcast_in_dim.2
  53.9 0.1 reshape_reshape.3.refs_8_
  54.0 0.1 stack.47.source_ref
  54.1 0.1 pad_add_fusion.where_ref
  54.2 1.6 %collective-permute-start.13 = (bf16[160,1280]{1,0:T(8,128)(2,1)S(1)}, bf16[160,1280]{1,0:T(8,128)(2,1)S(1)}, u32[]{:S(2)}, u32[]{:S(2)}) collective-permute-start(bf16[160,1280]{1,0:T(8,128)(2,1)S(1)} %broadcast_select_fusion.refs_3_), channel_id=1, source_target_pairs={{0,4},{4,0},{8,12},{12,8},{16,20},{20,16},{24,28},{28,24},{1,5},{5... | collective-permute-start | bytes 1228808 | tf_op jit(solution)/shard_map/ppermute | solution.py:210
  55.8 0.1 collective-permute-done.12.other_ref
  55.9 0.0 copy-done
  55.9 0.0 copy-done.11
  55.9 1.0 %copy-done.1 = bf16[512,512]{1,0:T(8,128)(2,1)S(1)} copy-done((bf16[512,512]{1,0:T(8,128)(2,1)S(1)}, bf16[512,512]{1,0:T(8,128)(2,1)}, u32[]{:S(2)}) %copy-start.1) | copy-done | bytes 524312
  57.0 0.0 copy-start.10
  57.0 9.4 %project.1 = (bf16[4,1280,192]{2,1,0:T(8,128)(2,1)S(1)}, bf16[1280,512]{1,0:T(8,128)(2,1)S(1)}, bf16[512,1280]{1,0:T(8,128)(2,1)S(1)}, bf16[160,768]{1,0:T(8,128)(2,1)}) custom-call(s32[16]{0:T(128)S(1)} %copy-done.11, s32[16]{0:T(128)S(1)} %convert_reduce_fusion.low_ref, s32[2]{0:T(128)S(1)} %pad_add_fusion.where_ref, bf16[640,640]{1,0:T(8,128)(2,1)S(1)} %bitcast.18, ...), custom_call_target="tpu_custom_call" | custom-call | flops 21474836480 | bytes 16777216 | tf_op jit(solution)/shard_map/project/pallas_call | solution.py:319
  66.4 0.0 collective-permute-done.13.refs_7_
  66.4 18.2 %keys.1 = (bf16[1280,512]{1,0:T(8,128)(2,1)S(1)}, bf16[1280,512]{1,0:T(8,128)(2,1)S(1)}, bf16[160,576]{1,0:T(8,128)(2,1)S(1)}) custom-call(s32[16]{0:T(128)S(1)} %convert_reduce_fusion.low_ref, s32[16]{0:T(128)S(1)} %copy-done.11, s32[8]{0:T(128)S(1)} %stack.47.source_ref, bf16[160,1280]{1,0:T(8,128)(2,1)S(1)} %constant_dynamic-update-slice_fusion.refs_0_, ...), custom_call_target="tpu_custom_call" | custom-call | flops 21474836480 | bytes 16777216 | tf_op jit(solution)/shard_map/keys/pallas_call | solution.py:349
  84.6 0.2 collective-permute-start.14
  84.8 1.3 %collective-permute-done.14 = bf16[160,576]{1,0:T(8,128)(2,1)S(1)} collective-permute-done((bf16[160,576]{1,0:T(8,128)(2,1)S(1)}, bf16[160,576]{1,0:T(8,128)(2,1)S(1)}, u32[]{:S(2)}, u32[]{:S(2)}) %collective-permute-start.14) | collective-permute-done | bytes 184352 | tf_op jit(solution)/shard_map/ppermute | solution.py:210
  86.1 0.1 convert_add_fusion.1
  86.2 1.5 %collective-permute-start.15 = (bf16[160,576]{1,0:T(8,128)(2,1)S(1)}, bf16[160,576]{1,0:T(8,128)(2,1)S(1)}, u32[]{:S(2)}, u32[]{:S(2)}) collective-permute-start(bf16[160,576]{1,0:T(8,128)(2,1)S(1)} %convert_add_fusion.1), channel_id=1, source_target_pairs={{0,2},{1,3},{2,0},{3,1},{4,6},{5,7},{6,4},{7,5},{8,10},{9,11},{10,... | collective-permute-start | bytes 552968 | tf_op jit(solution)/shard_map/ppermute | solution.py:210
  87.7 1.8 %fusion = f32[512,512]{1,0:T(8,128)} fusion(bf16[512,1280]{1,0:T(8,128)(2,1)S(1)} %get-tuple-element.51, bf16[1280,512]{1,0:T(8,128)(2,1)S(1)} %get-tuple-element.52), kind=kOutput, calls=%fused_computation.16 | convolution fusion | flops 671088640 | bytes 3670016 | tf_op jit(solution)/shard_map/dot_general | solution.py:30
  89.5 1.8 %fusion.1 = f32[512,512]{1,0:T(8,128)} fusion(bf16[512,1280]{1,0:T(8,128)(2,1)S(1)} %get-tuple-element.51, bf16[1280,512]{1,0:T(8,128)(2,1)S(1)} %get-tuple-element.53), kind=kOutput, calls=%fused_computation.17 | convolution fusion | flops 671088640 | bytes 3670016 | tf_op jit(solution)/shard_map/dot_general | solution.py:30
  91.4 2.0 %collective-permute-done.15 = bf16[160,576]{1,0:T(8,128)(2,1)S(1)} collective-permute-done((bf16[160,576]{1,0:T(8,128)(2,1)S(1)}, bf16[160,576]{1,0:T(8,128)(2,1)S(1)}, u32[]{:S(2)}, u32[]{:S(2)}) %collective-permute-start.15) | collective-permute-done | bytes 184352 | tf_op jit(solution)/shard_map/ppermute | solution.py:210
  93.4 0.8 convert_add_fusion
  (16 shorter events, 0.1 us)
Async XLA Ops:
  2.5 23.3 %collective-permute-start.2 = (bf16[160,1280]{1,0:T(8,128)(2,1)S(1)}, bf16[160,1280]{1,0:T(8,128)(2,1)S(1)}, u32[]{:S(2)}, u32[]{:S(2)}) collective-permute-start(bf16[160,1280]{1,0:T(8,128)(2,1)S(1)} %constant_dynamic-update-slice_fusion.refs_0_), channel_id=1, source_target_pairs={{0,4},{4,0},{8,12},{12,8},{16,20},{20,16},{24,28},{28,24},{1,5},{5... | collective-permute-start | bytes 1228808 | tf_op jit(solution)/shard_map/ppermute | solution.py:210
  5.6 20.3 %collective-permute-start.1 = (bf16[160,1280]{1,0:T(8,128)(2,1)S(1)}, bf16[160,1280]{1,0:T(8,128)(2,1)S(1)}, u32[]{:S(2)}, u32[]{:S(2)}) collective-permute-start(bf16[160,1280]{1,0:T(8,128)(2,1)S(1)} %constant_dynamic-update-slice_fusion.refs_0_), channel_id=1, source_target_pairs={{8,16},{12,20},{16,8},{20,12},{9,17},{13,21},{17,9},{21,13},{10,18... | collective-permute-start | bytes 1228808 | tf_op jit(solution)/shard_map/ppermute | solution.py:232
  6.2 19.6 %collective-permute-start = (bf16[160,1280]{1,0:T(8,128)(2,1)S(1)}, bf16[160,1280]{1,0:T(8,128)(2,1)S(1)}, u32[]{:S(2)}, u32[]{:S(2)}) collective-permute-start(bf16[160,1280]{1,0:T(8,128)(2,1)S(1)} %constant_dynamic-update-slice_fusion.refs_0_), channel_id=1, source_target_pairs={{0,8},{4,12},{8,0},{12,4},{16,24},{20,28},{24,16},{28,20},{1,9},{5... | collective-permute-start | bytes 1228808 | tf_op jit(solution)/shard_map/ppermute | solution.py:210
  11.5 9.5 %collective-permute-start.3 = (bf16[40,640]{1,0:T(8,128)(2,1)S(1)}, bf16[40,640]{1,0:T(8,128)(2,1)S(1)}, u32[]{:S(2)}, u32[]{:S(2)}) collective-permute-start(bf16[40,640]{1,0:T(8,128)(2,1)S(1)} %pad_dynamic-slice_fusion), channel_id=1, source_target_pairs={{0,16},{4,20},{8,24},{12,28},{16,0},{20,4},{24,8},{28,12},{1,17},{... | collective-permute-start | bytes 153608 | tf_op jit(solution)/shard_map/ppermute | solution.py:210
  21.0 4.7 %collective-permute-start.4 = (bf16[80,640]{1,0:T(8,128)(2,1)S(1)}, bf16[80,640]{1,0:T(8,128)(2,1)S(1)}, u32[]{:S(2)}, u32[]{:S(2)}) collective-permute-start(bf16[80,640]{1,0:T(8,128)(2,1)S(1)} %pad_maximum_fusion.3), channel_id=1, source_target_pairs={{0,8},{4,12},{8,0},{12,4},{16,24},{20,28},{24,16},{28,20},{1,9},{5... | collective-permute-start | bytes 307208 | tf_op jit(solution)/shard_map/ppermute | solution.py:210
  25.8 26.4 %copy-start.3 = (bf16[160,1280]{1,0:T(8,128)(2,1)}, bf16[160,1280]{1,0:T(8,128)(2,1)S(1)}, u32[]{:S(2)}) copy-start(bf16[160,1280]{1,0:T(8,128)(2,1)S(1)} %collective-permute-done.2.refs_4_) | copy-start | bytes 1228804
  25.8 26.4 %copy-start.5 = (bf16[160,1280]{1,0:T(8,128)(2,1)}, bf16[160,1280]{1,0:T(8,128)(2,1)S(1)}, u32[]{:S(2)}) copy-start(bf16[160,1280]{1,0:T(8,128)(2,1)S(1)} %collective-permute-done.refs_1_) | copy-start | bytes 1228804
  25.8 13.9 %collective-permute-start.6 = (bf16[160,1280]{1,0:T(8,128)(2,1)S(1)}, bf16[160,1280]{1,0:T(8,128)(2,1)}, u32[]{:S(2)}, u32[]{:S(2)}) collective-permute-start(bf16[160,1280]{1,0:T(8,128)(2,1)S(1)} %collective-permute-done.1), channel_id=1, source_target_pairs={{8,0},{12,4},{16,24},{20,28},{9,1},{13,5},{17,25},{21,29},{10,2},{... | collective-permute-start | bytes 1228808 | tf_op jit(solution)/shard_map/ppermute | solution.py:232
  27.1 12.7 %collective-permute-start.7 = (bf16[160,1280]{1,0:T(8,128)(2,1)S(1)}, bf16[160,1280]{1,0:T(8,128)(2,1)S(1)}, u32[]{:S(2)}, u32[]{:S(2)}) collective-permute-start(bf16[160,1280]{1,0:T(8,128)(2,1)S(1)} %collective-permute-done.refs_1_), channel_id=1, source_target_pairs={{0,4},{4,0},{8,12},{12,8},{16,20},{20,16},{24,28},{28,24},{1,5},{5... | collective-permute-start | bytes 1228808 | tf_op jit(solution)/shard_map/ppermute | solution.py:210
  27.7 12.8 %collective-permute-start.5 = (bf16[160,1280]{1,0:T(8,128)(2,1)S(1)}, bf16[160,1280]{1,0:T(8,128)(2,1)S(1)}, u32[]{:S(2)}, u32[]{:S(2)}) collective-permute-start(bf16[160,1280]{1,0:T(8,128)(2,1)S(1)} %collective-permute-done.refs_1_), channel_id=1, source_target_pairs={{8,16},{12,20},{16,8},{20,12},{9,17},{13,21},{17,9},{21,13},{10,18... | collective-permute-start | bytes 1228808 | tf_op jit(solution)/shard_map/ppermute | solution.py:232
  28.4 11.3 %collective-permute-start.8 = (bf16[160,640]{1,0:T(8,128)(2,1)S(1)}, bf16[160,640]{1,0:T(8,128)(2,1)S(1)}, u32[]{:S(2)}, u32[]{:S(2)}) collective-permute-start(bf16[160,640]{1,0:T(8,128)(2,1)S(1)} %pad_maximum_fusion.2), channel_id=1, source_target_pairs={{0,4},{4,0},{8,12},{12,8},{16,20},{20,16},{24,28},{28,24},{1,5},{5... | collective-permute-start | bytes 614408 | tf_op jit(solution)/shard_map/ppermute | solution.py:210
  39.8 0.8 copy-start.7
  41.6 8.0 %collective-permute-start.10 = (bf16[160,1280]{1,0:T(8,128)(2,1)S(1)}, bf16[160,1280]{1,0:T(8,128)(2,1)S(1)}, u32[]{:S(2)}, u32[]{:S(2)}) collective-permute-start(bf16[160,1280]{1,0:T(8,128)(2,1)S(1)} %broadcast_select_fusion.1.refs_2_), channel_id=1, source_target_pairs={{0,4},{4,0},{8,12},{12,8},{16,20},{20,16},{24,28},{28,24},{1,5},{5... | collective-permute-start | bytes 1228808 | tf_op jit(solution)/shard_map/ppermute | solution.py:210
  42.2 10.0 %collective-permute-start.9 = (bf16[160,1280]{1,0:T(8,128)(2,1)S(1)}, bf16[160,1280]{1,0:T(8,128)(2,1)S(1)}, u32[]{:S(2)}, u32[]{:S(2)}) collective-permute-start(bf16[160,1280]{1,0:T(8,128)(2,1)S(1)} %collective-permute-done.5), channel_id=1, source_target_pairs={{8,0},{12,4},{16,24},{20,28},{9,1},{13,5},{17,25},{21,29},{10,2},{... | collective-permute-start | bytes 1228808 | tf_op jit(solution)/shard_map/ppermute | solution.py:232
  43.5 8.7 %collective-permute-start.11 = (bf16[320,640]{1,0:T(8,128)(2,1)S(1)}, bf16[320,640]{1,0:T(8,128)(2,1)}, u32[]{:S(2)}, u32[]{:S(2)}) collective-permute-start(bf16[320,640]{1,0:T(8,128)(2,1)S(1)} %pad_maximum_fusion.1), channel_id=1, source_target_pairs={{0,2},{1,3},{2,0},{3,1},{4,6},{5,7},{6,4},{7,5},{8,10},{9,11},{10,... | collective-permute-start | bytes 1228808 | tf_op jit(solution)/shard_map/ppermute | solution.py:210
  49.6 0.8 copy-start.9
  52.3 1.4 %copy-start.12 = (s32[16]{0:T(128)S(1)}, s32[16]{0:T(128)}, u32[]{:S(2)}) copy-start(s32[16]{0:T(128)} %param.13) | copy-start | bytes 196
  52.3 3.6 %copy-start = (bf16[512,512]{1,0:T(8,128)(2,1)S(1)}, bf16[512,512]{1,0:T(8,128)(2,1)}, u32[]{:S(2)}) copy-start(bf16[512,512]{1,0:T(8,128)(2,1)} %refs_11_.1) | copy-start | bytes 1572868
  52.3 3.6 %copy-start.11 = (s32[16]{0:T(128)S(1)}, s32[16]{0:T(128)}, u32[]{:S(2)}) copy-start(s32[16]{0:T(128)} %order_ref.3) | copy-start | bytes 196
  53.5 2.4 %collective-permute-start.12 = (bf16[640,640]{1,0:T(8,128)(2,1)S(1)}, bf16[640,640]{1,0:T(8,128)(2,1)S(1)}, u32[]{:S(2)}, u32[]{:S(2)}) collective-permute-start(bf16[640,640]{1,0:T(8,128)(2,1)S(1)} %bitcast.17), channel_id=1, source_target_pairs={{0,1},{1,0},{2,3},{3,2},{4,5},{5,4},{6,7},{7,6},{8,9},{9,8},{10,11... | collective-permute-start | bytes 2457608 | tf_op jit(solution)/shard_map/ppermute | solution.py:210
  54.2 12.2 %collective-permute-start.13 = (bf16[160,1280]{1,0:T(8,128)(2,1)S(1)}, bf16[160,1280]{1,0:T(8,128)(2,1)S(1)}, u32[]{:S(2)}, u32[]{:S(2)}) collective-permute-start(bf16[160,1280]{1,0:T(8,128)(2,1)S(1)} %broadcast_select_fusion.refs_3_), channel_id=1, source_target_pairs={{0,4},{4,0},{8,12},{12,8},{16,20},{20,16},{24,28},{28,24},{1,5},{5... | collective-permute-start | bytes 1228808 | tf_op jit(solution)/shard_map/ppermute | solution.py:210
  55.9 1.0 %copy-start.1 = (bf16[512,512]{1,0:T(8,128)(2,1)S(1)}, bf16[512,512]{1,0:T(8,128)(2,1)}, u32[]{:S(2)}) copy-start(bf16[512,512]{1,0:T(8,128)(2,1)} %refs_12_.1) | copy-start | bytes 1572868
  57.0 9.4 %copy-start.2 = (bf16[512,512]{1,0:T(8,128)(2,1)S(1)}, bf16[512,512]{1,0:T(8,128)(2,1)}, u32[]{:S(2)}) copy-start(bf16[512,512]{1,0:T(8,128)(2,1)} %refs_12_.1) | copy-start | bytes 1572868
  57.0 9.4 %copy-start.4 = (bf16[160,1280]{1,0:T(8,128)(2,1)S(1)}, bf16[160,1280]{1,0:T(8,128)(2,1)}, u32[]{:S(2)}) copy-start(bf16[160,1280]{1,0:T(8,128)(2,1)} %copy-done.3) | copy-start | bytes 1228804
  57.0 9.4 %copy-start.6 = (bf16[160,1280]{1,0:T(8,128)(2,1)S(1)}, bf16[160,1280]{1,0:T(8,128)(2,1)}, u32[]{:S(2)}) copy-start(bf16[160,1280]{1,0:T(8,128)(2,1)} %copy-done.5) | copy-start | bytes 1228804
  57.0 9.4 %copy-start.8 = (bf16[160,1280]{1,0:T(8,128)(2,1)S(1)}, bf16[160,1280]{1,0:T(8,128)(2,1)}, u32[]{:S(2)}) copy-start(bf16[160,1280]{1,0:T(8,128)(2,1)} %copy-done.7) | copy-start | bytes 1228804
  57.0 9.4 %copy-start.10 = (bf16[160,1280]{1,0:T(8,128)(2,1)S(1)}, bf16[160,1280]{1,0:T(8,128)(2,1)}, u32[]{:S(2)}) copy-start(bf16[160,1280]{1,0:T(8,128)(2,1)} %copy-done.9) | copy-start | bytes 1228804
  84.6 1.5 %collective-permute-start.14 = (bf16[160,576]{1,0:T(8,128)(2,1)S(1)}, bf16[160,576]{1,0:T(8,128)(2,1)S(1)}, u32[]{:S(2)}, u32[]{:S(2)}) collective-permute-start(bf16[160,576]{1,0:T(8,128)(2,1)S(1)} %get-tuple-element.47), channel_id=1, source_target_pairs={{0,1},{1,0},{2,3},{3,2},{4,5},{5,4},{6,7},{7,6},{8,9},{9,8},{10,11... | collective-permute-start | bytes 552968 | tf_op jit(solution)/shard_map/ppermute | solution.py:210
  86.2 7.2 %collective-permute-start.15 = (bf16[160,576]{1,0:T(8,128)(2,1)S(1)}, bf16[160,576]{1,0:T(8,128)(2,1)S(1)}, u32[]{:S(2)}, u32[]{:S(2)}) collective-permute-start(bf16[160,576]{1,0:T(8,128)(2,1)S(1)} %convert_add_fusion.1), channel_id=1, source_target_pairs={{0,2},{1,3},{2,0},{3,1},{4,6},{5,7},{6,4},{7,5},{8,10},{9,11},{10,... | collective-permute-start | bytes 552968 | tf_op jit(solution)/shard_map/ppermute | solution.py:210

commit v3 on v2

--- a/solution.py
+++ b/solution.py
@@ -31,7 +31,7 @@
 
 
 def project_kernel(
-    devices, half, heads, pair, order_ref, low_ref, where_ref, mine_ref, other_ref, wk_in, wv_in, *refs
+    devices, half, heads, pair, resident, order_ref, low_ref, where_ref, mine_ref, other_ref, wk_in, wv_in, *refs
 ):
     x_refs = refs[: heads // pair]
     keys_ref, values_ref, turned_ref, dq_ref, latent, wk_ref, wv_ref, sem, weight_sem = refs[heads // pair :]
@@ -50,10 +50,13 @@
     for number, mask in enumerate(masks):
         for side, source in enumerate((mine_ref, other_ref)):
             block = order_ref[2 * (me ^ mask) + (core ^ side)]
+            rows = pl.ds(pl.multiple_of(block * half, 16), half)
+            from_rows = pl.ds(number * half, half)
+            if resident:
+                latent[rows, :] = source[from_rows, :]
+                continue
             copy = pltpu.make_async_copy(
-                source.at[pl.ds(number * half, half), :],
-                latent.at[pl.ds(pl.multiple_of(block * half, 16), half), :],
-                sem.at[2 * number + side],
+                source.at[from_rows, :], latent.at[rows, :], sem.at[2 * number + side]
             )
             copy.start()
             copies.append(copy)
@@ -98,19 +101,11 @@
         dq_ref[rows, :] = jnp.concatenate(outs, axis=1)
 
 
-def key_kernel(devices, half, here, begun, low_ref, order_ref, source_ref, *refs):
+def key_kernel(devices, half, here, begun, resident, low_ref, order_ref, source_ref, *refs):
     x_refs = refs[:devices]
-    low_rows_ref, *sources = refs[devices : devices + 5]
+    low_rows_ref, keys_ref, values_ref, wk_ref, wv_ref = refs[devices : devices + 5]
     dk_ref, dv_ref, dlat_ref = refs[devices + 5 + begun : devices + 8 + begun]
-    x_all, sum_nope, sum_value, sum_rope, sem = refs[devices + 8 + begun : devices + 13 + begun]
-    *held, held_sem = refs[devices + 13 + begun :]
-    keys_ref, values_ref, wk_ref, wv_ref = held
-    loads = [
-        pltpu.make_async_copy(source, target, held_sem.at[number])
-        for number, (source, target) in enumerate(zip(sources, held))
-    ]
-    for copy in loads:
-        copy.start()
+    x_all, sum_nope, sum_value, sum_rope, sem = refs[devices + 8 + begun :]
     blocks = 2 * devices
     total = blocks * half
     grad_at = here * WIDTH
@@ -119,17 +114,19 @@
         for side in range(2):
             block = order_ref[2 * source_ref[number] + side]
             rows = pl.ds(pl.multiple_of(block * half, 16), half)
+            from_rows = pl.ds(side * half, half)
+            if resident:
+                x_all[rows, :] = x_refs[number][from_rows, :]
+                continue
             copy = pltpu.make_async_copy(
-                x_refs[number].at[pl.ds(side * half, half), :],
-                x_all.at[rows, :],
-                sem.at[2 * number + side],
+                x_refs[number].at[from_rows, :], x_all.at[rows, :], sem.at[2 * number + side]
             )
             copy.start()
             copies.append(copy)
     sum_nope[...] = jnp.zeros_like(sum_nope)
     sum_value[...] = jnp.zeros_like(sum_value)
     sum_rope[...] = jnp.zeros_like(sum_rope)
-    for copy in loads[:2] + copies:
+    for copy in copies:
         copy.wait()
 
     def tile(first, start, span):
@@ -190,19 +187,19 @@
     lax.fori_loop(0, total // TILE, step, 0)
     dk_ref[...] = (sum_nope[...] * SCALE).astype(jnp.bfloat16)
     dv_ref[...] = sum_value[...].astype(jnp.bfloat16)
-    for copy in loads[2:]:
-        copy.wait()
+    own = []
     for side in range(2):
         block = order_ref[2 * source_ref[0] + side]
-        rows = pl.ds(pl.multiple_of(block * half, 16), half)
-        out = dot(dk_ref[rows, :], wk_ref[...], BY_COLUMNS)
-        out = out + dot(dv_ref[rows, :], wv_ref[...], BY_COLUMNS)
-        rope = sum_rope[rows, :] * SCALE
-        here_rows = pl.ds(side * half, half)
-        out = jnp.concatenate([out, rope], axis=1)
-        if begun:
-            out = out + refs[devices + 5][here_rows, :]
-        dlat_ref[here_rows, :] = out.astype(dlat_ref.dtype)
+        own.append(pl.ds(pl.multiple_of(block * half, 16), half))
+
+    def take(ref):
+        return jnp.concatenate([ref[rows, :] for rows in own], axis=0)
+
+    out = dot(take(dk_ref), wk_ref[...], BY_COLUMNS) + dot(take(dv_ref), wv_ref[...], BY_COLUMNS)
+    out = jnp.concatenate([out, take(sum_rope) * SCALE], axis=1)
+    if begun:
+        out = out + refs[devices + 5][...]
+    dlat_ref[...] = out.astype(dlat_ref.dtype)
 
 
 def swap(array, axis, mask):
@@ -239,12 +236,12 @@
     place = me // 2
     inner = (place == 1) | (place == 2)
     piece = mine.shape[0]
-    mine = join(mine, "seq", 4)
-    mine = join(mine, "seq", 2)
+    mine = jnp.concatenate([mine] + [swap(mine, "seq", mask) for mask in (4, 2, 6)], axis=0)
+    own, mine = hold((own, mine))
     near = swap(own, "seq", 2)
     third = along(own, middle)
     y_own = swap(own, "seq", 1)
-    near, third, y_own, mine = hold((near, third, y_own, mine))
+    near, third, y_own = hold((near, third, y_own))
     fourth = along(near, middle)
     handed = along(third, outward)
     y_near = swap(near, "seq", 1)
@@ -254,15 +251,15 @@
     last = along(fourth, outward)
     y_third = swap(third, "seq", 1)
     theirs = swap(mine, "head", 2)
-    last, y_third, mine, theirs = hold((last, y_third, mine, theirs))
-    fourth = jnp.where(inner, fourth, last)
-    fourth, mine, theirs = hold((fourth, mine, theirs))
-    y_fourth = swap(fourth, "seq", 1)
     first = lax.axis_index("head") < 2
     mine, theirs = (x.reshape(8, piece, mine.shape[1]) for x in (mine, theirs))
     mine = jnp.concatenate(
         [jnp.where(first, mine, theirs), jnp.where(first, theirs, mine)], axis=1
     ).reshape(16 * piece, mine.shape[2])
+    last, y_third, mine = hold((last, y_third, mine))
+    fourth = jnp.where(inner, fourth, last)
+    fourth, mine = hold((fourth, mine))
+    y_fourth = swap(fourth, "seq", 1)
     left = place < 2
     places = [place, place ^ 1, jnp.where(left, 2, 1), jnp.where(left, 3, 0)]
     y = me % 2
@@ -317,14 +314,14 @@
         return pltpu.CompilerParams(vmem_limit_bytes=(size if small else 60) * mebi)
 
     keys, values, turned, d_queries = pl.pallas_call(
-        functools.partial(project_kernel, devices, half, heads, pair),
+        functools.partial(project_kernel, devices, half, heads, pair, small),
         out_shape=(
             jax.ShapeDtypeStruct((heads, total, WIDTH), bf16),
             jax.ShapeDtypeStruct((total, heads * VDIM), bf16),
             jax.ShapeDtypeStruct((D_LAT, total), bf16),
             jax.ShapeDtypeStruct((local_rows, heads * WIDTH), bf16),
         ),
-        in_specs=[SMEM, SMEM, SMEM, HBM, HBM, HBM, HBM] + [VMEM] * len(packed),
+        in_specs=[SMEM, SMEM, SMEM] + [VMEM if small else HBM] * 2 + [HBM, HBM] + [VMEM] * len(packed),
         out_specs=(VMEM, VMEM, VMEM, VMEM),
         scratch_shapes=[
             pltpu.VMEM((total, LAT_LANES), bf16),
@@ -347,13 +344,13 @@
         pieces = gathered[first // pair]
         last = first + pair == heads
         dk, dv, *shares = pl.pallas_call(
-            functools.partial(key_kernel, devices, half, pair, len(shares)),
+            functools.partial(key_kernel, devices, half, pair, len(shares), small),
             out_shape=(
                 jax.ShapeDtypeStruct((total, pair * NOPE), bf16),
                 jax.ShapeDtypeStruct((total, pair * VDIM), bf16),
                 jax.ShapeDtypeStruct((local_rows, D_LAT + ROPE), bf16 if last else jnp.float32),
             ),
-            in_specs=[SMEM, SMEM, SMEM] + [HBM] * devices + [VMEM] + [HBM] * 4 + [VMEM] * len(shares),
+            in_specs=[SMEM, SMEM, SMEM] + [VMEM if small else HBM] * devices + [VMEM] * (5 + len(shares)),
             out_specs=(VMEM, VMEM, VMEM),
             scratch_shapes=[
                 pltpu.VMEM((total, pair * (WIDTH + VDIM)), bf16),
@@ -361,11 +358,6 @@
                 pltpu.VMEM((total, pair * VDIM), jnp.float32),
                 pltpu.VMEM((total, ROPE), jnp.float32),
                 pltpu.SemaphoreType.DMA((2 * devices,)),
-                pltpu.VMEM((pair, total, WIDTH), bf16),
-                pltpu.VMEM((total, pair * VDIM), bf16),
-                pltpu.VMEM((D_LAT, pair * NOPE), bf16),
-                pltpu.VMEM((D_LAT, pair * VDIM), bf16),
-                pltpu.SemaphoreType.DMA((4,)),
             ],
             compiler_params=params(28),
             cost_estimate=pl.CostEstimate(

time: 94.3 us -> 89.5 us (0.949)
  Pallas kernels: 27.5 us -> 21.4 us
  waiting for transfers between devices: 32.4 us -> 34.1 us
  starting transfers between devices: 20.5 us -> 21.6 us
  other arithmetic: 3.48 us -> 2.42 us
    pallas_call x1, Pallas kernels: 18.2 us -> 14.1 us  [shards(): pl.pallas_call(functools.partial(key_kernel, devices, half, pair, len(sha...]
    pallas_call x1, Pallas kernels: 9.37 us -> 7.3 us  [shards(): pl.pallas_call(functools.partial(project_kernel, devices, half, heads, pa...]
    ppermute x12 -> x13, waiting for transfers between devices: 30.7 us -> 32 us  [swap(): return lax.ppermute(array, axis, [(i, i ^ mask) for i in range(size)])]
    select_n x1, other arithmetic: 1.14 us -> 0.08 us  [gather_by_line(): jnp.where(first, mine, theirs)]
    select_n x1, other arithmetic: 0.04 us -> 1.05 us  [gather_by_line(): fourth = jnp.where(inner, fourth, last)]
    select_n x1, other arithmetic: 1.05 us -> 0.04 us  [gather_by_line(): third = jnp.where(inner, third, handed)]
    ppermute x12 -> x13, starting transfers between devices: 16.6 us -> 16.9 us  [swap(): return lax.ppermute(array, axis, [(i, i ^ mask) for i in range(size)])]
  transfers between devices with their start and end apart: 16 -> 17, of which waited for: 8 -> 12; matrix products, arithmetic and copies ran while one was open for 5% -> 7% of each run, Pallas kernels for 10% -> 8%
where the time goes in v3:
time: 89.5 us; the launch traced here: 89.6 us
  waiting for transfers between devices  34.1 us (38%)
  starting transfers between devices  21.6 us (24%)
  Pallas kernels  21.4 us (24%)
  local copies, waits for them, and re-layouts  5.59 us (6%)
  matrix products  3.62 us (4%)
  other arithmetic  2.42 us (3%)
  between operations  0.94 us (1%)
    ppermute x13, waiting for transfers between devices, swap(): return lax.ppermute(array, axis, [(i, i ^ mask) for i in range(size)])  32 us
    ppermute x13, starting transfers between devices, swap(): return lax.ppermute(array, axis, [(i, i ^ mask) for i in range(size)])  16.9 us
    pallas_call x1, Pallas kernels, shards(): pl.pallas_call(functools.partial(key_kernel, devices, half, pair, len(sha...  14.1 us
    pallas_call x1, Pallas kernels, shards(): pl.pallas_call(functools.partial(project_kernel, devices, half, heads, pa...  7.3 us
    ppermute x4, starting transfers between devices, along(): lax.ppermute(array, 'seq', [(2 * a + y, 2 * b + y) for a, b in pairs for...  4.66 us
    dot_general x2, matrix products, dot(): return lax.dot_general(a, b, dims, preferred_element_type=jnp.float32)  3.62 us
    unnamed x27, local copies, waits for them, and re-layouts  3.56 us
    ppermute x4, waiting for transfers between devices, along(): lax.ppermute(array, 'seq', [(2 * a + y, 2 * b + y) for a, b in pairs for...  2.01 us
  transfers between devices with their start and end apart: 17, of which 12 were waited for; matrix products, arithmetic and copies ran while one was open for 7% of the time, Pallas kernels for 8%

profile of v3, /device:TPU:0, one launch (start us, length us, event | category | flops | bytes accessed | tf_op | source)
XLA Modules:
  0.0 89.6 jit_solution(10251722987670961993)
XLA Ops:
  0.7 0.9 pad_dynamic-slice_fusion
  1.5 5.1 %collective-permute-start.2 = (bf16[40,640]{1,0:T(8,128)(2,1)S(1)}, bf16[40,640]{1,0:T(8,128)(2,1)S(1)}, u32[]{:S(2)}, u32[]{:S(2)}) collective-permute-start(bf16[40,640]{1,0:T(8,128)(2,1)S(1)} %pad_dynamic-slice_fusion), channel_id=1, source_target_pairs={{0,24},{4,28},{8,16},{12,20},{16,8},{20,12},{24,0},{28,4},{1,25},{... | collective-permute-start | bytes 153608 | tf_op jit(solution)/shard_map/ppermute | solution.py:207
  6.6 0.0 collective-permute-start.1
  6.6 0.6 collective-permute-start
  7.3 1.0 %constant_dynamic-update-slice_fusion.1 = bf16[160,1280]{1,0:T(8,128)(2,1)S(1)} fusion(bf16[160,768]{1,0:T(8,128)(2,1)} %param.7), kind=kLoop, calls=%fused_computation.12 | loop fusion | bytes 491520
  8.2 0.9 %constant_dynamic-update-slice_fusion.refs_0_ = bf16[160,1280]{1,0:T(8,128)(2,1)S(1)} fusion(bf16[160,1280]{1,0:T(8,128)(2,1)S(1)} %constant_dynamic-update-slice_fusion.1, bf16[160,512]{1,0:T(8,128)(2,1)} %param.11), kind=kLoop, calls=%fused_computation.11 | loop fusion | bytes 327680 | tf_op jit(solution)/shard_map/concatenate | solution.py:283
  9.2 0.0 collective-permute-done.2
  9.2 1.6 %collective-permute-done.1 = bf16[40,640]{1,0:T(8,128)(2,1)S(1)} collective-permute-done((bf16[40,640]{1,0:T(8,128)(2,1)S(1)}, bf16[40,640]{1,0:T(8,128)(2,1)S(1)}, u32[]{:S(2)}, u32[]{:S(2)}) %collective-permute-start.1) | collective-permute-done | bytes 51232 | tf_op jit(solution)/shard_map/ppermute | solution.py:207
  10.8 1.2 %collective-permute-done = bf16[40,640]{1,0:T(8,128)(2,1)S(1)} collective-permute-done((bf16[40,640]{1,0:T(8,128)(2,1)S(1)}, bf16[40,640]{1,0:T(8,128)(2,1)S(1)}, u32[]{:S(2)}, u32[]{:S(2)}) %collective-permute-start) | collective-permute-done | bytes 51232 | tf_op jit(solution)/shard_map/ppermute | solution.py:207
  12.0 1.6 %collective-permute-start.5 = (bf16[160,1280]{1,0:T(8,128)(2,1)S(1)}, bf16[160,1280]{1,0:T(8,128)(2,1)S(1)}, u32[]{:S(2)}, u32[]{:S(2)}) collective-permute-start(bf16[160,1280]{1,0:T(8,128)(2,1)S(1)} %constant_dynamic-update-slice_fusion.refs_0_), channel_id=1, source_target_pairs={{0,4},{4,0},{8,12},{12,8},{16,20},{20,16},{24,28},{28,24},{1,5},{5... | collective-permute-start | bytes 1228808 | tf_op jit(solution)/shard_map/ppermute | solution.py:207
  13.6 0.7 collective-permute-start.4
  14.3 3.2 %collective-permute-start.3 = (bf16[160,1280]{1,0:T(8,128)(2,1)S(1)}, bf16[160,1280]{1,0:T(8,128)(2,1)S(1)}, u32[]{:S(2)}, u32[]{:S(2)}) collective-permute-start(bf16[160,1280]{1,0:T(8,128)(2,1)S(1)} %constant_dynamic-update-slice_fusion.refs_0_), channel_id=1, source_target_pairs={{0,8},{4,12},{8,0},{12,4},{16,24},{20,28},{24,16},{28,20},{1,9},{5... | collective-permute-start | bytes 1228808 | tf_op jit(solution)/shard_map/ppermute | solution.py:207
  17.4 4.1 %collective-permute-done.5.refs_4_ = bf16[160,1280]{1,0:T(8,128)(2,1)S(1)} collective-permute-done((bf16[160,1280]{1,0:T(8,128)(2,1)S(1)}, bf16[160,1280]{1,0:T(8,128)(2,1)S(1)}, u32[]{:S(2)}, u32[]{:S(2)}) %collective-permute-start.5) | collective-permute-done | bytes 409632 | tf_op jit(solution)/shard_map/ppermute | solution.py:207
  21.5 0.7 copy-done.3
  22.3 0.0 collective-permute-done.4
  22.3 3.0 %collective-permute-done.3.refs_1_ = bf16[160,1280]{1,0:T(8,128)(2,1)S(1)} collective-permute-done((bf16[160,1280]{1,0:T(8,128)(2,1)S(1)}, bf16[160,1280]{1,0:T(8,128)(2,1)S(1)}, u32[]{:S(2)}, u32[]{:S(2)}) %collective-permute-start.3) | collective-permute-done | bytes 409632 | tf_op jit(solution)/shard_map/ppermute | solution.py:207
  25.2 1.3 %collective-permute-start.7 = (bf16[160,1280]{1,0:T(8,128)(2,1)S(1)}, bf16[160,1280]{1,0:T(8,128)(2,1)S(1)}, u32[]{:S(2)}, u32[]{:S(2)}) collective-permute-start(bf16[160,1280]{1,0:T(8,128)(2,1)S(1)} %collective-permute-done.4), channel_id=1, source_target_pairs={{8,0},{12,4},{16,24},{20,28},{9,1},{13,5},{17,25},{21,29},{10,2},{... | collective-permute-start | bytes 1228808 | tf_op jit(solution)/shard_map/ppermute | solution.py:229
  26.5 0.5 collective-permute-start.8
  27.0 1.4 %collective-permute-start.6 = (bf16[160,1280]{1,0:T(8,128)(2,1)S(1)}, bf16[160,1280]{1,0:T(8,128)(2,1)}, u32[]{:S(2)}, u32[]{:S(2)}) collective-permute-start(bf16[160,1280]{1,0:T(8,128)(2,1)S(1)} %collective-permute-done.3.refs_1_), channel_id=1, source_target_pairs={{8,16},{12,20},{16,8},{20,12},{9,17},{13,21},{17,9},{21,13},{10,18... | collective-permute-start | bytes 1228808 | tf_op jit(solution)/shard_map/ppermute | solution.py:229
  28.5 1.6 %collective-permute-start.9 = (bf16[160,640]{1,0:T(8,128)(2,1)S(1)}, bf16[160,640]{1,0:T(8,128)(2,1)S(1)}, u32[]{:S(2)}, u32[]{:S(2)}) collective-permute-start(bf16[160,640]{1,0:T(8,128)(2,1)S(1)} %pad_maximum_fusion.2), channel_id=1, source_target_pairs={{0,4},{4,0},{8,12},{12,8},{16,20},{20,16},{24,28},{28,24},{1,5},{5... | collective-permute-start | bytes 614408 | tf_op jit(solution)/shard_map/ppermute | solution.py:207
  30.0 9.8 %collective-permute-done.9 = bf16[160,640]{1,0:T(8,128)(2,1)S(1)} collective-permute-done((bf16[160,640]{1,0:T(8,128)(2,1)S(1)}, bf16[160,640]{1,0:T(8,128)(2,1)S(1)}, u32[]{:S(2)}, u32[]{:S(2)}) %collective-permute-start.9) | collective-permute-done | bytes 204832 | tf_op jit(solution)/shard_map/ppermute | solution.py:207
  39.9 0.0 collective-permute-done.7
  39.9 0.0 collective-permute-done.8.refs_5_
  39.9 0.0 copy-start.7
  39.9 0.0 collective-permute-done.6
  40.0 1.6 %collective-permute-start.12 = (bf16[320,640]{1,0:T(8,128)(2,1)S(1)}, bf16[320,640]{1,0:T(8,128)(2,1)S(1)}, u32[]{:S(2)}, u32[]{:S(2)}) collective-permute-start(bf16[320,640]{1,0:T(8,128)(2,1)S(1)} %pad_maximum_fusion.1), channel_id=1, source_target_pairs={{0,2},{1,3},{2,0},{3,1},{4,6},{5,7},{6,4},{7,5},{8,10},{9,11},{10,... | collective-permute-start | bytes 1228808 | tf_op jit(solution)/shard_map/ppermute | solution.py:207
  41.6 0.6 collective-permute-start.11
  42.2 1.3 %collective-permute-start.10 = (bf16[160,1280]{1,0:T(8,128)(2,1)}, bf16[160,1280]{1,0:T(8,128)(2,1)}, u32[]{:S(2)}, u32[]{:S(2)}) collective-permute-start(bf16[160,1280]{1,0:T(8,128)(2,1)} %collective-permute-done.6), channel_id=1, source_target_pairs={{8,0},{12,4},{16,24},{20,28},{9,1},{13,5},{17,25},{21,29},{10,2},{... | collective-permute-start | bytes 1228808 | tf_op jit(solution)/shard_map/ppermute | solution.py:229
  43.5 4.5 %collective-permute-done.12 = bf16[320,640]{1,0:T(8,128)(2,1)S(1)} collective-permute-done((bf16[320,640]{1,0:T(8,128)(2,1)S(1)}, bf16[320,640]{1,0:T(8,128)(2,1)S(1)}, u32[]{:S(2)}, u32[]{:S(2)}) %collective-permute-start.12) | collective-permute-done | bytes 409632 | tf_op jit(solution)/shard_map/ppermute | solution.py:207
  48.0 0.1 broadcast_select_fusion.1
  48.1 0.0 copy-done.5
  48.1 0.0 copy-done.7
  48.1 0.0 copy-start.12
  48.1 0.0 copy-start
  48.1 0.0 copy-start.11
  48.1 0.1 pad_maximum_fusion
  48.2 1.4 %collective-permute-done.11.refs_6_ = bf16[160,1280]{1,0:T(8,128)(2,1)S(1)} collective-permute-done((bf16[160,1280]{1,0:T(8,128)(2,1)S(1)}, bf16[160,1280]{1,0:T(8,128)(2,1)S(1)}, u32[]{:S(2)}, u32[]{:S(2)}) %collective-permute-start.11) | collective-permute-done | bytes 409632 | tf_op jit(solution)/shard_map/ppermute | solution.py:207
  49.6 0.8 copy-done.9
  50.4 2.0 %collective-permute-done.10 = bf16[160,1280]{1,0:T(8,128)(2,1)} collective-permute-done((bf16[160,1280]{1,0:T(8,128)(2,1)}, bf16[160,1280]{1,0:T(8,128)(2,1)}, u32[]{:S(2)}, u32[]{:S(2)}) %collective-permute-start.10) | collective-permute-done | bytes 409632 | tf_op jit(solution)/shard_map/ppermute | solution.py:229
  52.4 1.0 %broadcast_select_fusion.2.refs_3_ = bf16[160,1280]{1,0:T(8,128)(2,1)S(1)} fusion(bf16[160,1280]{1,0:T(8,128)(2,1)} %collective-permute-done.6, bf16[160,1280]{1,0:T(8,128)(2,1)} %collective-permute-done.10, pred[]{:T(512)S(6)} %or.3), kind=kLoop, calls=%fused_computation.6 | loop fusion | flops 204800 | bytes 1228801 | tf_op jit(solution)/shard_map/jit(_where)/select_n | solution.py:260
  53.4 0.1 collective-permute-start.13
  53.5 0.0 copy-done.12
  53.5 0.2 convert_reduce_fusion.low_ref
  53.7 0.1 broadcast_in_dim.2
  53.8 0.1 reshape_reshape.3.refs_8_
  53.9 0.1 stack.47.source_ref
  54.0 0.1 pad_add_fusion.where_ref
  54.0 1.5 %collective-permute-start.14 = (bf16[160,1280]{1,0:T(8,128)(2,1)S(1)}, bf16[160,1280]{1,0:T(8,128)(2,1)S(1)}, u32[]{:S(2)}, u32[]{:S(2)}) collective-permute-start(bf16[160,1280]{1,0:T(8,128)(2,1)S(1)} %broadcast_select_fusion.2.refs_3_), channel_id=1, source_target_pairs={{0,4},{4,0},{8,12},{12,8},{16,20},{20,16},{24,28},{28,24},{1,5},{5... | collective-permute-start | bytes 1228808 | tf_op jit(solution)/shard_map/ppermute | solution.py:207
  55.5 0.3 collective-permute-done.13.other_ref
  55.8 0.0 copy-done
  55.8 1.0 %copy-done.1 = bf16[512,512]{1,0:T(8,128)(2,1)S(1)} copy-done((bf16[512,512]{1,0:T(8,128)(2,1)S(1)}, bf16[512,512]{1,0:T(8,128)(2,1)}, u32[]{:S(2)}) %copy-start.1) | copy-done | bytes 524312
  56.9 0.0 copy-start.10
  56.9 7.3 %project.1 = (bf16[4,1280,192]{2,1,0:T(8,128)(2,1)S(1)}, bf16[1280,512]{1,0:T(8,128)(2,1)S(1)}, bf16[512,1280]{1,0:T(8,128)(2,1)S(1)}, bf16[160,768]{1,0:T(8,128)(2,1)}) custom-call(s32[16]{0:T(128)S(1)} %copy-done.11, s32[16]{0:T(128)S(1)} %convert_reduce_fusion.low_ref, s32[2]{0:T(128)S(1)} %pad_add_fusion.where_ref, bf16[640,640]{1,0:T(8,128)(2,1)S(1)} %bitcast.18, ...), custom_call_target="tpu_custom_call" | custom-call | flops 21474836480 | bytes 16777216 | tf_op jit(solution)/shard_map/project/pallas_call | solution.py:316
  64.2 1.7 %collective-permute-done.14.refs_7_ = bf16[160,1280]{1,0:T(8,128)(2,1)S(1)} collective-permute-done((bf16[160,1280]{1,0:T(8,128)(2,1)S(1)}, bf16[160,1280]{1,0:T(8,128)(2,1)S(1)}, u32[]{:S(2)}, u32[]{:S(2)}) %collective-permute-start.14) | collective-permute-done | bytes 409632 | tf_op jit(solution)/shard_map/ppermute | solution.py:207
  65.9 0.0 copy-done.2
  65.9 14.1 %keys.1 = (bf16[1280,512]{1,0:T(8,128)(2,1)S(1)}, bf16[1280,512]{1,0:T(8,128)(2,1)S(1)}, bf16[160,576]{1,0:T(8,128)(2,1)S(1)}) custom-call(s32[16]{0:T(128)S(1)} %convert_reduce_fusion.low_ref, s32[16]{0:T(128)S(1)} %copy-done.11, s32[8]{0:T(128)S(1)} %stack.47.source_ref, bf16[160,1280]{1,0:T(8,128)(2,1)S(1)} %constant_dynamic-update-slice_fusion.refs_0_, ...), custom_call_target="tpu_custom_call" | custom-call | flops 21474836480 | bytes 16777216 | tf_op jit(solution)/shard_map/keys/pallas_call | solution.py:346
  80.1 0.1 collective-permute-start.15
  80.1 1.4 %collective-permute-done.15 = bf16[160,576]{1,0:T(8,128)(2,1)S(1)} collective-permute-done((bf16[160,576]{1,0:T(8,128)(2,1)S(1)}, bf16[160,576]{1,0:T(8,128)(2,1)S(1)}, u32[]{:S(2)}, u32[]{:S(2)}) %collective-permute-start.15) | collective-permute-done | bytes 184352 | tf_op jit(solution)/shard_map/ppermute | solution.py:207
  81.6 0.1 convert_add_fusion.1
  81.6 0.5 collective-permute-start.16
  82.1 1.8 %fusion = f32[512,512]{1,0:T(8,128)} fusion(bf16[512,1280]{1,0:T(8,128)(2,1)S(1)} %get-tuple-element.49, bf16[1280,512]{1,0:T(8,128)(2,1)S(1)} %get-tuple-element.50), kind=kOutput, calls=%fused_computation.15 | convolution fusion | flops 671088640 | bytes 3670016 | tf_op jit(solution)/shard_map/dot_general | solution.py:30
  83.9 1.8 %fusion.1 = f32[512,512]{1,0:T(8,128)} fusion(bf16[512,1280]{1,0:T(8,128)(2,1)S(1)} %get-tuple-element.49, bf16[1280,512]{1,0:T(8,128)(2,1)S(1)} %get-tuple-element.51), kind=kOutput, calls=%fused_computation.16 | convolution fusion | flops 671088640 | bytes 3670016 | tf_op jit(solution)/shard_map/dot_general | solution.py:30
  85.7 3.1 %collective-permute-done.16 = bf16[160,576]{1,0:T(8,128)(2,1)S(1)} collective-permute-done((bf16[160,576]{1,0:T(8,128)(2,1)S(1)}, bf16[160,576]{1,0:T(8,128)(2,1)S(1)}, u32[]{:S(2)}, u32[]{:S(2)}) %collective-permute-start.16) | collective-permute-done | bytes 184352 | tf_op jit(solution)/shard_map/ppermute | solution.py:207
  88.8 0.8 convert_add_fusion
  (17 shorter events, 0.1 us)
Async XLA Ops:
  1.5 7.7 %collective-permute-start.2 = (bf16[40,640]{1,0:T(8,128)(2,1)S(1)}, bf16[40,640]{1,0:T(8,128)(2,1)S(1)}, u32[]{:S(2)}, u32[]{:S(2)}) collective-permute-start(bf16[40,640]{1,0:T(8,128)(2,1)S(1)} %pad_dynamic-slice_fusion), channel_id=1, source_target_pairs={{0,24},{4,28},{8,16},{12,20},{16,8},{20,12},{24,0},{28,4},{1,25},{... | collective-permute-start | bytes 153608 | tf_op jit(solution)/shard_map/ppermute | solution.py:207
  6.6 4.1 %collective-permute-start.1 = (bf16[40,640]{1,0:T(8,128)(2,1)S(1)}, bf16[40,640]{1,0:T(8,128)(2,1)S(1)}, u32[]{:S(2)}, u32[]{:S(2)}) collective-permute-start(bf16[40,640]{1,0:T(8,128)(2,1)S(1)} %pad_dynamic-slice_fusion), channel_id=1, source_target_pairs={{0,8},{4,12},{8,0},{12,4},{16,24},{20,28},{24,16},{28,20},{1,9},{5... | collective-permute-start | bytes 153608 | tf_op jit(solution)/shard_map/ppermute | solution.py:207
  6.6 5.3 %collective-permute-start = (bf16[40,640]{1,0:T(8,128)(2,1)S(1)}, bf16[40,640]{1,0:T(8,128)(2,1)S(1)}, u32[]{:S(2)}, u32[]{:S(2)}) collective-permute-start(bf16[40,640]{1,0:T(8,128)(2,1)S(1)} %pad_dynamic-slice_fusion), channel_id=1, source_target_pairs={{0,16},{4,20},{8,24},{12,28},{16,0},{20,4},{24,8},{28,12},{1,17},{... | collective-permute-start | bytes 153608 | tf_op jit(solution)/shard_map/ppermute | solution.py:207
  12.0 9.5 %collective-permute-start.5 = (bf16[160,1280]{1,0:T(8,128)(2,1)S(1)}, bf16[160,1280]{1,0:T(8,128)(2,1)S(1)}, u32[]{:S(2)}, u32[]{:S(2)}) collective-permute-start(bf16[160,1280]{1,0:T(8,128)(2,1)S(1)} %constant_dynamic-update-slice_fusion.refs_0_), channel_id=1, source_target_pairs={{0,4},{4,0},{8,12},{12,8},{16,20},{20,16},{24,28},{28,24},{1,5},{5... | collective-permute-start | bytes 1228808 | tf_op jit(solution)/shard_map/ppermute | solution.py:207
  13.6 8.7 %collective-permute-start.4 = (bf16[160,1280]{1,0:T(8,128)(2,1)S(1)}, bf16[160,1280]{1,0:T(8,128)(2,1)S(1)}, u32[]{:S(2)}, u32[]{:S(2)}) collective-permute-start(bf16[160,1280]{1,0:T(8,128)(2,1)S(1)} %constant_dynamic-update-slice_fusion.refs_0_), channel_id=1, source_target_pairs={{8,16},{12,20},{16,8},{20,12},{9,17},{13,21},{17,9},{21,13},{10,18... | collective-permute-start | bytes 1228808 | tf_op jit(solution)/shard_map/ppermute | solution.py:229
  14.3 11.0 %collective-permute-start.3 = (bf16[160,1280]{1,0:T(8,128)(2,1)S(1)}, bf16[160,1280]{1,0:T(8,128)(2,1)S(1)}, u32[]{:S(2)}, u32[]{:S(2)}) collective-permute-start(bf16[160,1280]{1,0:T(8,128)(2,1)S(1)} %constant_dynamic-update-slice_fusion.refs_0_), channel_id=1, source_target_pairs={{0,8},{4,12},{8,0},{12,4},{16,24},{20,28},{24,16},{28,20},{1,9},{5... | collective-permute-start | bytes 1228808 | tf_op jit(solution)/shard_map/ppermute | solution.py:207
  21.5 0.8 copy-start.3
  25.2 22.8 %copy-start.5 = (bf16[160,1280]{1,0:T(8,128)(2,1)}, bf16[160,1280]{1,0:T(8,128)(2,1)S(1)}, u32[]{:S(2)}) copy-start(bf16[160,1280]{1,0:T(8,128)(2,1)S(1)} %collective-permute-done.3.refs_1_) | copy-start | bytes 1228804
  25.2 14.7 %collective-permute-start.7 = (bf16[160,1280]{1,0:T(8,128)(2,1)S(1)}, bf16[160,1280]{1,0:T(8,128)(2,1)S(1)}, u32[]{:S(2)}, u32[]{:S(2)}) collective-permute-start(bf16[160,1280]{1,0:T(8,128)(2,1)S(1)} %collective-permute-done.4), channel_id=1, source_target_pairs={{8,0},{12,4},{16,24},{20,28},{9,1},{13,5},{17,25},{21,29},{10,2},{... | collective-permute-start | bytes 1228808 | tf_op jit(solution)/shard_map/ppermute | solution.py:229
  26.5 13.4 %collective-permute-start.8 = (bf16[160,1280]{1,0:T(8,128)(2,1)S(1)}, bf16[160,1280]{1,0:T(8,128)(2,1)S(1)}, u32[]{:S(2)}, u32[]{:S(2)}) collective-permute-start(bf16[160,1280]{1,0:T(8,128)(2,1)S(1)} %collective-permute-done.3.refs_1_), channel_id=1, source_target_pairs={{0,4},{4,0},{8,12},{12,8},{16,20},{20,16},{24,28},{28,24},{1,5},{5... | collective-permute-start | bytes 1228808 | tf_op jit(solution)/shard_map/ppermute | solution.py:207
  27.0 12.9 %collective-permute-start.6 = (bf16[160,1280]{1,0:T(8,128)(2,1)S(1)}, bf16[160,1280]{1,0:T(8,128)(2,1)}, u32[]{:S(2)}, u32[]{:S(2)}) collective-permute-start(bf16[160,1280]{1,0:T(8,128)(2,1)S(1)} %collective-permute-done.3.refs_1_), channel_id=1, source_target_pairs={{8,16},{12,20},{16,8},{20,12},{9,17},{13,21},{17,9},{21,13},{10,18... | collective-permute-start | bytes 1228808 | tf_op jit(solution)/shard_map/ppermute | solution.py:229
  28.5 11.4 %collective-permute-start.9 = (bf16[160,640]{1,0:T(8,128)(2,1)S(1)}, bf16[160,640]{1,0:T(8,128)(2,1)S(1)}, u32[]{:S(2)}, u32[]{:S(2)}) collective-permute-start(bf16[160,640]{1,0:T(8,128)(2,1)S(1)} %pad_maximum_fusion.2), channel_id=1, source_target_pairs={{0,4},{4,0},{8,12},{12,8},{16,20},{20,16},{24,28},{28,24},{1,5},{5... | collective-permute-start | bytes 614408 | tf_op jit(solution)/shard_map/ppermute | solution.py:207
  39.9 8.1 %copy-start.7 = (bf16[160,1280]{1,0:T(8,128)(2,1)}, bf16[160,1280]{1,0:T(8,128)(2,1)S(1)}, u32[]{:S(2)}) copy-start(bf16[160,1280]{1,0:T(8,128)(2,1)S(1)} %collective-permute-done.8.refs_5_) | copy-start | bytes 1228804
  40.0 8.0 %collective-permute-start.12 = (bf16[320,640]{1,0:T(8,128)(2,1)S(1)}, bf16[320,640]{1,0:T(8,128)(2,1)S(1)}, u32[]{:S(2)}, u32[]{:S(2)}) collective-permute-start(bf16[320,640]{1,0:T(8,128)(2,1)S(1)} %pad_maximum_fusion.1), channel_id=1, source_target_pairs={{0,2},{1,3},{2,0},{3,1},{4,6},{5,7},{6,4},{7,5},{8,10},{9,11},{10,... | collective-permute-start | bytes 1228808 | tf_op jit(solution)/shard_map/ppermute | solution.py:207
  41.6 8.0 %collective-permute-start.11 = (bf16[160,1280]{1,0:T(8,128)(2,1)S(1)}, bf16[160,1280]{1,0:T(8,128)(2,1)S(1)}, u32[]{:S(2)}, u32[]{:S(2)}) collective-permute-start(bf16[160,1280]{1,0:T(8,128)(2,1)S(1)} %broadcast_select_fusion.3.refs_2_), channel_id=1, source_target_pairs={{0,4},{4,0},{8,12},{12,8},{16,20},{20,16},{24,28},{28,24},{1,5},{5... | collective-permute-start | bytes 1228808 | tf_op jit(solution)/shard_map/ppermute | solution.py:207
  42.2 10.2 %collective-permute-start.10 = (bf16[160,1280]{1,0:T(8,128)(2,1)}, bf16[160,1280]{1,0:T(8,128)(2,1)}, u32[]{:S(2)}, u32[]{:S(2)}) collective-permute-start(bf16[160,1280]{1,0:T(8,128)(2,1)} %collective-permute-done.6), channel_id=1, source_target_pairs={{8,0},{12,4},{16,24},{20,28},{9,1},{13,5},{17,25},{21,29},{10,2},{... | collective-permute-start | bytes 1228808 | tf_op jit(solution)/shard_map/ppermute | solution.py:229
  48.1 5.4 %copy-start.12 = (s32[16]{0:T(128)S(1)}, s32[16]{0:T(128)}, u32[]{:S(2)}) copy-start(s32[16]{0:T(128)} %param.13) | copy-start | bytes 196
  48.1 7.7 %copy-start = (bf16[512,512]{1,0:T(8,128)(2,1)S(1)}, bf16[512,512]{1,0:T(8,128)(2,1)}, u32[]{:S(2)}) copy-start(bf16[512,512]{1,0:T(8,128)(2,1)} %refs_11_.1) | copy-start | bytes 1572868
  48.1 7.7 %copy-start.11 = (s32[16]{0:T(128)S(1)}, s32[16]{0:T(128)}, u32[]{:S(2)}) copy-start(s32[16]{0:T(128)} %order_ref.3) | copy-start | bytes 196
  49.6 0.8 copy-start.9
  53.4 2.4 %collective-permute-start.13 = (bf16[640,640]{1,0:T(8,128)(2,1)S(1)}, bf16[640,640]{1,0:T(8,128)(2,1)S(1)}, u32[]{:S(2)}, u32[]{:S(2)}) collective-permute-start(bf16[640,640]{1,0:T(8,128)(2,1)S(1)} %bitcast.17), channel_id=1, source_target_pairs={{0,1},{1,0},{2,3},{3,2},{4,5},{5,4},{6,7},{7,6},{8,9},{9,8},{10,11... | collective-permute-start | bytes 2457608 | tf_op jit(solution)/shard_map/ppermute | solution.py:207
  54.0 11.8 %collective-permute-start.14 = (bf16[160,1280]{1,0:T(8,128)(2,1)S(1)}, bf16[160,1280]{1,0:T(8,128)(2,1)S(1)}, u32[]{:S(2)}, u32[]{:S(2)}) collective-permute-start(bf16[160,1280]{1,0:T(8,128)(2,1)S(1)} %broadcast_select_fusion.2.refs_3_), channel_id=1, source_target_pairs={{0,4},{4,0},{8,12},{12,8},{16,20},{20,16},{24,28},{28,24},{1,5},{5... | collective-permute-start | bytes 1228808 | tf_op jit(solution)/shard_map/ppermute | solution.py:207
  55.8 1.0 %copy-start.1 = (bf16[512,512]{1,0:T(8,128)(2,1)S(1)}, bf16[512,512]{1,0:T(8,128)(2,1)}, u32[]{:S(2)}) copy-start(bf16[512,512]{1,0:T(8,128)(2,1)} %refs_12_.1) | copy-start | bytes 1572868
  56.9 9.0 %copy-start.2 = (bf16[512,512]{1,0:T(8,128)(2,1)S(1)}, bf16[512,512]{1,0:T(8,128)(2,1)}, u32[]{:S(2)}) copy-start(bf16[512,512]{1,0:T(8,128)(2,1)} %refs_12_.1) | copy-start | bytes 1572868
  56.9 9.0 %copy-start.4 = (bf16[160,1280]{1,0:T(8,128)(2,1)S(1)}, bf16[160,1280]{1,0:T(8,128)(2,1)}, u32[]{:S(2)}) copy-start(bf16[160,1280]{1,0:T(8,128)(2,1)} %copy-done.3) | copy-start | bytes 1228804
  56.9 9.0 %copy-start.6 = (bf16[160,1280]{1,0:T(8,128)(2,1)S(1)}, bf16[160,1280]{1,0:T(8,128)(2,1)}, u32[]{:S(2)}) copy-start(bf16[160,1280]{1,0:T(8,128)(2,1)} %copy-done.5) | copy-start | bytes 1228804
  56.9 9.0 %copy-start.8 = (bf16[160,1280]{1,0:T(8,128)(2,1)S(1)}, bf16[160,1280]{1,0:T(8,128)(2,1)}, u32[]{:S(2)}) copy-start(bf16[160,1280]{1,0:T(8,128)(2,1)} %copy-done.7) | copy-start | bytes 1228804
  56.9 9.0 %copy-start.10 = (bf16[160,1280]{1,0:T(8,128)(2,1)S(1)}, bf16[160,1280]{1,0:T(8,128)(2,1)}, u32[]{:S(2)}) copy-start(bf16[160,1280]{1,0:T(8,128)(2,1)} %copy-done.9) | copy-start | bytes 1228804
  80.1 1.5 %collective-permute-start.15 = (bf16[160,576]{1,0:T(8,128)(2,1)S(1)}, bf16[160,576]{1,0:T(8,128)(2,1)S(1)}, u32[]{:S(2)}, u32[]{:S(2)}) collective-permute-start(bf16[160,576]{1,0:T(8,128)(2,1)S(1)} %get-tuple-element.45), channel_id=1, source_target_pairs={{0,1},{1,0},{2,3},{3,2},{4,5},{5,4},{6,7},{7,6},{8,9},{9,8},{10,11... | collective-permute-start | bytes 552968 | tf_op jit(solution)/shard_map/ppermute | solution.py:207
  81.6 7.2 %collective-permute-start.16 = (bf16[160,576]{1,0:T(8,128)(2,1)S(1)}, bf16[160,576]{1,0:T(8,128)(2,1)S(1)}, u32[]{:S(2)}, u32[]{:S(2)}) collective-permute-start(bf16[160,576]{1,0:T(8,128)(2,1)S(1)} %convert_add_fusion.1), channel_id=1, source_target_pairs={{0,2},{1,3},{2,0},{3,1},{4,6},{5,7},{6,4},{7,5},{8,10},{9,11},{10,... | collective-permute-start | bytes 552968 | tf_op jit(solution)/shard_map/ppermute | solution.py:207

commit v4 on v3

--- a/solution.py
+++ b/solution.py
@@ -241,30 +241,30 @@
     near = swap(own, "seq", 2)
     third = along(own, middle)
     y_own = swap(own, "seq", 1)
-    near, third, y_own = hold((near, third, y_own))
+    mine = join(mine, "seq", 1)
+    near, third, y_own, mine = hold((near, third, y_own, mine))
     fourth = along(near, middle)
     handed = along(third, outward)
     y_near = swap(near, "seq", 1)
-    mine = join(mine, "seq", 1)
-    fourth, handed, y_near, mine = hold((fourth, handed, y_near, mine))
+    theirs = swap(mine, "head", 2)
+    fourth, handed, y_near, mine, theirs = hold((fourth, handed, y_near, mine, theirs))
     third = jnp.where(inner, third, handed)
     last = along(fourth, outward)
     y_third = swap(third, "seq", 1)
-    theirs = swap(mine, "head", 2)
     first = lax.axis_index("head") < 2
     mine, theirs = (x.reshape(8, piece, mine.shape[1]) for x in (mine, theirs))
     mine = jnp.concatenate(
         [jnp.where(first, mine, theirs), jnp.where(first, theirs, mine)], axis=1
     ).reshape(16 * piece, mine.shape[2])
-    last, y_third, mine = hold((last, y_third, mine))
+    other = swap(mine, "head", 1)
+    last, y_third = hold((last, y_third))
     fourth = jnp.where(inner, fourth, last)
-    fourth, mine = hold((fourth, mine))
     y_fourth = swap(fourth, "seq", 1)
     left = place < 2
     places = [place, place ^ 1, jnp.where(left, 2, 1), jnp.where(left, 3, 0)]
     y = me % 2
     sources = [2 * p + y for p in places] + [2 * p + 1 - y for p in places]
-    return [own, near, third, fourth, y_own, y_near, y_third, y_fourth], jnp.stack(sources), mine
+    return [own, near, third, fourth, y_own, y_near, y_third, y_fourth], jnp.stack(sources), mine, other
 
 
 def shards(queries, latent_rope, w_uk, w_uv, d_out, block_order, block_doc):
@@ -298,14 +298,14 @@
         mine = lax.dynamic_slice_in_dim(
             mine, lax.axis_index("head") // 2 * (half // 2), half // 2, axis=0
         )
-        pieces, sources, mine = gather_by_line(packed[0], mine, me)
+        pieces, sources, mine, other = gather_by_line(packed[0], mine, me)
         gathered = [pieces]
     else:
         mine = gather_latent(mine, devices)
         gathered = [gather(x, devices) for x in packed]
         order = list(range(0, devices, 2)) + list(range(1, devices, 2))
         sources = jnp.stack([me ^ m for m in order])
-    other = swap(mine, "head", 1)
+        other = swap(mine, "head", 1)
 
     bf16 = jnp.bfloat16
     mebi = 1024 * 1024

time: 89.5 us -> 85.4 us (0.954)
  waiting for transfers between devices: 34.1 us -> 30.7 us
  local copies, waits for them, and re-layouts: 5.59 us -> 3.79 us
  starting transfers between devices: 21.6 us -> 22.6 us
    ppermute x13, waiting for transfers between devices: 32 us -> 21.7 us  [swap(): return lax.ppermute(array, axis, [(i, i ^ mask) for i in range(size)])]
    ppermute x4, waiting for transfers between devices: 2.01 us -> 9.05 us  [along(): lax.ppermute(array, 'seq', [(2 * a + y, 2 * b + y) for a, b in pairs for...]
    unnamed x27 -> x21, local copies, waits for them, and re-layouts: 3.56 us -> 1.76 us
    ppermute x13, starting transfers between devices: 16.9 us -> 18 us  [swap(): return lax.ppermute(array, axis, [(i, i ^ mask) for i in range(size)])]
  transfers between devices with their start and end apart: 17 -> 17, of which waited for: 12 -> 9; matrix products, arithmetic and copies ran while one was open for 7% -> 8% of each run, Pallas kernels for 8% -> 8%
where the time goes in v4:
time: 85.4 us; the launch traced here: 85.5 us
  waiting for transfers between devices  30.7 us (36%)
  starting transfers between devices  22.6 us (26%)
  Pallas kernels  21.3 us (25%)
  local copies, waits for them, and re-layouts  3.79 us (4%)
  matrix products  3.62 us (4%)
  other arithmetic  2.42 us (3%)
  between operations  0.94 us (1%)
    ppermute x13, waiting for transfers between devices, swap(): return lax.ppermute(array, axis, [(i, i ^ mask) for i in range(size)])  21.7 us
    ppermute x13, starting transfers between devices, swap(): return lax.ppermute(array, axis, [(i, i ^ mask) for i in range(size)])  18 us
    pallas_call x1, Pallas kernels, shards(): pl.pallas_call(functools.partial(key_kernel, devices, half, pair, len(sha...  14.1 us
    ppermute x4, waiting for transfers between devices, along(): lax.ppermute(array, 'seq', [(2 * a + y, 2 * b + y) for a, b in pairs for...  9.05 us
    pallas_call x1, Pallas kernels, shards(): pl.pallas_call(functools.partial(project_kernel, devices, half, heads, pa...  7.27 us
    ppermute x4, starting transfers between devices, along(): lax.ppermute(array, 'seq', [(2 * a + y, 2 * b + y) for a, b in pairs for...  4.66 us
    dot_general x2, matrix products, dot(): return lax.dot_general(a, b, dims, preferred_element_type=jnp.float32)  3.62 us
    unnamed x21, local copies, waits for them, and re-layouts  1.76 us
  transfers between devices with their start and end apart: 17, of which 9 were waited for; matrix products, arithmetic and copies ran while one was open for 8% of the time, Pallas kernels for 8%

profile of v4, /device:TPU:0, one launch (start us, length us, event | category | flops | bytes accessed | tf_op | source)
XLA Modules:
  0.0 85.5 jit_solution(12159605086309576889)
XLA Ops:
  0.6 0.0 copy-start.9
  0.7 0.9 %pad_dynamic-slice_fusion = bf16[40,640]{1,0:T(8,128)(2,1)S(1)} fusion(s32[]{:T(128)S(6)} %dynamic_slice.7, bf16[160,576]{1,0:T(8,128)(2,1)} %param.8), kind=kLoop, calls=%fused_computation.9 | loop fusion | bytes 235524 | tf_op jit(solution)/shard_map/dynamic_slice | solution.py:298
  1.5 5.1 %collective-permute-start.2 = (bf16[40,640]{1,0:T(8,128)(2,1)S(1)}, bf16[40,640]{1,0:T(8,128)(2,1)S(1)}, u32[]{:S(2)}, u32[]{:S(2)}) collective-permute-start(bf16[40,640]{1,0:T(8,128)(2,1)S(1)} %pad_dynamic-slice_fusion), channel_id=1, source_target_pairs={{0,24},{4,28},{8,16},{12,20},{16,8},{20,12},{24,0},{28,4},{1,25},{... | collective-permute-start | bytes 153608 | tf_op jit(solution)/shard_map/ppermute | solution.py:207
  6.7 0.0 collective-permute-start.1
  6.7 0.6 collective-permute-start
  7.3 1.0 %constant_dynamic-update-slice_fusion.1 = bf16[160,1280]{1,0:T(8,128)(2,1)S(1)} fusion(bf16[160,768]{1,0:T(8,128)(2,1)} %param.7), kind=kLoop, calls=%fused_computation.12 | loop fusion | bytes 491520
  8.3 0.9 %constant_dynamic-update-slice_fusion.refs_0_ = bf16[160,1280]{1,0:T(8,128)(2,1)S(1)} fusion(bf16[160,1280]{1,0:T(8,128)(2,1)S(1)} %constant_dynamic-update-slice_fusion.1, bf16[160,512]{1,0:T(8,128)(2,1)} %param.11), kind=kLoop, calls=%fused_computation.11 | loop fusion | bytes 327680 | tf_op jit(solution)/shard_map/concatenate | solution.py:283
  9.2 0.0 collective-permute-done.2
  9.2 1.6 %collective-permute-done.1 = bf16[40,640]{1,0:T(8,128)(2,1)S(1)} collective-permute-done((bf16[40,640]{1,0:T(8,128)(2,1)S(1)}, bf16[40,640]{1,0:T(8,128)(2,1)S(1)}, u32[]{:S(2)}, u32[]{:S(2)}) %collective-permute-start.1) | collective-permute-done | bytes 51232 | tf_op jit(solution)/shard_map/ppermute | solution.py:207
  10.8 1.2 %collective-permute-done = bf16[40,640]{1,0:T(8,128)(2,1)S(1)} collective-permute-done((bf16[40,640]{1,0:T(8,128)(2,1)S(1)}, bf16[40,640]{1,0:T(8,128)(2,1)S(1)}, u32[]{:S(2)}, u32[]{:S(2)}) %collective-permute-start) | collective-permute-done | bytes 51232 | tf_op jit(solution)/shard_map/ppermute | solution.py:207
  12.0 1.6 %collective-permute-start.5 = (bf16[160,1280]{1,0:T(8,128)(2,1)S(1)}, bf16[160,1280]{1,0:T(8,128)(2,1)S(1)}, u32[]{:S(2)}, u32[]{:S(2)}) collective-permute-start(bf16[160,1280]{1,0:T(8,128)(2,1)S(1)} %constant_dynamic-update-slice_fusion.refs_0_), channel_id=1, source_target_pairs={{0,4},{4,0},{8,12},{12,8},{16,20},{20,16},{24,28},{28,24},{1,5},{5... | collective-permute-start | bytes 1228808 | tf_op jit(solution)/shard_map/ppermute | solution.py:207
  13.6 0.7 collective-permute-start.4
  14.3 3.2 %collective-permute-start.3 = (bf16[160,1280]{1,0:T(8,128)(2,1)S(1)}, bf16[160,1280]{1,0:T(8,128)(2,1)S(1)}, u32[]{:S(2)}, u32[]{:S(2)}) collective-permute-start(bf16[160,1280]{1,0:T(8,128)(2,1)S(1)} %constant_dynamic-update-slice_fusion.refs_0_), channel_id=1, source_target_pairs={{0,8},{4,12},{8,0},{12,4},{16,24},{20,28},{24,16},{28,20},{1,9},{5... | collective-permute-start | bytes 1228808 | tf_op jit(solution)/shard_map/ppermute | solution.py:207
  17.5 0.5 collective-permute-start.6
  17.9 8.0 %collective-permute-done.6 = bf16[160,640]{1,0:T(8,128)(2,1)S(1)} collective-permute-done((bf16[160,640]{1,0:T(8,128)(2,1)S(1)}, bf16[160,640]{1,0:T(8,128)(2,1)S(1)}, u32[]{:S(2)}, u32[]{:S(2)}) %collective-permute-start.6) | collective-permute-done | bytes 204832 | tf_op jit(solution)/shard_map/ppermute | solution.py:207
  26.0 0.0 collective-permute-done.5.refs_4_
  26.0 0.0 copy-start.2
  26.0 0.7 copy-done.2
  26.7 0.0 collective-permute-done.4
  26.7 0.0 collective-permute-done.3.refs_1_
  26.7 1.3 %collective-permute-start.8 = (bf16[160,1280]{1,0:T(8,128)(2,1)S(1)}, bf16[160,1280]{1,0:T(8,128)(2,1)S(1)}, u32[]{:S(2)}, u32[]{:S(2)}) collective-permute-start(bf16[160,1280]{1,0:T(8,128)(2,1)S(1)} %collective-permute-done.4), channel_id=1, source_target_pairs={{8,0},{12,4},{16,24},{20,28},{9,1},{13,5},{17,25},{21,29},{10,2},{... | collective-permute-start | bytes 1228808 | tf_op jit(solution)/shard_map/ppermute | solution.py:229
  28.0 1.5 %collective-permute-start.10 = (bf16[320,640]{1,0:T(8,128)(2,1)S(1)}, bf16[320,640]{1,0:T(8,128)(2,1)S(1)}, u32[]{:S(2)}, u32[]{:S(2)}) collective-permute-start(bf16[320,640]{1,0:T(8,128)(2,1)S(1)} %pad_maximum_fusion.1), channel_id=1, source_target_pairs={{0,2},{1,3},{2,0},{3,1},{4,6},{5,7},{6,4},{7,5},{8,10},{9,11},{10,... | collective-permute-start | bytes 1228808 | tf_op jit(solution)/shard_map/ppermute | solution.py:207
  29.6 1.5 %collective-permute-start.9 = (bf16[160,1280]{1,0:T(8,128)(2,1)S(1)}, bf16[160,1280]{1,0:T(8,128)(2,1)S(1)}, u32[]{:S(2)}, u32[]{:S(2)}) collective-permute-start(bf16[160,1280]{1,0:T(8,128)(2,1)S(1)} %collective-permute-done.3.refs_1_), channel_id=1, source_target_pairs={{0,4},{4,0},{8,12},{12,8},{16,20},{20,16},{24,28},{28,24},{1,5},{5... | collective-permute-start | bytes 1228808 | tf_op jit(solution)/shard_map/ppermute | solution.py:207
  31.1 1.4 %collective-permute-start.7 = (bf16[160,1280]{1,0:T(8,128)(2,1)S(1)}, bf16[160,1280]{1,0:T(8,128)(2,1)}, u32[]{:S(2)}, u32[]{:S(2)}) collective-permute-start(bf16[160,1280]{1,0:T(8,128)(2,1)S(1)} %collective-permute-done.3.refs_1_), channel_id=1, source_target_pairs={{8,16},{12,20},{16,8},{20,12},{9,17},{13,21},{17,9},{21,13},{10,18... | collective-permute-start | bytes 1228808 | tf_op jit(solution)/shard_map/ppermute | solution.py:229
  32.5 0.0 copy-done.9
  32.5 0.2 convert_reduce_fusion.low_ref
  32.7 4.5 %collective-permute-done.8 = bf16[160,1280]{1,0:T(8,128)(2,1)S(1)} collective-permute-done((bf16[160,1280]{1,0:T(8,128)(2,1)S(1)}, bf16[160,1280]{1,0:T(8,128)(2,1)S(1)}, u32[]{:S(2)}, u32[]{:S(2)}) %collective-permute-start.8) | collective-permute-done | bytes 409632 | tf_op jit(solution)/shard_map/ppermute | solution.py:229
  37.2 0.0 collective-permute-done.10
  37.2 1.9 %collective-permute-done.9.refs_5_ = bf16[160,1280]{1,0:T(8,128)(2,1)S(1)} collective-permute-done((bf16[160,1280]{1,0:T(8,128)(2,1)S(1)}, bf16[160,1280]{1,0:T(8,128)(2,1)S(1)}, u32[]{:S(2)}, u32[]{:S(2)}) %collective-permute-start.9) | collective-permute-done | bytes 409632 | tf_op jit(solution)/shard_map/ppermute | solution.py:207
  39.1 0.0 collective-permute-done.7
  39.1 1.6 %collective-permute-start.13 = (bf16[160,1280]{1,0:T(8,128)(2,1)S(1)}, bf16[160,1280]{1,0:T(8,128)(2,1)}, u32[]{:S(2)}, u32[]{:S(2)}) collective-permute-start(bf16[160,1280]{1,0:T(8,128)(2,1)S(1)} %broadcast_select_fusion.1.refs_2_), channel_id=1, source_target_pairs={{0,4},{4,0},{8,12},{12,8},{16,20},{20,16},{24,28},{28,24},{1,5},{5... | collective-permute-start | bytes 1228808 | tf_op jit(solution)/shard_map/ppermute | solution.py:207
  40.7 1.3 %collective-permute-start.12 = (bf16[160,1280]{1,0:T(8,128)(2,1)}, bf16[160,1280]{1,0:T(8,128)(2,1)}, u32[]{:S(2)}, u32[]{:S(2)}) collective-permute-start(bf16[160,1280]{1,0:T(8,128)(2,1)} %collective-permute-done.7), channel_id=1, source_target_pairs={{8,0},{12,4},{16,24},{20,28},{9,1},{13,5},{17,25},{21,29},{10,2},{... | collective-permute-start | bytes 1228808 | tf_op jit(solution)/shard_map/ppermute | solution.py:229
  42.0 0.1 broadcast_select_fusion.3
  42.1 0.0 copy-done.4
  42.1 0.0 copy-done.6
  42.1 0.0 copy-start
  42.1 0.0 copy-start.1
  42.1 0.0 copy-start.8
  42.2 0.1 pad_maximum_fusion
  42.2 0.1 collective-permute-start.11
  42.3 0.1 broadcast_in_dim.2
  42.4 0.1 reshape_reshape.3.refs_8_
  42.5 0.1 stack.47.source_ref
  42.6 0.1 pad_add_fusion.where_ref
  42.7 4.6 %collective-permute-done.13.refs_6_ = bf16[160,1280]{1,0:T(8,128)(2,1)} collective-permute-done((bf16[160,1280]{1,0:T(8,128)(2,1)S(1)}, bf16[160,1280]{1,0:T(8,128)(2,1)}, u32[]{:S(2)}, u32[]{:S(2)}) %collective-permute-start.13) | collective-permute-done | bytes 409632 | tf_op jit(solution)/shard_map/ppermute | solution.py:207
  47.3 4.6 %collective-permute-done.12 = bf16[160,1280]{1,0:T(8,128)(2,1)} collective-permute-done((bf16[160,1280]{1,0:T(8,128)(2,1)}, bf16[160,1280]{1,0:T(8,128)(2,1)}, u32[]{:S(2)}, u32[]{:S(2)}) %collective-permute-start.12) | collective-permute-done | bytes 409632 | tf_op jit(solution)/shard_map/ppermute | solution.py:229
  51.8 1.0 %broadcast_select_fusion.refs_3_ = bf16[160,1280]{1,0:T(8,128)(2,1)S(1)} fusion(bf16[160,1280]{1,0:T(8,128)(2,1)} %collective-permute-done.7, bf16[160,1280]{1,0:T(8,128)(2,1)} %collective-permute-done.12, pred[]{:T(512)S(6)} %or.3), kind=kLoop, calls=%fused_computation.4 | loop fusion | flops 204800 | bytes 1228801 | tf_op jit(solution)/shard_map/jit(_where)/select_n | solution.py:261
  52.9 0.0 copy-start.3
  52.9 0.0 copy-start.5
  52.9 0.0 copy-start.7
  52.9 1.6 %collective-permute-start.14 = (bf16[160,1280]{1,0:T(8,128)(2,1)S(1)}, bf16[160,1280]{1,0:T(8,128)(2,1)S(1)}, u32[]{:S(2)}, u32[]{:S(2)}) collective-permute-start(bf16[160,1280]{1,0:T(8,128)(2,1)S(1)} %broadcast_select_fusion.refs_3_), channel_id=1, source_target_pairs={{0,4},{4,0},{8,12},{12,8},{16,20},{20,16},{24,28},{28,24},{1,5},{5... | collective-permute-start | bytes 1228808 | tf_op jit(solution)/shard_map/ppermute | solution.py:207
  54.5 0.0 collective-permute-done.11.other_ref
  54.5 0.0 copy-done
  54.5 7.3 %project.1 = (bf16[4,1280,192]{2,1,0:T(8,128)(2,1)S(1)}, bf16[1280,512]{1,0:T(8,128)(2,1)S(1)}, bf16[512,1280]{1,0:T(8,128)(2,1)S(1)}, bf16[160,768]{1,0:T(8,128)(2,1)}) custom-call(s32[16]{0:T(128)S(1)} %copy-done.8, s32[16]{0:T(128)S(1)} %convert_reduce_fusion.low_ref, s32[2]{0:T(128)S(1)} %pad_add_fusion.where_ref, bf16[640,640]{1,0:T(8,128)(2,1)S(1)} %bitcast.18, ...), custom_call_target="tpu_custom_call" | custom-call | flops 21474836480 | bytes 16777216 | tf_op jit(solution)/shard_map/project/pallas_call | solution.py:316
  61.8 0.0 collective-permute-done.14.refs_7_
  61.8 14.1 %keys.1 = (bf16[1280,512]{1,0:T(8,128)(2,1)S(1)}, bf16[1280,512]{1,0:T(8,128)(2,1)S(1)}, bf16[160,576]{1,0:T(8,128)(2,1)S(1)}) custom-call(s32[16]{0:T(128)S(1)} %convert_reduce_fusion.low_ref, s32[16]{0:T(128)S(1)} %copy-done.8, s32[8]{0:T(128)S(1)} %stack.47.source_ref, bf16[160,1280]{1,0:T(8,128)(2,1)S(1)} %constant_dynamic-update-slice_fusion.refs_0_, ...), custom_call_target="tpu_custom_call" | custom-call | flops 21474836480 | bytes 16777216 | tf_op jit(solution)/shard_map/keys/pallas_call | solution.py:346
  75.9 0.1 collective-permute-start.15
  76.0 1.4 %collective-permute-done.15 = bf16[160,576]{1,0:T(8,128)(2,1)S(1)} collective-permute-done((bf16[160,576]{1,0:T(8,128)(2,1)S(1)}, bf16[160,576]{1,0:T(8,128)(2,1)S(1)}, u32[]{:S(2)}, u32[]{:S(2)}) %collective-permute-start.15) | collective-permute-done | bytes 184352 | tf_op jit(solution)/shard_map/ppermute | solution.py:207
  77.4 0.1 convert_add_fusion.1
  77.5 0.6 collective-permute-start.16
  78.1 1.8 %fusion = f32[512,512]{1,0:T(8,128)} fusion(bf16[512,1280]{1,0:T(8,128)(2,1)S(1)} %get-tuple-element.47, bf16[1280,512]{1,0:T(8,128)(2,1)S(1)} %get-tuple-element.48), kind=kOutput, calls=%fused_computation.15 | convolution fusion | flops 671088640 | bytes 3670016 | tf_op jit(solution)/shard_map/dot_general | solution.py:30
  79.9 1.8 %fusion.1 = f32[512,512]{1,0:T(8,128)} fusion(bf16[512,1280]{1,0:T(8,128)(2,1)S(1)} %get-tuple-element.47, bf16[1280,512]{1,0:T(8,128)(2,1)S(1)} %get-tuple-element.49), kind=kOutput, calls=%fused_computation.16 | convolution fusion | flops 671088640 | bytes 3670016 | tf_op jit(solution)/shard_map/dot_general | solution.py:30
  81.7 2.9 %collective-permute-done.16 = bf16[160,576]{1,0:T(8,128)(2,1)S(1)} collective-permute-done((bf16[160,576]{1,0:T(8,128)(2,1)S(1)}, bf16[160,576]{1,0:T(8,128)(2,1)S(1)}, u32[]{:S(2)}, u32[]{:S(2)}) %collective-permute-start.16) | collective-permute-done | bytes 184352 | tf_op jit(solution)/shard_map/ppermute | solution.py:207
  84.7 0.8 convert_add_fusion
  (11 shorter events, 0.1 us)
Async XLA Ops:
  0.6 31.9 %copy-start.9 = (s32[16]{0:T(128)S(1)}, s32[16]{0:T(128)}, u32[]{:S(2)}) copy-start(s32[16]{0:T(128)} %param.13) | copy-start | bytes 196
  1.5 7.7 %collective-permute-start.2 = (bf16[40,640]{1,0:T(8,128)(2,1)S(1)}, bf16[40,640]{1,0:T(8,128)(2,1)S(1)}, u32[]{:S(2)}, u32[]{:S(2)}) collective-permute-start(bf16[40,640]{1,0:T(8,128)(2,1)S(1)} %pad_dynamic-slice_fusion), channel_id=1, source_target_pairs={{0,24},{4,28},{8,16},{12,20},{16,8},{20,12},{24,0},{28,4},{1,25},{... | collective-permute-start | bytes 153608 | tf_op jit(solution)/shard_map/ppermute | solution.py:207
  6.7 4.1 %collective-permute-start.1 = (bf16[40,640]{1,0:T(8,128)(2,1)S(1)}, bf16[40,640]{1,0:T(8,128)(2,1)S(1)}, u32[]{:S(2)}, u32[]{:S(2)}) collective-permute-start(bf16[40,640]{1,0:T(8,128)(2,1)S(1)} %pad_dynamic-slice_fusion), channel_id=1, source_target_pairs={{0,8},{4,12},{8,0},{12,4},{16,24},{20,28},{24,16},{28,20},{1,9},{5... | collective-permute-start | bytes 153608 | tf_op jit(solution)/shard_map/ppermute | solution.py:207
  6.7 5.3 %collective-permute-start = (bf16[40,640]{1,0:T(8,128)(2,1)S(1)}, bf16[40,640]{1,0:T(8,128)(2,1)S(1)}, u32[]{:S(2)}, u32[]{:S(2)}) collective-permute-start(bf16[40,640]{1,0:T(8,128)(2,1)S(1)} %pad_dynamic-slice_fusion), channel_id=1, source_target_pairs={{0,16},{4,20},{8,24},{12,28},{16,0},{20,4},{24,8},{28,12},{1,17},{... | collective-permute-start | bytes 153608 | tf_op jit(solution)/shard_map/ppermute | solution.py:207
  12.0 14.0 %collective-permute-start.5 = (bf16[160,1280]{1,0:T(8,128)(2,1)S(1)}, bf16[160,1280]{1,0:T(8,128)(2,1)S(1)}, u32[]{:S(2)}, u32[]{:S(2)}) collective-permute-start(bf16[160,1280]{1,0:T(8,128)(2,1)S(1)} %constant_dynamic-update-slice_fusion.refs_0_), channel_id=1, source_target_pairs={{0,4},{4,0},{8,12},{12,8},{16,20},{20,16},{24,28},{28,24},{1,5},{5... | collective-permute-start | bytes 1228808 | tf_op jit(solution)/shard_map/ppermute | solution.py:207
  13.6 13.1 %collective-permute-start.4 = (bf16[160,1280]{1,0:T(8,128)(2,1)S(1)}, bf16[160,1280]{1,0:T(8,128)(2,1)S(1)}, u32[]{:S(2)}, u32[]{:S(2)}) collective-permute-start(bf16[160,1280]{1,0:T(8,128)(2,1)S(1)} %constant_dynamic-update-slice_fusion.refs_0_), channel_id=1, source_target_pairs={{8,16},{12,20},{16,8},{20,12},{9,17},{13,21},{17,9},{21,13},{10,18... | collective-permute-start | bytes 1228808 | tf_op jit(solution)/shard_map/ppermute | solution.py:229
  14.3 12.5 %collective-permute-start.3 = (bf16[160,1280]{1,0:T(8,128)(2,1)S(1)}, bf16[160,1280]{1,0:T(8,128)(2,1)S(1)}, u32[]{:S(2)}, u32[]{:S(2)}) collective-permute-start(bf16[160,1280]{1,0:T(8,128)(2,1)S(1)} %constant_dynamic-update-slice_fusion.refs_0_), channel_id=1, source_target_pairs={{0,8},{4,12},{8,0},{12,4},{16,24},{20,28},{24,16},{28,20},{1,9},{5... | collective-permute-start | bytes 1228808 | tf_op jit(solution)/shard_map/ppermute | solution.py:207
  17.5 8.5 %collective-permute-start.6 = (bf16[160,640]{1,0:T(8,128)(2,1)S(1)}, bf16[160,640]{1,0:T(8,128)(2,1)S(1)}, u32[]{:S(2)}, u32[]{:S(2)}) collective-permute-start(bf16[160,640]{1,0:T(8,128)(2,1)S(1)} %pad_maximum_fusion.2), channel_id=1, source_target_pairs={{0,4},{4,0},{8,12},{12,8},{16,20},{20,16},{24,28},{28,24},{1,5},{5... | collective-permute-start | bytes 614408 | tf_op jit(solution)/shard_map/ppermute | solution.py:207
  26.0 0.8 copy-start.2
  26.7 15.4 %copy-start.4 = (bf16[160,1280]{1,0:T(8,128)(2,1)}, bf16[160,1280]{1,0:T(8,128)(2,1)S(1)}, u32[]{:S(2)}) copy-start(bf16[160,1280]{1,0:T(8,128)(2,1)S(1)} %collective-permute-done.3.refs_1_) | copy-start | bytes 1228804
  26.7 10.4 %collective-permute-start.8 = (bf16[160,1280]{1,0:T(8,128)(2,1)S(1)}, bf16[160,1280]{1,0:T(8,128)(2,1)S(1)}, u32[]{:S(2)}, u32[]{:S(2)}) collective-permute-start(bf16[160,1280]{1,0:T(8,128)(2,1)S(1)} %collective-permute-done.4), channel_id=1, source_target_pairs={{8,0},{12,4},{16,24},{20,28},{9,1},{13,5},{17,25},{21,29},{10,2},{... | collective-permute-start | bytes 1228808 | tf_op jit(solution)/shard_map/ppermute | solution.py:229
  28.0 9.1 %collective-permute-start.10 = (bf16[320,640]{1,0:T(8,128)(2,1)S(1)}, bf16[320,640]{1,0:T(8,128)(2,1)S(1)}, u32[]{:S(2)}, u32[]{:S(2)}) collective-permute-start(bf16[320,640]{1,0:T(8,128)(2,1)S(1)} %pad_maximum_fusion.1), channel_id=1, source_target_pairs={{0,2},{1,3},{2,0},{3,1},{4,6},{5,7},{6,4},{7,5},{8,10},{9,11},{10,... | collective-permute-start | bytes 1228808 | tf_op jit(solution)/shard_map/ppermute | solution.py:207
  29.6 9.5 %collective-permute-start.9 = (bf16[160,1280]{1,0:T(8,128)(2,1)S(1)}, bf16[160,1280]{1,0:T(8,128)(2,1)S(1)}, u32[]{:S(2)}, u32[]{:S(2)}) collective-permute-start(bf16[160,1280]{1,0:T(8,128)(2,1)S(1)} %collective-permute-done.3.refs_1_), channel_id=1, source_target_pairs={{0,4},{4,0},{8,12},{12,8},{16,20},{20,16},{24,28},{28,24},{1,5},{5... | collective-permute-start | bytes 1228808 | tf_op jit(solution)/shard_map/ppermute | solution.py:207
  31.1 8.0 %collective-permute-start.7 = (bf16[160,1280]{1,0:T(8,128)(2,1)S(1)}, bf16[160,1280]{1,0:T(8,128)(2,1)}, u32[]{:S(2)}, u32[]{:S(2)}) collective-permute-start(bf16[160,1280]{1,0:T(8,128)(2,1)S(1)} %collective-permute-done.3.refs_1_), channel_id=1, source_target_pairs={{8,16},{12,20},{16,8},{20,12},{9,17},{13,21},{17,9},{21,13},{10,18... | collective-permute-start | bytes 1228808 | tf_op jit(solution)/shard_map/ppermute | solution.py:229
  39.1 3.0 %copy-start.6 = (bf16[160,1280]{1,0:T(8,128)(2,1)}, bf16[160,1280]{1,0:T(8,128)(2,1)S(1)}, u32[]{:S(2)}) copy-start(bf16[160,1280]{1,0:T(8,128)(2,1)S(1)} %collective-permute-done.9.refs_5_) | copy-start | bytes 1228804
  39.1 8.1 %collective-permute-start.13 = (bf16[160,1280]{1,0:T(8,128)(2,1)S(1)}, bf16[160,1280]{1,0:T(8,128)(2,1)}, u32[]{:S(2)}, u32[]{:S(2)}) collective-permute-start(bf16[160,1280]{1,0:T(8,128)(2,1)S(1)} %broadcast_select_fusion.1.refs_2_), channel_id=1, source_target_pairs={{0,4},{4,0},{8,12},{12,8},{16,20},{20,16},{24,28},{28,24},{1,5},{5... | collective-permute-start | bytes 1228808 | tf_op jit(solution)/shard_map/ppermute | solution.py:207
  40.7 11.1 %collective-permute-start.12 = (bf16[160,1280]{1,0:T(8,128)(2,1)}, bf16[160,1280]{1,0:T(8,128)(2,1)}, u32[]{:S(2)}, u32[]{:S(2)}) collective-permute-start(bf16[160,1280]{1,0:T(8,128)(2,1)} %collective-permute-done.7), channel_id=1, source_target_pairs={{8,0},{12,4},{16,24},{20,28},{9,1},{13,5},{17,25},{21,29},{10,2},{... | collective-permute-start | bytes 1228808 | tf_op jit(solution)/shard_map/ppermute | solution.py:229
  42.1 12.4 %copy-start = (bf16[512,512]{1,0:T(8,128)(2,1)S(1)}, bf16[512,512]{1,0:T(8,128)(2,1)}, u32[]{:S(2)}) copy-start(bf16[512,512]{1,0:T(8,128)(2,1)} %refs_11_.1) | copy-start | bytes 1572868
  42.1 12.4 %copy-start.1 = (bf16[512,512]{1,0:T(8,128)(2,1)S(1)}, bf16[512,512]{1,0:T(8,128)(2,1)}, u32[]{:S(2)}) copy-start(bf16[512,512]{1,0:T(8,128)(2,1)} %refs_12_.1) | copy-start | bytes 1572868
  42.1 12.4 %copy-start.8 = (s32[16]{0:T(128)S(1)}, s32[16]{0:T(128)}, u32[]{:S(2)}) copy-start(s32[16]{0:T(128)} %order_ref.3) | copy-start | bytes 196
  42.2 12.3 %collective-permute-start.11 = (bf16[640,640]{1,0:T(8,128)(2,1)S(1)}, bf16[640,640]{1,0:T(8,128)(2,1)S(1)}, u32[]{:S(2)}, u32[]{:S(2)}) collective-permute-start(bf16[640,640]{1,0:T(8,128)(2,1)S(1)} %bitcast.17), channel_id=1, source_target_pairs={{0,1},{1,0},{2,3},{3,2},{4,5},{5,4},{6,7},{7,6},{8,9},{9,8},{10,11... | collective-permute-start | bytes 2457608 | tf_op jit(solution)/shard_map/ppermute | solution.py:207
  52.9 8.9 %copy-start.3 = (bf16[160,1280]{1,0:T(8,128)(2,1)S(1)}, bf16[160,1280]{1,0:T(8,128)(2,1)}, u32[]{:S(2)}) copy-start(bf16[160,1280]{1,0:T(8,128)(2,1)} %copy-done.2) | copy-start | bytes 1228804
  52.9 8.9 %copy-start.5 = (bf16[160,1280]{1,0:T(8,128)(2,1)S(1)}, bf16[160,1280]{1,0:T(8,128)(2,1)}, u32[]{:S(2)}) copy-start(bf16[160,1280]{1,0:T(8,128)(2,1)} %copy-done.4) | copy-start | bytes 1228804
  52.9 8.9 %copy-start.7 = (bf16[160,1280]{1,0:T(8,128)(2,1)S(1)}, bf16[160,1280]{1,0:T(8,128)(2,1)}, u32[]{:S(2)}) copy-start(bf16[160,1280]{1,0:T(8,128)(2,1)} %copy-done.6) | copy-start | bytes 1228804
  52.9 8.9 %collective-permute-start.14 = (bf16[160,1280]{1,0:T(8,128)(2,1)S(1)}, bf16[160,1280]{1,0:T(8,128)(2,1)S(1)}, u32[]{:S(2)}, u32[]{:S(2)}) collective-permute-start(bf16[160,1280]{1,0:T(8,128)(2,1)S(1)} %broadcast_select_fusion.refs_3_), channel_id=1, source_target_pairs={{0,4},{4,0},{8,12},{12,8},{16,20},{20,16},{24,28},{28,24},{1,5},{5... | collective-permute-start | bytes 1228808 | tf_op jit(solution)/shard_map/ppermute | solution.py:207
  75.9 1.5 %collective-permute-start.15 = (bf16[160,576]{1,0:T(8,128)(2,1)S(1)}, bf16[160,576]{1,0:T(8,128)(2,1)S(1)}, u32[]{:S(2)}, u32[]{:S(2)}) collective-permute-start(bf16[160,576]{1,0:T(8,128)(2,1)S(1)} %get-tuple-element.43), channel_id=1, source_target_pairs={{0,1},{1,0},{2,3},{3,2},{4,5},{5,4},{6,7},{7,6},{8,9},{9,8},{10,11... | collective-permute-start | bytes 552968 | tf_op jit(solution)/shard_map/ppermute | solution.py:207
  77.5 7.2 %collective-permute-start.16 = (bf16[160,576]{1,0:T(8,128)(2,1)S(1)}, bf16[160,576]{1,0:T(8,128)(2,1)S(1)}, u32[]{:S(2)}, u32[]{:S(2)}) collective-permute-start(bf16[160,576]{1,0:T(8,128)(2,1)S(1)} %convert_add_fusion.1), channel_id=1, source_target_pairs={{0,2},{1,3},{2,0},{3,1},{4,6},{5,7},{6,4},{7,5},{8,10},{9,11},{10,... | collective-permute-start | bytes 552968 | tf_op jit(solution)/shard_map/ppermute | solution.py:207

commit v5 on v4

--- a/solution.py
+++ b/solution.py
@@ -159,11 +159,9 @@
             return key_grad[:, NOPE:]
 
         rope = 0.0
-        begun_heads = [begin(0)]
+        opened = [begin(head) for head in range(here)]
         for head in range(here):
-            if head + 1 < here:
-                begun_heads.append(begin(head + 1))
-            rope = rope + end(*middle(*begun_heads[head]))
+            rope = rope + end(*middle(*opened[head]))
         sum_rope[window, :] += rope
 
     def step(number, carry):
@@ -237,9 +235,9 @@
     inner = (place == 1) | (place == 2)
     piece = mine.shape[0]
     mine = jnp.concatenate([mine] + [swap(mine, "seq", mask) for mask in (4, 2, 6)], axis=0)
-    own, mine = hold((own, mine))
-    near = swap(own, "seq", 2)
-    third = along(own, middle)
+    held_own, mine = hold((own, mine))
+    near = swap(held_own, "seq", 2)
+    third = along(held_own, middle)
     y_own = swap(own, "seq", 1)
     mine = join(mine, "seq", 1)
     near, third, y_own, mine = hold((near, third, y_own, mine))

time: 85.4 us -> 84.4 us (0.988)
  waiting for transfers between devices: 30.7 us -> 29.3 us
  starting transfers between devices: 22.6 us -> 23.9 us
    ppermute x13, waiting for transfers between devices: 21.7 us -> 18.1 us  [swap(): return lax.ppermute(array, axis, [(i, i ^ mask) for i in range(size)])]
    ppermute x4, waiting for transfers between devices: 9.05 us -> 11.2 us  [along(): lax.ppermute(array, 'seq', [(2 * a + y, 2 * b + y) for a, b in pairs for...]
    ppermute x13, starting transfers between devices: 18 us -> 19.2 us  [swap(): return lax.ppermute(array, axis, [(i, i ^ mask) for i in range(size)])]
  transfers between devices with their start and end apart: 17 -> 17, of which waited for: 9 -> 8; matrix products, arithmetic and copies ran while one was open for 8% -> 9% of each run, Pallas kernels for 8% -> 9%
where the time goes in v5:
time: 84.4 us; the launch traced here: 84.8 us
  waiting for transfers between devices  29.3 us (35%)
  starting transfers between devices  23.9 us (28%)
  Pallas kernels  20.8 us (25%)
  local copies, waits for them, and re-layouts  3.79 us (4%)
  matrix products  3.62 us (4%)
  other arithmetic  2.42 us (3%)
  between operations  0.93 us (1%)
    ppermute x13, starting transfers between devices, swap(): return lax.ppermute(array, axis, [(i, i ^ mask) for i in range(size)])  19.2 us
    ppermute x13, waiting for transfers between devices, swap(): return lax.ppermute(array, axis, [(i, i ^ mask) for i in range(size)])  18.1 us
    pallas_call x1, Pallas kernels, shards(): pl.pallas_call(functools.partial(key_kernel, devices, half, pair, len(sha...  13.5 us
    ppermute x4, waiting for transfers between devices, along(): lax.ppermute(array, 'seq', [(2 * a + y, 2 * b + y) for a, b in pairs for...  11.2 us
    pallas_call x1, Pallas kernels, shards(): pl.pallas_call(functools.partial(project_kernel, devices, half, heads, pa...  7.3 us
    ppermute x4, starting transfers between devices, along(): lax.ppermute(array, 'seq', [(2 * a + y, 2 * b + y) for a, b in pairs for...  4.67 us
    dot_general x2, matrix products, dot(): return lax.dot_general(a, b, dims, preferred_element_type=jnp.float32)  3.62 us
    unnamed x21, local copies, waits for them, and re-layouts  1.76 us
  transfers between devices with their start and end apart: 17, of which 8 were waited for; matrix products, arithmetic and copies ran while one was open for 9% of the time, Pallas kernels for 9%

profile of v5, /device:TPU:0, one launch (start us, length us, event | category | flops | bytes accessed | tf_op | source)
XLA Modules:
  0.0 84.8 jit_solution(3682173204432195183)
XLA Ops:
  0.6 0.0 copy-start.9
  0.7 0.9 %pad_dynamic-slice_fusion = bf16[40,640]{1,0:T(8,128)(2,1)S(1)} fusion(s32[]{:T(128)S(6)} %dynamic_slice.7, bf16[160,576]{1,0:T(8,128)(2,1)} %param.8), kind=kLoop, calls=%fused_computation.9 | loop fusion | bytes 235524 | tf_op jit(solution)/shard_map/dynamic_slice | solution.py:296
  1.5 5.1 %collective-permute-start.2 = (bf16[40,640]{1,0:T(8,128)(2,1)S(1)}, bf16[40,640]{1,0:T(8,128)(2,1)S(1)}, u32[]{:S(2)}, u32[]{:S(2)}) collective-permute-start(bf16[40,640]{1,0:T(8,128)(2,1)S(1)} %pad_dynamic-slice_fusion), channel_id=1, source_target_pairs={{0,24},{4,28},{8,16},{12,20},{16,8},{20,12},{24,0},{28,4},{1,25},{... | collective-permute-start | bytes 153608 | tf_op jit(solution)/shard_map/ppermute | solution.py:205
  6.7 0.0 collective-permute-start.1
  6.7 0.6 collective-permute-start
  7.3 1.0 %constant_dynamic-update-slice_fusion.1 = bf16[160,1280]{1,0:T(8,128)(2,1)S(1)} fusion(bf16[160,768]{1,0:T(8,128)(2,1)} %param.7), kind=kLoop, calls=%fused_computation.12 | loop fusion | bytes 491520
  8.3 0.9 %constant_dynamic-update-slice_fusion.refs_0_ = bf16[160,1280]{1,0:T(8,128)(2,1)S(1)} fusion(bf16[160,1280]{1,0:T(8,128)(2,1)S(1)} %constant_dynamic-update-slice_fusion.1, bf16[160,512]{1,0:T(8,128)(2,1)} %param.11), kind=kLoop, calls=%fused_computation.11 | loop fusion | bytes 327680 | tf_op jit(solution)/shard_map/concatenate | solution.py:281
  9.2 1.7 %collective-permute-start.5 = (bf16[160,1280]{1,0:T(8,128)(2,1)S(1)}, bf16[160,1280]{1,0:T(8,128)(2,1)S(1)}, u32[]{:S(2)}, u32[]{:S(2)}) collective-permute-start(bf16[160,1280]{1,0:T(8,128)(2,1)S(1)} %constant_dynamic-update-slice_fusion.refs_0_), channel_id=1, source_target_pairs={{0,4},{4,0},{8,12},{12,8},{16,20},{20,16},{24,28},{28,24},{1,5},{5... | collective-permute-start | bytes 1228808 | tf_op jit(solution)/shard_map/ppermute | solution.py:205
  10.9 0.0 collective-permute-done.2
  10.9 0.0 collective-permute-done.1
  10.9 1.1 %collective-permute-done = bf16[40,640]{1,0:T(8,128)(2,1)S(1)} collective-permute-done((bf16[40,640]{1,0:T(8,128)(2,1)S(1)}, bf16[40,640]{1,0:T(8,128)(2,1)S(1)}, u32[]{:S(2)}, u32[]{:S(2)}) %collective-permute-start) | collective-permute-done | bytes 51232 | tf_op jit(solution)/shard_map/ppermute | solution.py:205
  12.0 0.7 collective-permute-start.4
  12.7 3.1 %collective-permute-start.3 = (bf16[160,1280]{1,0:T(8,128)(2,1)S(1)}, bf16[160,1280]{1,0:T(8,128)(2,1)S(1)}, u32[]{:S(2)}, u32[]{:S(2)}) collective-permute-start(bf16[160,1280]{1,0:T(8,128)(2,1)S(1)} %constant_dynamic-update-slice_fusion.refs_0_), channel_id=1, source_target_pairs={{0,8},{4,12},{8,0},{12,4},{16,24},{20,28},{24,16},{28,20},{1,9},{5... | collective-permute-start | bytes 1228808 | tf_op jit(solution)/shard_map/ppermute | solution.py:205
  15.8 1.6 %collective-permute-start.6 = (bf16[160,640]{1,0:T(8,128)(2,1)S(1)}, bf16[160,640]{1,0:T(8,128)(2,1)S(1)}, u32[]{:S(2)}, u32[]{:S(2)}) collective-permute-start(bf16[160,640]{1,0:T(8,128)(2,1)S(1)} %pad_maximum_fusion.2), channel_id=1, source_target_pairs={{0,4},{4,0},{8,12},{12,8},{16,20},{20,16},{24,28},{28,24},{1,5},{5... | collective-permute-start | bytes 614408 | tf_op jit(solution)/shard_map/ppermute | solution.py:205
  17.4 6.9 %collective-permute-done.6 = bf16[160,640]{1,0:T(8,128)(2,1)S(1)} collective-permute-done((bf16[160,640]{1,0:T(8,128)(2,1)S(1)}, bf16[160,640]{1,0:T(8,128)(2,1)S(1)}, u32[]{:S(2)}, u32[]{:S(2)}) %collective-permute-start.6) | collective-permute-done | bytes 204832 | tf_op jit(solution)/shard_map/ppermute | solution.py:205
  24.3 0.0 collective-permute-done.5.refs_4_
  24.3 0.0 copy-start.2
  24.4 0.7 copy-done.2
  25.1 0.0 collective-permute-done.4
  25.1 0.0 collective-permute-done.3.refs_1_
  25.1 1.3 %collective-permute-start.8 = (bf16[160,1280]{1,0:T(8,128)(2,1)S(1)}, bf16[160,1280]{1,0:T(8,128)(2,1)S(1)}, u32[]{:S(2)}, u32[]{:S(2)}) collective-permute-start(bf16[160,1280]{1,0:T(8,128)(2,1)S(1)} %collective-permute-done.4), channel_id=1, source_target_pairs={{8,0},{12,4},{16,24},{20,28},{9,1},{13,5},{17,25},{21,29},{10,2},{... | collective-permute-start | bytes 1228808 | tf_op jit(solution)/shard_map/ppermute | solution.py:227
  26.4 1.5 %collective-permute-start.10 = (bf16[320,640]{1,0:T(8,128)(2,1)S(1)}, bf16[320,640]{1,0:T(8,128)(2,1)S(1)}, u32[]{:S(2)}, u32[]{:S(2)}) collective-permute-start(bf16[320,640]{1,0:T(8,128)(2,1)S(1)} %pad_maximum_fusion.1), channel_id=1, source_target_pairs={{0,2},{1,3},{2,0},{3,1},{4,6},{5,7},{6,4},{7,5},{8,10},{9,11},{10,... | collective-permute-start | bytes 1228808 | tf_op jit(solution)/shard_map/ppermute | solution.py:205
  27.9 1.5 %collective-permute-start.9 = (bf16[160,1280]{1,0:T(8,128)(2,1)S(1)}, bf16[160,1280]{1,0:T(8,128)(2,1)S(1)}, u32[]{:S(2)}, u32[]{:S(2)}) collective-permute-start(bf16[160,1280]{1,0:T(8,128)(2,1)S(1)} %collective-permute-done.3.refs_1_), channel_id=1, source_target_pairs={{0,4},{4,0},{8,12},{12,8},{16,20},{20,16},{24,28},{28,24},{1,5},{5... | collective-permute-start | bytes 1228808 | tf_op jit(solution)/shard_map/ppermute | solution.py:205
  29.5 1.4 %collective-permute-start.7 = (bf16[160,1280]{1,0:T(8,128)(2,1)S(1)}, bf16[160,1280]{1,0:T(8,128)(2,1)}, u32[]{:S(2)}, u32[]{:S(2)}) collective-permute-start(bf16[160,1280]{1,0:T(8,128)(2,1)S(1)} %collective-permute-done.3.refs_1_), channel_id=1, source_target_pairs={{8,16},{12,20},{16,8},{20,12},{9,17},{13,21},{17,9},{21,13},{10,18... | collective-permute-start | bytes 1228808 | tf_op jit(solution)/shard_map/ppermute | solution.py:227
  30.9 0.0 copy-done.9
  30.9 0.2 convert_reduce_fusion.low_ref
  31.1 5.7 %collective-permute-done.8 = bf16[160,1280]{1,0:T(8,128)(2,1)S(1)} collective-permute-done((bf16[160,1280]{1,0:T(8,128)(2,1)S(1)}, bf16[160,1280]{1,0:T(8,128)(2,1)S(1)}, u32[]{:S(2)}, u32[]{:S(2)}) %collective-permute-start.8) | collective-permute-done | bytes 409632 | tf_op jit(solution)/shard_map/ppermute | solution.py:227
  36.7 0.0 collective-permute-done.10
  36.7 0.7 collective-permute-done.9.refs_5_
  37.5 0.0 collective-permute-done.7
  37.5 1.6 %collective-permute-start.13 = (bf16[160,1280]{1,0:T(8,128)(2,1)S(1)}, bf16[160,1280]{1,0:T(8,128)(2,1)}, u32[]{:S(2)}, u32[]{:S(2)}) collective-permute-start(bf16[160,1280]{1,0:T(8,128)(2,1)S(1)} %broadcast_select_fusion.1.refs_2_), channel_id=1, source_target_pairs={{0,4},{4,0},{8,12},{12,8},{16,20},{20,16},{24,28},{28,24},{1,5},{5... | collective-permute-start | bytes 1228808 | tf_op jit(solution)/shard_map/ppermute | solution.py:205
  39.1 1.3 %collective-permute-start.12 = (bf16[160,1280]{1,0:T(8,128)(2,1)}, bf16[160,1280]{1,0:T(8,128)(2,1)}, u32[]{:S(2)}, u32[]{:S(2)}) collective-permute-start(bf16[160,1280]{1,0:T(8,128)(2,1)} %collective-permute-done.7), channel_id=1, source_target_pairs={{8,0},{12,4},{16,24},{20,28},{9,1},{13,5},{17,25},{21,29},{10,2},{... | collective-permute-start | bytes 1228808 | tf_op jit(solution)/shard_map/ppermute | solution.py:227
  40.4 0.1 broadcast_select_fusion.3
  40.5 0.0 copy-done.4
  40.5 0.0 copy-done.6
  40.5 0.0 copy-start
  40.5 0.0 copy-start.1
  40.5 0.0 copy-start.8
  40.5 0.1 pad_maximum_fusion
  40.6 0.1 collective-permute-start.11
  40.7 0.1 broadcast_in_dim.2
  40.8 0.1 reshape_reshape.3.refs_8_
  40.9 0.1 stack.47.source_ref
  40.9 0.1 pad_add_fusion.where_ref
  41.0 5.1 %collective-permute-done.13.refs_6_ = bf16[160,1280]{1,0:T(8,128)(2,1)} collective-permute-done((bf16[160,1280]{1,0:T(8,128)(2,1)S(1)}, bf16[160,1280]{1,0:T(8,128)(2,1)}, u32[]{:S(2)}, u32[]{:S(2)}) %collective-permute-start.13) | collective-permute-done | bytes 409632 | tf_op jit(solution)/shard_map/ppermute | solution.py:205
  46.1 5.6 %collective-permute-done.12 = bf16[160,1280]{1,0:T(8,128)(2,1)} collective-permute-done((bf16[160,1280]{1,0:T(8,128)(2,1)}, bf16[160,1280]{1,0:T(8,128)(2,1)}, u32[]{:S(2)}, u32[]{:S(2)}) %collective-permute-start.12) | collective-permute-done | bytes 409632 | tf_op jit(solution)/shard_map/ppermute | solution.py:227
  51.7 1.0 %broadcast_select_fusion.refs_3_ = bf16[160,1280]{1,0:T(8,128)(2,1)S(1)} fusion(bf16[160,1280]{1,0:T(8,128)(2,1)} %collective-permute-done.7, bf16[160,1280]{1,0:T(8,128)(2,1)} %collective-permute-done.12, pred[]{:T(512)S(6)} %or.3), kind=kLoop, calls=%fused_computation.4 | loop fusion | flops 204800 | bytes 1228801 | tf_op jit(solution)/shard_map/jit(_where)/select_n | solution.py:259
  52.7 0.0 copy-start.3
  52.7 0.0 copy-start.5
  52.7 0.0 copy-start.7
  52.7 1.6 %collective-permute-start.14 = (bf16[160,1280]{1,0:T(8,128)(2,1)S(1)}, bf16[160,1280]{1,0:T(8,128)(2,1)S(1)}, u32[]{:S(2)}, u32[]{:S(2)}) collective-permute-start(bf16[160,1280]{1,0:T(8,128)(2,1)S(1)} %broadcast_select_fusion.refs_3_), channel_id=1, source_target_pairs={{0,4},{4,0},{8,12},{12,8},{16,20},{20,16},{24,28},{28,24},{1,5},{5... | collective-permute-start | bytes 1228808 | tf_op jit(solution)/shard_map/ppermute | solution.py:205
  54.3 0.0 collective-permute-done.11.other_ref
  54.3 0.0 copy-done
  54.3 7.3 %project.1 = (bf16[4,1280,192]{2,1,0:T(8,128)(2,1)S(1)}, bf16[1280,512]{1,0:T(8,128)(2,1)S(1)}, bf16[512,1280]{1,0:T(8,128)(2,1)S(1)}, bf16[160,768]{1,0:T(8,128)(2,1)}) custom-call(s32[16]{0:T(128)S(1)} %copy-done.8, s32[16]{0:T(128)S(1)} %convert_reduce_fusion.low_ref, s32[2]{0:T(128)S(1)} %pad_add_fusion.where_ref, bf16[640,640]{1,0:T(8,128)(2,1)S(1)} %bitcast.18, ...), custom_call_target="tpu_custom_call" | custom-call | flops 21474836480 | bytes 16777216 | tf_op jit(solution)/shard_map/project/pallas_call | solution.py:314
  61.7 0.0 collective-permute-done.14.refs_7_
  61.7 13.5 %keys.1 = (bf16[1280,512]{1,0:T(8,128)(2,1)S(1)}, bf16[1280,512]{1,0:T(8,128)(2,1)S(1)}, bf16[160,576]{1,0:T(8,128)(2,1)S(1)}) custom-call(s32[16]{0:T(128)S(1)} %convert_reduce_fusion.low_ref, s32[16]{0:T(128)S(1)} %copy-done.8, s32[8]{0:T(128)S(1)} %stack.47.source_ref, bf16[160,1280]{1,0:T(8,128)(2,1)S(1)} %constant_dynamic-update-slice_fusion.refs_0_, ...), custom_call_target="tpu_custom_call" | custom-call | flops 21474836480 | bytes 16777216 | tf_op jit(solution)/shard_map/keys/pallas_call | solution.py:344
  75.2 0.1 collective-permute-start.15
  75.3 1.4 %collective-permute-done.15 = bf16[160,576]{1,0:T(8,128)(2,1)S(1)} collective-permute-done((bf16[160,576]{1,0:T(8,128)(2,1)S(1)}, bf16[160,576]{1,0:T(8,128)(2,1)S(1)}, u32[]{:S(2)}, u32[]{:S(2)}) %collective-permute-start.15) | collective-permute-done | bytes 184352 | tf_op jit(solution)/shard_map/ppermute | solution.py:205
  76.7 0.1 convert_add_fusion.1
  76.8 0.7 collective-permute-start.16
  77.5 1.8 %fusion = f32[512,512]{1,0:T(8,128)} fusion(bf16[512,1280]{1,0:T(8,128)(2,1)S(1)} %get-tuple-element.47, bf16[1280,512]{1,0:T(8,128)(2,1)S(1)} %get-tuple-element.48), kind=kOutput, calls=%fused_computation.15 | convolution fusion | flops 671088640 | bytes 3670016 | tf_op jit(solution)/shard_map/dot_general | solution.py:30
  79.3 1.8 %fusion.1 = f32[512,512]{1,0:T(8,128)} fusion(bf16[512,1280]{1,0:T(8,128)(2,1)S(1)} %get-tuple-element.47, bf16[1280,512]{1,0:T(8,128)(2,1)S(1)} %get-tuple-element.49), kind=kOutput, calls=%fused_computation.16 | convolution fusion | flops 671088640 | bytes 3670016 | tf_op jit(solution)/shard_map/dot_general | solution.py:30
  81.1 2.9 %collective-permute-done.16 = bf16[160,576]{1,0:T(8,128)(2,1)S(1)} collective-permute-done((bf16[160,576]{1,0:T(8,128)(2,1)S(1)}, bf16[160,576]{1,0:T(8,128)(2,1)S(1)}, u32[]{:S(2)}, u32[]{:S(2)}) %collective-permute-start.16) | collective-permute-done | bytes 184352 | tf_op jit(solution)/shard_map/ppermute | solution.py:205
  84.0 0.8 convert_add_fusion
  (11 shorter events, 0.1 us)
Async XLA Ops:
  0.6 30.2 %copy-start.9 = (s32[16]{0:T(128)S(1)}, s32[16]{0:T(128)}, u32[]{:S(2)}) copy-start(s32[16]{0:T(128)} %param.13) | copy-start | bytes 196
  1.5 9.4 %collective-permute-start.2 = (bf16[40,640]{1,0:T(8,128)(2,1)S(1)}, bf16[40,640]{1,0:T(8,128)(2,1)S(1)}, u32[]{:S(2)}, u32[]{:S(2)}) collective-permute-start(bf16[40,640]{1,0:T(8,128)(2,1)S(1)} %pad_dynamic-slice_fusion), channel_id=1, source_target_pairs={{0,24},{4,28},{8,16},{12,20},{16,8},{20,12},{24,0},{28,4},{1,25},{... | collective-permute-start | bytes 153608 | tf_op jit(solution)/shard_map/ppermute | solution.py:205
  6.7 4.3 %collective-permute-start.1 = (bf16[40,640]{1,0:T(8,128)(2,1)S(1)}, bf16[40,640]{1,0:T(8,128)(2,1)S(1)}, u32[]{:S(2)}, u32[]{:S(2)}) collective-permute-start(bf16[40,640]{1,0:T(8,128)(2,1)S(1)} %pad_dynamic-slice_fusion), channel_id=1, source_target_pairs={{0,8},{4,12},{8,0},{12,4},{16,24},{20,28},{24,16},{28,20},{1,9},{5... | collective-permute-start | bytes 153608 | tf_op jit(solution)/shard_map/ppermute | solution.py:205
  6.7 5.3 %collective-permute-start = (bf16[40,640]{1,0:T(8,128)(2,1)S(1)}, bf16[40,640]{1,0:T(8,128)(2,1)S(1)}, u32[]{:S(2)}, u32[]{:S(2)}) collective-permute-start(bf16[40,640]{1,0:T(8,128)(2,1)S(1)} %pad_dynamic-slice_fusion), channel_id=1, source_target_pairs={{0,16},{4,20},{8,24},{12,28},{16,0},{20,4},{24,8},{28,12},{1,17},{... | collective-permute-start | bytes 153608 | tf_op jit(solution)/shard_map/ppermute | solution.py:205
  9.2 15.1 %collective-permute-start.5 = (bf16[160,1280]{1,0:T(8,128)(2,1)S(1)}, bf16[160,1280]{1,0:T(8,128)(2,1)S(1)}, u32[]{:S(2)}, u32[]{:S(2)}) collective-permute-start(bf16[160,1280]{1,0:T(8,128)(2,1)S(1)} %constant_dynamic-update-slice_fusion.refs_0_), channel_id=1, source_target_pairs={{0,4},{4,0},{8,12},{12,8},{16,20},{20,16},{24,28},{28,24},{1,5},{5... | collective-permute-start | bytes 1228808 | tf_op jit(solution)/shard_map/ppermute | solution.py:205
  12.0 13.1 %collective-permute-start.4 = (bf16[160,1280]{1,0:T(8,128)(2,1)S(1)}, bf16[160,1280]{1,0:T(8,128)(2,1)S(1)}, u32[]{:S(2)}, u32[]{:S(2)}) collective-permute-start(bf16[160,1280]{1,0:T(8,128)(2,1)S(1)} %constant_dynamic-update-slice_fusion.refs_0_), channel_id=1, source_target_pairs={{8,16},{12,20},{16,8},{20,12},{9,17},{13,21},{17,9},{21,13},{10,18... | collective-permute-start | bytes 1228808 | tf_op jit(solution)/shard_map/ppermute | solution.py:227
  12.7 12.4 %collective-permute-start.3 = (bf16[160,1280]{1,0:T(8,128)(2,1)S(1)}, bf16[160,1280]{1,0:T(8,128)(2,1)S(1)}, u32[]{:S(2)}, u32[]{:S(2)}) collective-permute-start(bf16[160,1280]{1,0:T(8,128)(2,1)S(1)} %constant_dynamic-update-slice_fusion.refs_0_), channel_id=1, source_target_pairs={{0,8},{4,12},{8,0},{12,4},{16,24},{20,28},{24,16},{28,20},{1,9},{5... | collective-permute-start | bytes 1228808 | tf_op jit(solution)/shard_map/ppermute | solution.py:205
  15.8 8.5 %collective-permute-start.6 = (bf16[160,640]{1,0:T(8,128)(2,1)S(1)}, bf16[160,640]{1,0:T(8,128)(2,1)S(1)}, u32[]{:S(2)}, u32[]{:S(2)}) collective-permute-start(bf16[160,640]{1,0:T(8,128)(2,1)S(1)} %pad_maximum_fusion.2), channel_id=1, source_target_pairs={{0,4},{4,0},{8,12},{12,8},{16,20},{20,16},{24,28},{28,24},{1,5},{5... | collective-permute-start | bytes 614408 | tf_op jit(solution)/shard_map/ppermute | solution.py:205
  24.3 0.8 copy-start.2
  25.1 15.4 %copy-start.4 = (bf16[160,1280]{1,0:T(8,128)(2,1)}, bf16[160,1280]{1,0:T(8,128)(2,1)S(1)}, u32[]{:S(2)}) copy-start(bf16[160,1280]{1,0:T(8,128)(2,1)S(1)} %collective-permute-done.3.refs_1_) | copy-start | bytes 1228804
  25.1 11.6 %collective-permute-start.8 = (bf16[160,1280]{1,0:T(8,128)(2,1)S(1)}, bf16[160,1280]{1,0:T(8,128)(2,1)S(1)}, u32[]{:S(2)}, u32[]{:S(2)}) collective-permute-start(bf16[160,1280]{1,0:T(8,128)(2,1)S(1)} %collective-permute-done.4), channel_id=1, source_target_pairs={{8,0},{12,4},{16,24},{20,28},{9,1},{13,5},{17,25},{21,29},{10,2},{... | collective-permute-start | bytes 1228808 | tf_op jit(solution)/shard_map/ppermute | solution.py:227
  26.4 10.3 %collective-permute-start.10 = (bf16[320,640]{1,0:T(8,128)(2,1)S(1)}, bf16[320,640]{1,0:T(8,128)(2,1)S(1)}, u32[]{:S(2)}, u32[]{:S(2)}) collective-permute-start(bf16[320,640]{1,0:T(8,128)(2,1)S(1)} %pad_maximum_fusion.1), channel_id=1, source_target_pairs={{0,2},{1,3},{2,0},{3,1},{4,6},{5,7},{6,4},{7,5},{8,10},{9,11},{10,... | collective-permute-start | bytes 1228808 | tf_op jit(solution)/shard_map/ppermute | solution.py:205
  27.9 9.5 %collective-permute-start.9 = (bf16[160,1280]{1,0:T(8,128)(2,1)S(1)}, bf16[160,1280]{1,0:T(8,128)(2,1)S(1)}, u32[]{:S(2)}, u32[]{:S(2)}) collective-permute-start(bf16[160,1280]{1,0:T(8,128)(2,1)S(1)} %collective-permute-done.3.refs_1_), channel_id=1, source_target_pairs={{0,4},{4,0},{8,12},{12,8},{16,20},{20,16},{24,28},{28,24},{1,5},{5... | collective-permute-start | bytes 1228808 | tf_op jit(solution)/shard_map/ppermute | solution.py:205
  29.5 8.0 %collective-permute-start.7 = (bf16[160,1280]{1,0:T(8,128)(2,1)S(1)}, bf16[160,1280]{1,0:T(8,128)(2,1)}, u32[]{:S(2)}, u32[]{:S(2)}) collective-permute-start(bf16[160,1280]{1,0:T(8,128)(2,1)S(1)} %collective-permute-done.3.refs_1_), channel_id=1, source_target_pairs={{8,16},{12,20},{16,8},{20,12},{9,17},{13,21},{17,9},{21,13},{10,18... | collective-permute-start | bytes 1228808 | tf_op jit(solution)/shard_map/ppermute | solution.py:227
  37.4 3.0 %copy-start.6 = (bf16[160,1280]{1,0:T(8,128)(2,1)}, bf16[160,1280]{1,0:T(8,128)(2,1)S(1)}, u32[]{:S(2)}) copy-start(bf16[160,1280]{1,0:T(8,128)(2,1)S(1)} %collective-permute-done.9.refs_5_) | copy-start | bytes 1228804
  37.5 8.6 %collective-permute-start.13 = (bf16[160,1280]{1,0:T(8,128)(2,1)S(1)}, bf16[160,1280]{1,0:T(8,128)(2,1)}, u32[]{:S(2)}, u32[]{:S(2)}) collective-permute-start(bf16[160,1280]{1,0:T(8,128)(2,1)S(1)} %broadcast_select_fusion.1.refs_2_), channel_id=1, source_target_pairs={{0,4},{4,0},{8,12},{12,8},{16,20},{20,16},{24,28},{28,24},{1,5},{5... | collective-permute-start | bytes 1228808 | tf_op jit(solution)/shard_map/ppermute | solution.py:205
  39.1 12.6 %collective-permute-start.12 = (bf16[160,1280]{1,0:T(8,128)(2,1)}, bf16[160,1280]{1,0:T(8,128)(2,1)}, u32[]{:S(2)}, u32[]{:S(2)}) collective-permute-start(bf16[160,1280]{1,0:T(8,128)(2,1)} %collective-permute-done.7), channel_id=1, source_target_pairs={{8,0},{12,4},{16,24},{20,28},{9,1},{13,5},{17,25},{21,29},{10,2},{... | collective-permute-start | bytes 1228808 | tf_op jit(solution)/shard_map/ppermute | solution.py:227
  40.5 13.8 %copy-start = (bf16[512,512]{1,0:T(8,128)(2,1)S(1)}, bf16[512,512]{1,0:T(8,128)(2,1)}, u32[]{:S(2)}) copy-start(bf16[512,512]{1,0:T(8,128)(2,1)} %refs_11_.1) | copy-start | bytes 1572868
  40.5 13.8 %copy-start.1 = (bf16[512,512]{1,0:T(8,128)(2,1)S(1)}, bf16[512,512]{1,0:T(8,128)(2,1)}, u32[]{:S(2)}) copy-start(bf16[512,512]{1,0:T(8,128)(2,1)} %refs_12_.1) | copy-start | bytes 1572868
  40.5 13.8 %copy-start.8 = (s32[16]{0:T(128)S(1)}, s32[16]{0:T(128)}, u32[]{:S(2)}) copy-start(s32[16]{0:T(128)} %order_ref.3) | copy-start | bytes 196
  40.6 13.7 %collective-permute-start.11 = (bf16[640,640]{1,0:T(8,128)(2,1)S(1)}, bf16[640,640]{1,0:T(8,128)(2,1)S(1)}, u32[]{:S(2)}, u32[]{:S(2)}) collective-permute-start(bf16[640,640]{1,0:T(8,128)(2,1)S(1)} %bitcast.17), channel_id=1, source_target_pairs={{0,1},{1,0},{2,3},{3,2},{4,5},{5,4},{6,7},{7,6},{8,9},{9,8},{10,11... | collective-permute-start | bytes 2457608 | tf_op jit(solution)/shard_map/ppermute | solution.py:205
  52.7 9.0 %copy-start.3 = (bf16[160,1280]{1,0:T(8,128)(2,1)S(1)}, bf16[160,1280]{1,0:T(8,128)(2,1)}, u32[]{:S(2)}) copy-start(bf16[160,1280]{1,0:T(8,128)(2,1)} %copy-done.2) | copy-start | bytes 1228804
  52.7 9.0 %copy-start.5 = (bf16[160,1280]{1,0:T(8,128)(2,1)S(1)}, bf16[160,1280]{1,0:T(8,128)(2,1)}, u32[]{:S(2)}) copy-start(bf16[160,1280]{1,0:T(8,128)(2,1)} %copy-done.4) | copy-start | bytes 1228804
  52.7 9.0 %copy-start.7 = (bf16[160,1280]{1,0:T(8,128)(2,1)S(1)}, bf16[160,1280]{1,0:T(8,128)(2,1)}, u32[]{:S(2)}) copy-start(bf16[160,1280]{1,0:T(8,128)(2,1)} %copy-done.6) | copy-start | bytes 1228804
  52.7 8.9 %collective-permute-start.14 = (bf16[160,1280]{1,0:T(8,128)(2,1)S(1)}, bf16[160,1280]{1,0:T(8,128)(2,1)S(1)}, u32[]{:S(2)}, u32[]{:S(2)}) collective-permute-start(bf16[160,1280]{1,0:T(8,128)(2,1)S(1)} %broadcast_select_fusion.refs_3_), channel_id=1, source_target_pairs={{0,4},{4,0},{8,12},{12,8},{16,20},{20,16},{24,28},{28,24},{1,5},{5... | collective-permute-start | bytes 1228808 | tf_op jit(solution)/shard_map/ppermute | solution.py:205
  75.2 1.5 %collective-permute-start.15 = (bf16[160,576]{1,0:T(8,128)(2,1)S(1)}, bf16[160,576]{1,0:T(8,128)(2,1)S(1)}, u32[]{:S(2)}, u32[]{:S(2)}) collective-permute-start(bf16[160,576]{1,0:T(8,128)(2,1)S(1)} %get-tuple-element.43), channel_id=1, source_target_pairs={{0,1},{1,0},{2,3},{3,2},{4,5},{5,4},{6,7},{7,6},{8,9},{9,8},{10,11... | collective-permute-start | bytes 552968 | tf_op jit(solution)/shard_map/ppermute | solution.py:205
  76.8 7.2 %collective-permute-start.16 = (bf16[160,576]{1,0:T(8,128)(2,1)S(1)}, bf16[160,576]{1,0:T(8,128)(2,1)S(1)}, u32[]{:S(2)}, u32[]{:S(2)}) collective-permute-start(bf16[160,576]{1,0:T(8,128)(2,1)S(1)} %convert_add_fusion.1), channel_id=1, source_target_pairs={{0,2},{1,3},{2,0},{3,1},{4,6},{5,7},{6,4},{7,5},{8,10},{9,11},{10,... | collective-permute-start | bytes 552968 | tf_op jit(solution)/shard_map/ppermute | solution.py:205

commit v6 on v5

--- a/solution.py
+++ b/solution.py
@@ -84,19 +84,22 @@
         seen = (key_pos <= query_pos) & (key_pos >= low_ref[block] * half)
         bias = jnp.where(seen, 0.0, NEG_FILL)
         rows = pl.ds(side * half, half)
-        outs = []
+        opened = []
         for head in range(heads):
             x_ref, at = x_refs[head // pair], head % pair
             query = x_ref[rows, at * WIDTH : (at + 1) * WIDTH]
             grad = x_ref[rows, grad_at + at * VDIM : grad_at + (at + 1) * VDIM]
-            keys = keys_ref[head, window, :]
             values = values_ref[window, head * VDIM : (head + 1) * VDIM]
-            scores = dot(query, keys, BY_COLUMNS) * SCALE_LOG2 + bias
+            scores = dot(query, keys_ref[head, window, :], BY_COLUMNS)
+            opened.append((scores, dot(grad, values, BY_COLUMNS)))
+        outs = []
+        for head, (scores, grad_probs) in enumerate(opened):
+            scores = scores * SCALE_LOG2 + bias
             expo = jnp.exp2(scores - jnp.max(scores, axis=1, keepdims=True))
             probs = expo * (1.0 / jnp.sum(expo, axis=1, keepdims=True))
-            grad_probs = dot(grad, values, BY_COLUMNS)
             delta = jnp.sum(probs * grad_probs, axis=1, keepdims=True)
             grad_scores = (probs * (grad_probs - delta) * SCALE).astype(jnp.bfloat16)
+            keys = keys_ref[head, window, :]
             outs.append(dot(grad_scores, keys, BY_ROWS).astype(jnp.bfloat16))
         dq_ref[rows, :] = jnp.concatenate(outs, axis=1)
 

time: 84.4 us -> 84 us (level)
  Pallas kernels: 20.8 us -> 19.2 us
    pallas_call x1, Pallas kernels: 7.3 us -> 5.69 us  [shards(): pl.pallas_call(functools.partial(project_kernel, devices, half, heads, pa...]
  transfers between devices with their start and end apart: 17 -> 17, of which waited for: 8 -> 9; matrix products, arithmetic and copies ran while one was open for 9% -> 9% of each run, Pallas kernels for 9% -> 7%
where the time goes in v6:
time: 84 us; the launch traced here: 83.9 us
  waiting for transfers between devices  30 us (36%)
  starting transfers between devices  23.9 us (28%)
  Pallas kernels  19.2 us (23%)
  local copies, waits for them, and re-layouts  3.79 us (5%)
  matrix products  3.62 us (4%)
  other arithmetic  2.42 us (3%)
  between operations  0.9 us (1%)
    ppermute x13, starting transfers between devices, swap(): return lax.ppermute(array, axis, [(i, i ^ mask) for i in range(size)])  19.2 us
    ppermute x13, waiting for transfers between devices, swap(): return lax.ppermute(array, axis, [(i, i ^ mask) for i in range(size)])  18.8 us
    pallas_call x1, Pallas kernels, shards(): pl.pallas_call(functools.partial(key_kernel, devices, half, pair, len(sha...  13.5 us
    ppermute x4, waiting for transfers between devices, along(): lax.ppermute(array, 'seq', [(2 * a + y, 2 * b + y) for a, b in pairs for...  11.2 us
    pallas_call x1, Pallas kernels, shards(): pl.pallas_call(functools.partial(project_kernel, devices, half, heads, pa...  5.69 us
    ppermute x4, starting transfers between devices, along(): lax.ppermute(array, 'seq', [(2 * a + y, 2 * b + y) for a, b in pairs for...  4.67 us
    dot_general x2, matrix products, dot(): return lax.dot_general(a, b, dims, preferred_element_type=jnp.float32)  3.62 us
    unnamed x21, local copies, waits for them, and re-layouts  1.76 us
  transfers between devices with their start and end apart: 17, of which 9 were waited for; matrix products, arithmetic and copies ran while one was open for 9% of the time, Pallas kernels for 7%

profile of v6, /device:TPU:0, one launch (start us, length us, event | category | flops | bytes accessed | tf_op | source)
XLA Modules:
  0.0 83.9 jit_solution(7528334245165074533)
XLA Ops:
  0.6 0.0 copy-start.9
  0.7 0.9 %pad_dynamic-slice_fusion = bf16[40,640]{1,0:T(8,128)(2,1)S(1)} fusion(s32[]{:T(128)S(6)} %dynamic_slice.7, bf16[160,576]{1,0:T(8,128)(2,1)} %param.8), kind=kLoop, calls=%fused_computation.9 | loop fusion | bytes 235524 | tf_op jit(solution)/shard_map/dynamic_slice | solution.py:299
  1.5 5.1 %collective-permute-start.2 = (bf16[40,640]{1,0:T(8,128)(2,1)S(1)}, bf16[40,640]{1,0:T(8,128)(2,1)S(1)}, u32[]{:S(2)}, u32[]{:S(2)}) collective-permute-start(bf16[40,640]{1,0:T(8,128)(2,1)S(1)} %pad_dynamic-slice_fusion), channel_id=1, source_target_pairs={{0,24},{4,28},{8,16},{12,20},{16,8},{20,12},{24,0},{28,4},{1,25},{... | collective-permute-start | bytes 153608 | tf_op jit(solution)/shard_map/ppermute | solution.py:208
  6.7 0.0 collective-permute-start.1
  6.7 0.6 collective-permute-start
  7.3 1.0 %constant_dynamic-update-slice_fusion.1 = bf16[160,1280]{1,0:T(8,128)(2,1)S(1)} fusion(bf16[160,768]{1,0:T(8,128)(2,1)} %param.7), kind=kLoop, calls=%fused_computation.12 | loop fusion | bytes 491520
  8.3 0.9 %constant_dynamic-update-slice_fusion.refs_0_ = bf16[160,1280]{1,0:T(8,128)(2,1)S(1)} fusion(bf16[160,1280]{1,0:T(8,128)(2,1)S(1)} %constant_dynamic-update-slice_fusion.1, bf16[160,512]{1,0:T(8,128)(2,1)} %param.11), kind=kLoop, calls=%fused_computation.11 | loop fusion | bytes 327680 | tf_op jit(solution)/shard_map/concatenate | solution.py:284
  9.2 1.7 %collective-permute-start.5 = (bf16[160,1280]{1,0:T(8,128)(2,1)S(1)}, bf16[160,1280]{1,0:T(8,128)(2,1)S(1)}, u32[]{:S(2)}, u32[]{:S(2)}) collective-permute-start(bf16[160,1280]{1,0:T(8,128)(2,1)S(1)} %constant_dynamic-update-slice_fusion.refs_0_), channel_id=1, source_target_pairs={{0,4},{4,0},{8,12},{12,8},{16,20},{20,16},{24,28},{28,24},{1,5},{5... | collective-permute-start | bytes 1228808 | tf_op jit(solution)/shard_map/ppermute | solution.py:208
  10.9 0.0 collective-permute-done.2
  10.9 0.0 collective-permute-done.1
  10.9 1.1 %collective-permute-done = bf16[40,640]{1,0:T(8,128)(2,1)S(1)} collective-permute-done((bf16[40,640]{1,0:T(8,128)(2,1)S(1)}, bf16[40,640]{1,0:T(8,128)(2,1)S(1)}, u32[]{:S(2)}, u32[]{:S(2)}) %collective-permute-start) | collective-permute-done | bytes 51232 | tf_op jit(solution)/shard_map/ppermute | solution.py:208
  12.0 0.7 collective-permute-start.4
  12.7 3.1 %collective-permute-start.3 = (bf16[160,1280]{1,0:T(8,128)(2,1)S(1)}, bf16[160,1280]{1,0:T(8,128)(2,1)S(1)}, u32[]{:S(2)}, u32[]{:S(2)}) collective-permute-start(bf16[160,1280]{1,0:T(8,128)(2,1)S(1)} %constant_dynamic-update-slice_fusion.refs_0_), channel_id=1, source_target_pairs={{0,8},{4,12},{8,0},{12,4},{16,24},{20,28},{24,16},{28,20},{1,9},{5... | collective-permute-start | bytes 1228808 | tf_op jit(solution)/shard_map/ppermute | solution.py:208
  15.8 1.6 %collective-permute-start.6 = (bf16[160,640]{1,0:T(8,128)(2,1)S(1)}, bf16[160,640]{1,0:T(8,128)(2,1)S(1)}, u32[]{:S(2)}, u32[]{:S(2)}) collective-permute-start(bf16[160,640]{1,0:T(8,128)(2,1)S(1)} %pad_maximum_fusion.2), channel_id=1, source_target_pairs={{0,4},{4,0},{8,12},{12,8},{16,20},{20,16},{24,28},{28,24},{1,5},{5... | collective-permute-start | bytes 614408 | tf_op jit(solution)/shard_map/ppermute | solution.py:208
  17.4 6.9 %collective-permute-done.6 = bf16[160,640]{1,0:T(8,128)(2,1)S(1)} collective-permute-done((bf16[160,640]{1,0:T(8,128)(2,1)S(1)}, bf16[160,640]{1,0:T(8,128)(2,1)S(1)}, u32[]{:S(2)}, u32[]{:S(2)}) %collective-permute-start.6) | collective-permute-done | bytes 204832 | tf_op jit(solution)/shard_map/ppermute | solution.py:208
  24.3 0.0 collective-permute-done.5.refs_4_
  24.3 0.0 copy-start.2
  24.4 0.7 copy-done.2
  25.1 0.0 collective-permute-done.4
  25.1 0.0 collective-permute-done.3.refs_1_
  25.1 1.3 %collective-permute-start.8 = (bf16[160,1280]{1,0:T(8,128)(2,1)S(1)}, bf16[160,1280]{1,0:T(8,128)(2,1)S(1)}, u32[]{:S(2)}, u32[]{:S(2)}) collective-permute-start(bf16[160,1280]{1,0:T(8,128)(2,1)S(1)} %collective-permute-done.4), channel_id=1, source_target_pairs={{8,0},{12,4},{16,24},{20,28},{9,1},{13,5},{17,25},{21,29},{10,2},{... | collective-permute-start | bytes 1228808 | tf_op jit(solution)/shard_map/ppermute | solution.py:230
  26.4 1.5 %collective-permute-start.10 = (bf16[320,640]{1,0:T(8,128)(2,1)S(1)}, bf16[320,640]{1,0:T(8,128)(2,1)S(1)}, u32[]{:S(2)}, u32[]{:S(2)}) collective-permute-start(bf16[320,640]{1,0:T(8,128)(2,1)S(1)} %pad_maximum_fusion.1), channel_id=1, source_target_pairs={{0,2},{1,3},{2,0},{3,1},{4,6},{5,7},{6,4},{7,5},{8,10},{9,11},{10,... | collective-permute-start | bytes 1228808 | tf_op jit(solution)/shard_map/ppermute | solution.py:208
  27.9 1.5 %collective-permute-start.9 = (bf16[160,1280]{1,0:T(8,128)(2,1)S(1)}, bf16[160,1280]{1,0:T(8,128)(2,1)S(1)}, u32[]{:S(2)}, u32[]{:S(2)}) collective-permute-start(bf16[160,1280]{1,0:T(8,128)(2,1)S(1)} %collective-permute-done.3.refs_1_), channel_id=1, source_target_pairs={{0,4},{4,0},{8,12},{12,8},{16,20},{20,16},{24,28},{28,24},{1,5},{5... | collective-permute-start | bytes 1228808 | tf_op jit(solution)/shard_map/ppermute | solution.py:208
  29.5 1.4 %collective-permute-start.7 = (bf16[160,1280]{1,0:T(8,128)(2,1)S(1)}, bf16[160,1280]{1,0:T(8,128)(2,1)}, u32[]{:S(2)}, u32[]{:S(2)}) collective-permute-start(bf16[160,1280]{1,0:T(8,128)(2,1)S(1)} %collective-permute-done.3.refs_1_), channel_id=1, source_target_pairs={{8,16},{12,20},{16,8},{20,12},{9,17},{13,21},{17,9},{21,13},{10,18... | collective-permute-start | bytes 1228808 | tf_op jit(solution)/shard_map/ppermute | solution.py:230
  30.9 0.0 copy-done.9
  30.9 0.2 convert_reduce_fusion.low_ref
  31.1 5.7 %collective-permute-done.8 = bf16[160,1280]{1,0:T(8,128)(2,1)S(1)} collective-permute-done((bf16[160,1280]{1,0:T(8,128)(2,1)S(1)}, bf16[160,1280]{1,0:T(8,128)(2,1)S(1)}, u32[]{:S(2)}, u32[]{:S(2)}) %collective-permute-start.8) | collective-permute-done | bytes 409632 | tf_op jit(solution)/shard_map/ppermute | solution.py:230
  36.7 0.0 collective-permute-done.10
  36.7 0.7 collective-permute-done.9.refs_5_
  37.5 0.0 collective-permute-done.7
  37.5 1.6 %collective-permute-start.13 = (bf16[160,1280]{1,0:T(8,128)(2,1)S(1)}, bf16[160,1280]{1,0:T(8,128)(2,1)}, u32[]{:S(2)}, u32[]{:S(2)}) collective-permute-start(bf16[160,1280]{1,0:T(8,128)(2,1)S(1)} %broadcast_select_fusion.1.refs_2_), channel_id=1, source_target_pairs={{0,4},{4,0},{8,12},{12,8},{16,20},{20,16},{24,28},{28,24},{1,5},{5... | collective-permute-start | bytes 1228808 | tf_op jit(solution)/shard_map/ppermute | solution.py:208
  39.1 1.3 %collective-permute-start.12 = (bf16[160,1280]{1,0:T(8,128)(2,1)}, bf16[160,1280]{1,0:T(8,128)(2,1)}, u32[]{:S(2)}, u32[]{:S(2)}) collective-permute-start(bf16[160,1280]{1,0:T(8,128)(2,1)} %collective-permute-done.7), channel_id=1, source_target_pairs={{8,0},{12,4},{16,24},{20,28},{9,1},{13,5},{17,25},{21,29},{10,2},{... | collective-permute-start | bytes 1228808 | tf_op jit(solution)/shard_map/ppermute | solution.py:230
  40.4 0.1 broadcast_select_fusion.3
  40.5 0.0 copy-done.4
  40.5 0.0 copy-start
  40.5 0.0 copy-start.1
  40.5 0.0 copy-start.8
  40.5 0.1 pad_maximum_fusion
  40.6 0.1 collective-permute-start.11
  40.7 0.1 broadcast_in_dim.2
  40.8 0.1 reshape_reshape.3.refs_8_
  40.9 0.1 stack.47.source_ref
  40.9 0.1 pad_add_fusion.where_ref
  41.0 5.1 %collective-permute-done.13.refs_6_ = bf16[160,1280]{1,0:T(8,128)(2,1)} collective-permute-done((bf16[160,1280]{1,0:T(8,128)(2,1)S(1)}, bf16[160,1280]{1,0:T(8,128)(2,1)}, u32[]{:S(2)}, u32[]{:S(2)}) %collective-permute-start.13) | collective-permute-done | bytes 409632 | tf_op jit(solution)/shard_map/ppermute | solution.py:208
  46.1 5.6 %collective-permute-done.12 = bf16[160,1280]{1,0:T(8,128)(2,1)} collective-permute-done((bf16[160,1280]{1,0:T(8,128)(2,1)}, bf16[160,1280]{1,0:T(8,128)(2,1)}, u32[]{:S(2)}, u32[]{:S(2)}) %collective-permute-start.12) | collective-permute-done | bytes 409632 | tf_op jit(solution)/shard_map/ppermute | solution.py:230
  51.7 1.0 %broadcast_select_fusion.refs_3_ = bf16[160,1280]{1,0:T(8,128)(2,1)S(1)} fusion(bf16[160,1280]{1,0:T(8,128)(2,1)} %collective-permute-done.7, bf16[160,1280]{1,0:T(8,128)(2,1)} %collective-permute-done.12, pred[]{:T(512)S(6)} %or.3), kind=kLoop, calls=%fused_computation.4 | loop fusion | flops 204800 | bytes 1228801 | tf_op jit(solution)/shard_map/jit(_where)/select_n | solution.py:262
  52.7 0.0 copy-start.3
  52.7 0.0 copy-start.5
  52.7 0.0 copy-start.7
  52.7 1.6 %collective-permute-start.14 = (bf16[160,1280]{1,0:T(8,128)(2,1)S(1)}, bf16[160,1280]{1,0:T(8,128)(2,1)S(1)}, u32[]{:S(2)}, u32[]{:S(2)}) collective-permute-start(bf16[160,1280]{1,0:T(8,128)(2,1)S(1)} %broadcast_select_fusion.refs_3_), channel_id=1, source_target_pairs={{0,4},{4,0},{8,12},{12,8},{16,20},{20,16},{24,28},{28,24},{1,5},{5... | collective-permute-start | bytes 1228808 | tf_op jit(solution)/shard_map/ppermute | solution.py:208
  54.3 0.0 collective-permute-done.11.other_ref
  54.3 0.0 copy-done.8
  54.3 5.7 %project.1 = (bf16[4,1280,192]{2,1,0:T(8,128)(2,1)S(1)}, bf16[1280,512]{1,0:T(8,128)(2,1)S(1)}, bf16[512,1280]{1,0:T(8,128)(2,1)S(1)}, bf16[160,768]{1,0:T(8,128)(2,1)}) custom-call(s32[16]{0:T(128)S(1)} %copy-done.8, s32[16]{0:T(128)S(1)} %convert_reduce_fusion.low_ref, s32[2]{0:T(128)S(1)} %pad_add_fusion.where_ref, bf16[640,640]{1,0:T(8,128)(2,1)S(1)} %bitcast.18, ...), custom_call_target="tpu_custom_call" | custom-call | flops 21474836480 | bytes 16777216 | tf_op jit(solution)/shard_map/project/pallas_call | solution.py:317
  60.0 0.7 collective-permute-done.14.refs_7_
  60.8 0.0 copy-done.7
  60.8 13.5 %keys.1 = (bf16[1280,512]{1,0:T(8,128)(2,1)S(1)}, bf16[1280,512]{1,0:T(8,128)(2,1)S(1)}, bf16[160,576]{1,0:T(8,128)(2,1)S(1)}) custom-call(s32[16]{0:T(128)S(1)} %convert_reduce_fusion.low_ref, s32[16]{0:T(128)S(1)} %copy-done.8, s32[8]{0:T(128)S(1)} %stack.47.source_ref, bf16[160,1280]{1,0:T(8,128)(2,1)S(1)} %constant_dynamic-update-slice_fusion.refs_0_, ...), custom_call_target="tpu_custom_call" | custom-call | flops 21474836480 | bytes 16777216 | tf_op jit(solution)/shard_map/keys/pallas_call | solution.py:347
  74.3 0.1 collective-permute-start.15
  74.4 1.4 %collective-permute-done.15 = bf16[160,576]{1,0:T(8,128)(2,1)S(1)} collective-permute-done((bf16[160,576]{1,0:T(8,128)(2,1)S(1)}, bf16[160,576]{1,0:T(8,128)(2,1)S(1)}, u32[]{:S(2)}, u32[]{:S(2)}) %collective-permute-start.15) | collective-permute-done | bytes 184352 | tf_op jit(solution)/shard_map/ppermute | solution.py:208
  75.8 0.1 convert_add_fusion.1
  75.9 0.7 collective-permute-start.16
  76.5 1.8 %fusion = f32[512,512]{1,0:T(8,128)} fusion(bf16[512,1280]{1,0:T(8,128)(2,1)S(1)} %get-tuple-element.47, bf16[1280,512]{1,0:T(8,128)(2,1)S(1)} %get-tuple-element.48), kind=kOutput, calls=%fused_computation.15 | convolution fusion | flops 671088640 | bytes 3670016 | tf_op jit(solution)/shard_map/dot_general | solution.py:30
  78.3 1.8 %fusion.1 = f32[512,512]{1,0:T(8,128)} fusion(bf16[512,1280]{1,0:T(8,128)(2,1)S(1)} %get-tuple-element.47, bf16[1280,512]{1,0:T(8,128)(2,1)S(1)} %get-tuple-element.49), kind=kOutput, calls=%fused_computation.16 | convolution fusion | flops 671088640 | bytes 3670016 | tf_op jit(solution)/shard_map/dot_general | solution.py:30
  80.1 2.9 %collective-permute-done.16 = bf16[160,576]{1,0:T(8,128)(2,1)S(1)} collective-permute-done((bf16[160,576]{1,0:T(8,128)(2,1)S(1)}, bf16[160,576]{1,0:T(8,128)(2,1)S(1)}, u32[]{:S(2)}, u32[]{:S(2)}) %collective-permute-start.16) | collective-permute-done | bytes 184352 | tf_op jit(solution)/shard_map/ppermute | solution.py:208
  83.0 0.8 convert_add_fusion
  (11 shorter events, 0.1 us)
Async XLA Ops:
  0.6 30.2 %copy-start.9 = (s32[16]{0:T(128)S(1)}, s32[16]{0:T(128)}, u32[]{:S(2)}) copy-start(s32[16]{0:T(128)} %param.13) | copy-start | bytes 196
  1.5 9.4 %collective-permute-start.2 = (bf16[40,640]{1,0:T(8,128)(2,1)S(1)}, bf16[40,640]{1,0:T(8,128)(2,1)S(1)}, u32[]{:S(2)}, u32[]{:S(2)}) collective-permute-start(bf16[40,640]{1,0:T(8,128)(2,1)S(1)} %pad_dynamic-slice_fusion), channel_id=1, source_target_pairs={{0,24},{4,28},{8,16},{12,20},{16,8},{20,12},{24,0},{28,4},{1,25},{... | collective-permute-start | bytes 153608 | tf_op jit(solution)/shard_map/ppermute | solution.py:208
  6.7 4.3 %collective-permute-start.1 = (bf16[40,640]{1,0:T(8,128)(2,1)S(1)}, bf16[40,640]{1,0:T(8,128)(2,1)S(1)}, u32[]{:S(2)}, u32[]{:S(2)}) collective-permute-start(bf16[40,640]{1,0:T(8,128)(2,1)S(1)} %pad_dynamic-slice_fusion), channel_id=1, source_target_pairs={{0,8},{4,12},{8,0},{12,4},{16,24},{20,28},{24,16},{28,20},{1,9},{5... | collective-permute-start | bytes 153608 | tf_op jit(solution)/shard_map/ppermute | solution.py:208
  6.7 5.3 %collective-permute-start = (bf16[40,640]{1,0:T(8,128)(2,1)S(1)}, bf16[40,640]{1,0:T(8,128)(2,1)S(1)}, u32[]{:S(2)}, u32[]{:S(2)}) collective-permute-start(bf16[40,640]{1,0:T(8,128)(2,1)S(1)} %pad_dynamic-slice_fusion), channel_id=1, source_target_pairs={{0,16},{4,20},{8,24},{12,28},{16,0},{20,4},{24,8},{28,12},{1,17},{... | collective-permute-start | bytes 153608 | tf_op jit(solution)/shard_map/ppermute | solution.py:208
  9.2 15.1 %collective-permute-start.5 = (bf16[160,1280]{1,0:T(8,128)(2,1)S(1)}, bf16[160,1280]{1,0:T(8,128)(2,1)S(1)}, u32[]{:S(2)}, u32[]{:S(2)}) collective-permute-start(bf16[160,1280]{1,0:T(8,128)(2,1)S(1)} %constant_dynamic-update-slice_fusion.refs_0_), channel_id=1, source_target_pairs={{0,4},{4,0},{8,12},{12,8},{16,20},{20,16},{24,28},{28,24},{1,5},{5... | collective-permute-start | bytes 1228808 | tf_op jit(solution)/shard_map/ppermute | solution.py:208
  12.0 13.1 %collective-permute-start.4 = (bf16[160,1280]{1,0:T(8,128)(2,1)S(1)}, bf16[160,1280]{1,0:T(8,128)(2,1)S(1)}, u32[]{:S(2)}, u32[]{:S(2)}) collective-permute-start(bf16[160,1280]{1,0:T(8,128)(2,1)S(1)} %constant_dynamic-update-slice_fusion.refs_0_), channel_id=1, source_target_pairs={{8,16},{12,20},{16,8},{20,12},{9,17},{13,21},{17,9},{21,13},{10,18... | collective-permute-start | bytes 1228808 | tf_op jit(solution)/shard_map/ppermute | solution.py:230
  12.7 12.4 %collective-permute-start.3 = (bf16[160,1280]{1,0:T(8,128)(2,1)S(1)}, bf16[160,1280]{1,0:T(8,128)(2,1)S(1)}, u32[]{:S(2)}, u32[]{:S(2)}) collective-permute-start(bf16[160,1280]{1,0:T(8,128)(2,1)S(1)} %constant_dynamic-update-slice_fusion.refs_0_), channel_id=1, source_target_pairs={{0,8},{4,12},{8,0},{12,4},{16,24},{20,28},{24,16},{28,20},{1,9},{5... | collective-permute-start | bytes 1228808 | tf_op jit(solution)/shard_map/ppermute | solution.py:208
  15.8 8.5 %collective-permute-start.6 = (bf16[160,640]{1,0:T(8,128)(2,1)S(1)}, bf16[160,640]{1,0:T(8,128)(2,1)S(1)}, u32[]{:S(2)}, u32[]{:S(2)}) collective-permute-start(bf16[160,640]{1,0:T(8,128)(2,1)S(1)} %pad_maximum_fusion.2), channel_id=1, source_target_pairs={{0,4},{4,0},{8,12},{12,8},{16,20},{20,16},{24,28},{28,24},{1,5},{5... | collective-permute-start | bytes 614408 | tf_op jit(solution)/shard_map/ppermute | solution.py:208
  24.3 0.8 copy-start.2
  25.1 15.4 %copy-start.4 = (bf16[160,1280]{1,0:T(8,128)(2,1)}, bf16[160,1280]{1,0:T(8,128)(2,1)S(1)}, u32[]{:S(2)}) copy-start(bf16[160,1280]{1,0:T(8,128)(2,1)S(1)} %collective-permute-done.3.refs_1_) | copy-start | bytes 1228804
  25.1 11.6 %collective-permute-start.8 = (bf16[160,1280]{1,0:T(8,128)(2,1)S(1)}, bf16[160,1280]{1,0:T(8,128)(2,1)S(1)}, u32[]{:S(2)}, u32[]{:S(2)}) collective-permute-start(bf16[160,1280]{1,0:T(8,128)(2,1)S(1)} %collective-permute-done.4), channel_id=1, source_target_pairs={{8,0},{12,4},{16,24},{20,28},{9,1},{13,5},{17,25},{21,29},{10,2},{... | collective-permute-start | bytes 1228808 | tf_op jit(solution)/shard_map/ppermute | solution.py:230
  26.4 10.3 %collective-permute-start.10 = (bf16[320,640]{1,0:T(8,128)(2,1)S(1)}, bf16[320,640]{1,0:T(8,128)(2,1)S(1)}, u32[]{:S(2)}, u32[]{:S(2)}) collective-permute-start(bf16[320,640]{1,0:T(8,128)(2,1)S(1)} %pad_maximum_fusion.1), channel_id=1, source_target_pairs={{0,2},{1,3},{2,0},{3,1},{4,6},{5,7},{6,4},{7,5},{8,10},{9,11},{10,... | collective-permute-start | bytes 1228808 | tf_op jit(solution)/shard_map/ppermute | solution.py:208
  27.9 9.5 %collective-permute-start.9 = (bf16[160,1280]{1,0:T(8,128)(2,1)S(1)}, bf16[160,1280]{1,0:T(8,128)(2,1)S(1)}, u32[]{:S(2)}, u32[]{:S(2)}) collective-permute-start(bf16[160,1280]{1,0:T(8,128)(2,1)S(1)} %collective-permute-done.3.refs_1_), channel_id=1, source_target_pairs={{0,4},{4,0},{8,12},{12,8},{16,20},{20,16},{24,28},{28,24},{1,5},{5... | collective-permute-start | bytes 1228808 | tf_op jit(solution)/shard_map/ppermute | solution.py:208
  29.5 8.0 %collective-permute-start.7 = (bf16[160,1280]{1,0:T(8,128)(2,1)S(1)}, bf16[160,1280]{1,0:T(8,128)(2,1)}, u32[]{:S(2)}, u32[]{:S(2)}) collective-permute-start(bf16[160,1280]{1,0:T(8,128)(2,1)S(1)} %collective-permute-done.3.refs_1_), channel_id=1, source_target_pairs={{8,16},{12,20},{16,8},{20,12},{9,17},{13,21},{17,9},{21,13},{10,18... | collective-permute-start | bytes 1228808 | tf_op jit(solution)/shard_map/ppermute | solution.py:230
  37.4 3.0 %copy-start.6 = (bf16[160,1280]{1,0:T(8,128)(2,1)}, bf16[160,1280]{1,0:T(8,128)(2,1)S(1)}, u32[]{:S(2)}) copy-start(bf16[160,1280]{1,0:T(8,128)(2,1)S(1)} %collective-permute-done.9.refs_5_) | copy-start | bytes 1228804
  37.5 8.6 %collective-permute-start.13 = (bf16[160,1280]{1,0:T(8,128)(2,1)S(1)}, bf16[160,1280]{1,0:T(8,128)(2,1)}, u32[]{:S(2)}, u32[]{:S(2)}) collective-permute-start(bf16[160,1280]{1,0:T(8,128)(2,1)S(1)} %broadcast_select_fusion.1.refs_2_), channel_id=1, source_target_pairs={{0,4},{4,0},{8,12},{12,8},{16,20},{20,16},{24,28},{28,24},{1,5},{5... | collective-permute-start | bytes 1228808 | tf_op jit(solution)/shard_map/ppermute | solution.py:208
  39.1 12.6 %collective-permute-start.12 = (bf16[160,1280]{1,0:T(8,128)(2,1)}, bf16[160,1280]{1,0:T(8,128)(2,1)}, u32[]{:S(2)}, u32[]{:S(2)}) collective-permute-start(bf16[160,1280]{1,0:T(8,128)(2,1)} %collective-permute-done.7), channel_id=1, source_target_pairs={{8,0},{12,4},{16,24},{20,28},{9,1},{13,5},{17,25},{21,29},{10,2},{... | collective-permute-start | bytes 1228808 | tf_op jit(solution)/shard_map/ppermute | solution.py:230
  40.5 13.8 %copy-start = (bf16[512,512]{1,0:T(8,128)(2,1)S(1)}, bf16[512,512]{1,0:T(8,128)(2,1)}, u32[]{:S(2)}) copy-start(bf16[512,512]{1,0:T(8,128)(2,1)} %refs_11_.1) | copy-start | bytes 1572868
  40.5 13.8 %copy-start.1 = (bf16[512,512]{1,0:T(8,128)(2,1)S(1)}, bf16[512,512]{1,0:T(8,128)(2,1)}, u32[]{:S(2)}) copy-start(bf16[512,512]{1,0:T(8,128)(2,1)} %refs_12_.1) | copy-start | bytes 1572868
  40.5 13.8 %copy-start.8 = (s32[16]{0:T(128)S(1)}, s32[16]{0:T(128)}, u32[]{:S(2)}) copy-start(s32[16]{0:T(128)} %order_ref.3) | copy-start | bytes 196
  40.6 13.7 %collective-permute-start.11 = (bf16[640,640]{1,0:T(8,128)(2,1)S(1)}, bf16[640,640]{1,0:T(8,128)(2,1)S(1)}, u32[]{:S(2)}, u32[]{:S(2)}) collective-permute-start(bf16[640,640]{1,0:T(8,128)(2,1)S(1)} %bitcast.17), channel_id=1, source_target_pairs={{0,1},{1,0},{2,3},{3,2},{4,5},{5,4},{6,7},{7,6},{8,9},{9,8},{10,11... | collective-permute-start | bytes 2457608 | tf_op jit(solution)/shard_map/ppermute | solution.py:208
  52.7 8.1 %copy-start.3 = (bf16[160,1280]{1,0:T(8,128)(2,1)S(1)}, bf16[160,1280]{1,0:T(8,128)(2,1)}, u32[]{:S(2)}) copy-start(bf16[160,1280]{1,0:T(8,128)(2,1)} %copy-done.2) | copy-start | bytes 1228804
  52.7 8.0 %copy-start.5 = (bf16[160,1280]{1,0:T(8,128)(2,1)S(1)}, bf16[160,1280]{1,0:T(8,128)(2,1)}, u32[]{:S(2)}) copy-start(bf16[160,1280]{1,0:T(8,128)(2,1)} %copy-done.4) | copy-start | bytes 1228804
  52.7 8.0 %copy-start.7 = (bf16[160,1280]{1,0:T(8,128)(2,1)S(1)}, bf16[160,1280]{1,0:T(8,128)(2,1)}, u32[]{:S(2)}) copy-start(bf16[160,1280]{1,0:T(8,128)(2,1)} %copy-done.6) | copy-start | bytes 1228804
  52.7 8.0 %collective-permute-start.14 = (bf16[160,1280]{1,0:T(8,128)(2,1)S(1)}, bf16[160,1280]{1,0:T(8,128)(2,1)S(1)}, u32[]{:S(2)}, u32[]{:S(2)}) collective-permute-start(bf16[160,1280]{1,0:T(8,128)(2,1)S(1)} %broadcast_select_fusion.refs_3_), channel_id=1, source_target_pairs={{0,4},{4,0},{8,12},{12,8},{16,20},{20,16},{24,28},{28,24},{1,5},{5... | collective-permute-start | bytes 1228808 | tf_op jit(solution)/shard_map/ppermute | solution.py:208
  74.3 1.5 %collective-permute-start.15 = (bf16[160,576]{1,0:T(8,128)(2,1)S(1)}, bf16[160,576]{1,0:T(8,128)(2,1)S(1)}, u32[]{:S(2)}, u32[]{:S(2)}) collective-permute-start(bf16[160,576]{1,0:T(8,128)(2,1)S(1)} %get-tuple-element.43), channel_id=1, source_target_pairs={{0,1},{1,0},{2,3},{3,2},{4,5},{5,4},{6,7},{7,6},{8,9},{9,8},{10,11... | collective-permute-start | bytes 552968 | tf_op jit(solution)/shard_map/ppermute | solution.py:208
  75.9 7.2 %collective-permute-start.16 = (bf16[160,576]{1,0:T(8,128)(2,1)S(1)}, bf16[160,576]{1,0:T(8,128)(2,1)S(1)}, u32[]{:S(2)}, u32[]{:S(2)}) collective-permute-start(bf16[160,576]{1,0:T(8,128)(2,1)S(1)} %convert_add_fusion.1), channel_id=1, source_target_pairs={{0,2},{1,3},{2,0},{3,1},{4,6},{5,7},{6,4},{7,5},{8,10},{9,11},{10,... | collective-permute-start | bytes 552968 | tf_op jit(solution)/shard_map/ppermute | solution.py:208

commit v7 on v6

--- a/solution.py
+++ b/solution.py
@@ -162,9 +162,13 @@
             return key_grad[:, NOPE:]
 
         rope = 0.0
-        opened = [begin(head) for head in range(here)]
-        for head in range(here):
-            rope = rope + end(*middle(*opened[head]))
+        weighed = None
+        for opened in [begin(head) for head in range(here)]:
+            following = middle(*opened)
+            if weighed is not None:
+                rope = rope + end(*weighed)
+            weighed = following
+        rope = rope + end(*weighed)
         sum_rope[window, :] += rope
 
     def step(number, carry):

time: 84 us -> 83.2 us (level)
  Pallas kernels: 19.2 us -> 17.7 us
    pallas_call x1, Pallas kernels: 13.5 us -> 12 us  [shards(): pl.pallas_call(functools.partial(key_kernel, devices, half, pair, len(sha...]
where the time goes in v7:
time: 83.2 us; the launch traced here: 82.4 us
  waiting for transfers between devices  30 us (36%)
  starting transfers between devices  23.9 us (29%)
  Pallas kernels  17.7 us (21%)
  local copies, waits for them, and re-layouts  3.79 us (5%)
  matrix products  3.62 us (4%)
  other arithmetic  2.42 us (3%)
  between operations  0.9 us (1%)
    ppermute x13, starting transfers between devices, swap(): return lax.ppermute(array, axis, [(i, i ^ mask) for i in range(size)])  19.2 us
    ppermute x13, waiting for transfers between devices, swap(): return lax.ppermute(array, axis, [(i, i ^ mask) for i in range(size)])  18.8 us
    pallas_call x1, Pallas kernels, shards(): pl.pallas_call(functools.partial(key_kernel, devices, half, pair, len(sha...  12 us
    ppermute x4, waiting for transfers between devices, along(): lax.ppermute(array, 'seq', [(2 * a + y, 2 * b + y) for a, b in pairs for...  11.2 us
    pallas_call x1, Pallas kernels, shards(): pl.pallas_call(functools.partial(project_kernel, devices, half, heads, pa...  5.69 us
    ppermute x4, starting transfers between devices, along(): lax.ppermute(array, 'seq', [(2 * a + y, 2 * b + y) for a, b in pairs for...  4.67 us
    dot_general x2, matrix products, dot(): return lax.dot_general(a, b, dims, preferred_element_type=jnp.float32)  3.62 us
    unnamed x21, local copies, waits for them, and re-layouts  1.76 us
  transfers between devices with their start and end apart: 17, of which 9 were waited for; matrix products, arithmetic and copies ran while one was open for 9% of the time, Pallas kernels for 7%

profile of v7, /device:TPU:0, one launch (start us, length us, event | category | flops | bytes accessed | tf_op | source)
XLA Modules:
  0.0 82.4 jit_solution(947598003085274966)
XLA Ops:
  0.6 0.0 copy-start.9
  0.7 0.9 %pad_dynamic-slice_fusion = bf16[40,640]{1,0:T(8,128)(2,1)S(1)} fusion(s32[]{:T(128)S(6)} %dynamic_slice.7, bf16[160,576]{1,0:T(8,128)(2,1)} %param.8), kind=kLoop, calls=%fused_computation.9 | loop fusion | bytes 235524 | tf_op jit(solution)/shard_map/dynamic_slice | solution.py:303
  1.5 5.1 %collective-permute-start.2 = (bf16[40,640]{1,0:T(8,128)(2,1)S(1)}, bf16[40,640]{1,0:T(8,128)(2,1)S(1)}, u32[]{:S(2)}, u32[]{:S(2)}) collective-permute-start(bf16[40,640]{1,0:T(8,128)(2,1)S(1)} %pad_dynamic-slice_fusion), channel_id=1, source_target_pairs={{0,24},{4,28},{8,16},{12,20},{16,8},{20,12},{24,0},{28,4},{1,25},{... | collective-permute-start | bytes 153608 | tf_op jit(solution)/shard_map/ppermute | solution.py:212
  6.7 0.0 collective-permute-start.1
  6.7 0.6 collective-permute-start
  7.3 1.0 %constant_dynamic-update-slice_fusion.1 = bf16[160,1280]{1,0:T(8,128)(2,1)S(1)} fusion(bf16[160,768]{1,0:T(8,128)(2,1)} %param.7), kind=kLoop, calls=%fused_computation.12 | loop fusion | bytes 491520
  8.3 0.9 %constant_dynamic-update-slice_fusion.refs_0_ = bf16[160,1280]{1,0:T(8,128)(2,1)S(1)} fusion(bf16[160,1280]{1,0:T(8,128)(2,1)S(1)} %constant_dynamic-update-slice_fusion.1, bf16[160,512]{1,0:T(8,128)(2,1)} %param.11), kind=kLoop, calls=%fused_computation.11 | loop fusion | bytes 327680 | tf_op jit(solution)/shard_map/concatenate | solution.py:288
  9.2 1.7 %collective-permute-start.5 = (bf16[160,1280]{1,0:T(8,128)(2,1)S(1)}, bf16[160,1280]{1,0:T(8,128)(2,1)S(1)}, u32[]{:S(2)}, u32[]{:S(2)}) collective-permute-start(bf16[160,1280]{1,0:T(8,128)(2,1)S(1)} %constant_dynamic-update-slice_fusion.refs_0_), channel_id=1, source_target_pairs={{0,4},{4,0},{8,12},{12,8},{16,20},{20,16},{24,28},{28,24},{1,5},{5... | collective-permute-start | bytes 1228808 | tf_op jit(solution)/shard_map/ppermute | solution.py:212
  10.9 0.0 collective-permute-done.2
  10.9 0.0 collective-permute-done.1
  10.9 1.1 %collective-permute-done = bf16[40,640]{1,0:T(8,128)(2,1)S(1)} collective-permute-done((bf16[40,640]{1,0:T(8,128)(2,1)S(1)}, bf16[40,640]{1,0:T(8,128)(2,1)S(1)}, u32[]{:S(2)}, u32[]{:S(2)}) %collective-permute-start) | collective-permute-done | bytes 51232 | tf_op jit(solution)/shard_map/ppermute | solution.py:212
  12.0 0.7 collective-permute-start.4
  12.7 3.1 %collective-permute-start.3 = (bf16[160,1280]{1,0:T(8,128)(2,1)S(1)}, bf16[160,1280]{1,0:T(8,128)(2,1)S(1)}, u32[]{:S(2)}, u32[]{:S(2)}) collective-permute-start(bf16[160,1280]{1,0:T(8,128)(2,1)S(1)} %constant_dynamic-update-slice_fusion.refs_0_), channel_id=1, source_target_pairs={{0,8},{4,12},{8,0},{12,4},{16,24},{20,28},{24,16},{28,20},{1,9},{5... | collective-permute-start | bytes 1228808 | tf_op jit(solution)/shard_map/ppermute | solution.py:212
  15.8 1.6 %collective-permute-start.6 = (bf16[160,640]{1,0:T(8,128)(2,1)S(1)}, bf16[160,640]{1,0:T(8,128)(2,1)S(1)}, u32[]{:S(2)}, u32[]{:S(2)}) collective-permute-start(bf16[160,640]{1,0:T(8,128)(2,1)S(1)} %pad_maximum_fusion.2), channel_id=1, source_target_pairs={{0,4},{4,0},{8,12},{12,8},{16,20},{20,16},{24,28},{28,24},{1,5},{5... | collective-permute-start | bytes 614408 | tf_op jit(solution)/shard_map/ppermute | solution.py:212
  17.4 6.9 %collective-permute-done.6 = bf16[160,640]{1,0:T(8,128)(2,1)S(1)} collective-permute-done((bf16[160,640]{1,0:T(8,128)(2,1)S(1)}, bf16[160,640]{1,0:T(8,128)(2,1)S(1)}, u32[]{:S(2)}, u32[]{:S(2)}) %collective-permute-start.6) | collective-permute-done | bytes 204832 | tf_op jit(solution)/shard_map/ppermute | solution.py:212
  24.3 0.0 collective-permute-done.5.refs_4_
  24.3 0.0 copy-start.2
  24.4 0.7 copy-done.2
  25.1 0.0 collective-permute-done.4
  25.1 0.0 collective-permute-done.3.refs_1_
  25.1 1.3 %collective-permute-start.8 = (bf16[160,1280]{1,0:T(8,128)(2,1)S(1)}, bf16[160,1280]{1,0:T(8,128)(2,1)S(1)}, u32[]{:S(2)}, u32[]{:S(2)}) collective-permute-start(bf16[160,1280]{1,0:T(8,128)(2,1)S(1)} %collective-permute-done.4), channel_id=1, source_target_pairs={{8,0},{12,4},{16,24},{20,28},{9,1},{13,5},{17,25},{21,29},{10,2},{... | collective-permute-start | bytes 1228808 | tf_op jit(solution)/shard_map/ppermute | solution.py:234
  26.4 1.5 %collective-permute-start.10 = (bf16[320,640]{1,0:T(8,128)(2,1)S(1)}, bf16[320,640]{1,0:T(8,128)(2,1)S(1)}, u32[]{:S(2)}, u32[]{:S(2)}) collective-permute-start(bf16[320,640]{1,0:T(8,128)(2,1)S(1)} %pad_maximum_fusion.1), channel_id=1, source_target_pairs={{0,2},{1,3},{2,0},{3,1},{4,6},{5,7},{6,4},{7,5},{8,10},{9,11},{10,... | collective-permute-start | bytes 1228808 | tf_op jit(solution)/shard_map/ppermute | solution.py:212
  27.9 1.5 %collective-permute-start.9 = (bf16[160,1280]{1,0:T(8,128)(2,1)S(1)}, bf16[160,1280]{1,0:T(8,128)(2,1)S(1)}, u32[]{:S(2)}, u32[]{:S(2)}) collective-permute-start(bf16[160,1280]{1,0:T(8,128)(2,1)S(1)} %collective-permute-done.3.refs_1_), channel_id=1, source_target_pairs={{0,4},{4,0},{8,12},{12,8},{16,20},{20,16},{24,28},{28,24},{1,5},{5... | collective-permute-start | bytes 1228808 | tf_op jit(solution)/shard_map/ppermute | solution.py:212
  29.5 1.4 %collective-permute-start.7 = (bf16[160,1280]{1,0:T(8,128)(2,1)S(1)}, bf16[160,1280]{1,0:T(8,128)(2,1)}, u32[]{:S(2)}, u32[]{:S(2)}) collective-permute-start(bf16[160,1280]{1,0:T(8,128)(2,1)S(1)} %collective-permute-done.3.refs_1_), channel_id=1, source_target_pairs={{8,16},{12,20},{16,8},{20,12},{9,17},{13,21},{17,9},{21,13},{10,18... | collective-permute-start | bytes 1228808 | tf_op jit(solution)/shard_map/ppermute | solution.py:234
  30.9 0.0 copy-done.9
  30.9 0.2 convert_reduce_fusion.low_ref
  31.1 5.7 %collective-permute-done.8 = bf16[160,1280]{1,0:T(8,128)(2,1)S(1)} collective-permute-done((bf16[160,1280]{1,0:T(8,128)(2,1)S(1)}, bf16[160,1280]{1,0:T(8,128)(2,1)S(1)}, u32[]{:S(2)}, u32[]{:S(2)}) %collective-permute-start.8) | collective-permute-done | bytes 409632 | tf_op jit(solution)/shard_map/ppermute | solution.py:234
  36.7 0.0 collective-permute-done.10
  36.7 0.7 collective-permute-done.9.refs_5_
  37.5 0.0 collective-permute-done.7
  37.5 1.6 %collective-permute-start.13 = (bf16[160,1280]{1,0:T(8,128)(2,1)S(1)}, bf16[160,1280]{1,0:T(8,128)(2,1)}, u32[]{:S(2)}, u32[]{:S(2)}) collective-permute-start(bf16[160,1280]{1,0:T(8,128)(2,1)S(1)} %broadcast_select_fusion.1.refs_2_), channel_id=1, source_target_pairs={{0,4},{4,0},{8,12},{12,8},{16,20},{20,16},{24,28},{28,24},{1,5},{5... | collective-permute-start | bytes 1228808 | tf_op jit(solution)/shard_map/ppermute | solution.py:212
  39.1 1.3 %collective-permute-start.12 = (bf16[160,1280]{1,0:T(8,128)(2,1)}, bf16[160,1280]{1,0:T(8,128)(2,1)}, u32[]{:S(2)}, u32[]{:S(2)}) collective-permute-start(bf16[160,1280]{1,0:T(8,128)(2,1)} %collective-permute-done.7), channel_id=1, source_target_pairs={{8,0},{12,4},{16,24},{20,28},{9,1},{13,5},{17,25},{21,29},{10,2},{... | collective-permute-start | bytes 1228808 | tf_op jit(solution)/shard_map/ppermute | solution.py:234
  40.4 0.1 broadcast_select_fusion.3
  40.5 0.0 copy-done.4
  40.5 0.0 copy-start
  40.5 0.0 copy-start.1
  40.5 0.0 copy-start.8
  40.5 0.1 pad_maximum_fusion
  40.6 0.1 collective-permute-start.11
  40.7 0.1 broadcast_in_dim.2
  40.8 0.1 reshape_reshape.3.refs_8_
  40.9 0.1 stack.47.source_ref
  40.9 0.1 pad_add_fusion.where_ref
  41.0 5.1 %collective-permute-done.13.refs_6_ = bf16[160,1280]{1,0:T(8,128)(2,1)} collective-permute-done((bf16[160,1280]{1,0:T(8,128)(2,1)S(1)}, bf16[160,1280]{1,0:T(8,128)(2,1)}, u32[]{:S(2)}, u32[]{:S(2)}) %collective-permute-start.13) | collective-permute-done | bytes 409632 | tf_op jit(solution)/shard_map/ppermute | solution.py:212
  46.1 5.6 %collective-permute-done.12 = bf16[160,1280]{1,0:T(8,128)(2,1)} collective-permute-done((bf16[160,1280]{1,0:T(8,128)(2,1)}, bf16[160,1280]{1,0:T(8,128)(2,1)}, u32[]{:S(2)}, u32[]{:S(2)}) %collective-permute-start.12) | collective-permute-done | bytes 409632 | tf_op jit(solution)/shard_map/ppermute | solution.py:234
  51.7 1.0 %broadcast_select_fusion.refs_3_ = bf16[160,1280]{1,0:T(8,128)(2,1)S(1)} fusion(bf16[160,1280]{1,0:T(8,128)(2,1)} %collective-permute-done.7, bf16[160,1280]{1,0:T(8,128)(2,1)} %collective-permute-done.12, pred[]{:T(512)S(6)} %or.3), kind=kLoop, calls=%fused_computation.4 | loop fusion | flops 204800 | bytes 1228801 | tf_op jit(solution)/shard_map/jit(_where)/select_n | solution.py:266
  52.7 0.0 copy-start.3
  52.7 0.0 copy-start.5
  52.7 0.0 copy-start.7
  52.7 1.6 %collective-permute-start.14 = (bf16[160,1280]{1,0:T(8,128)(2,1)S(1)}, bf16[160,1280]{1,0:T(8,128)(2,1)S(1)}, u32[]{:S(2)}, u32[]{:S(2)}) collective-permute-start(bf16[160,1280]{1,0:T(8,128)(2,1)S(1)} %broadcast_select_fusion.refs_3_), channel_id=1, source_target_pairs={{0,4},{4,0},{8,12},{12,8},{16,20},{20,16},{24,28},{28,24},{1,5},{5... | collective-permute-start | bytes 1228808 | tf_op jit(solution)/shard_map/ppermute | solution.py:212
  54.3 0.0 collective-permute-done.11.other_ref
  54.3 0.0 copy-done
  54.3 5.7 %project.1 = (bf16[4,1280,192]{2,1,0:T(8,128)(2,1)S(1)}, bf16[1280,512]{1,0:T(8,128)(2,1)S(1)}, bf16[512,1280]{1,0:T(8,128)(2,1)S(1)}, bf16[160,768]{1,0:T(8,128)(2,1)}) custom-call(s32[16]{0:T(128)S(1)} %copy-done.8, s32[16]{0:T(128)S(1)} %convert_reduce_fusion.low_ref, s32[2]{0:T(128)S(1)} %pad_add_fusion.where_ref, bf16[640,640]{1,0:T(8,128)(2,1)S(1)} %bitcast.18, ...), custom_call_target="tpu_custom_call" | custom-call | flops 21474836480 | bytes 16777216 | tf_op jit(solution)/shard_map/project/pallas_call | solution.py:321
  60.0 0.7 collective-permute-done.14.refs_7_
  60.8 0.0 copy-done.7
  60.8 12.0 %keys.1 = (bf16[1280,512]{1,0:T(8,128)(2,1)S(1)}, bf16[1280,512]{1,0:T(8,128)(2,1)S(1)}, bf16[160,576]{1,0:T(8,128)(2,1)S(1)}) custom-call(s32[16]{0:T(128)S(1)} %convert_reduce_fusion.low_ref, s32[16]{0:T(128)S(1)} %copy-done.8, s32[8]{0:T(128)S(1)} %stack.47.source_ref, bf16[160,1280]{1,0:T(8,128)(2,1)S(1)} %constant_dynamic-update-slice_fusion.refs_0_, ...), custom_call_target="tpu_custom_call" | custom-call | flops 21474836480 | bytes 16777216 | tf_op jit(solution)/shard_map/keys/pallas_call | solution.py:351
  72.8 0.1 collective-permute-start.15
  72.9 1.4 %collective-permute-done.15 = bf16[160,576]{1,0:T(8,128)(2,1)S(1)} collective-permute-done((bf16[160,576]{1,0:T(8,128)(2,1)S(1)}, bf16[160,576]{1,0:T(8,128)(2,1)S(1)}, u32[]{:S(2)}, u32[]{:S(2)}) %collective-permute-start.15) | collective-permute-done | bytes 184352 | tf_op jit(solution)/shard_map/ppermute | solution.py:212
  74.3 0.1 convert_add_fusion.1
  74.4 0.7 collective-permute-start.16
  75.0 1.8 %fusion = f32[512,512]{1,0:T(8,128)} fusion(bf16[512,1280]{1,0:T(8,128)(2,1)S(1)} %get-tuple-element.47, bf16[1280,512]{1,0:T(8,128)(2,1)S(1)} %get-tuple-element.48), kind=kOutput, calls=%fused_computation.15 | convolution fusion | flops 671088640 | bytes 3670016 | tf_op jit(solution)/shard_map/dot_general | solution.py:30
  76.8 1.8 %fusion.1 = f32[512,512]{1,0:T(8,128)} fusion(bf16[512,1280]{1,0:T(8,128)(2,1)S(1)} %get-tuple-element.47, bf16[1280,512]{1,0:T(8,128)(2,1)S(1)} %get-tuple-element.49), kind=kOutput, calls=%fused_computation.16 | convolution fusion | flops 671088640 | bytes 3670016 | tf_op jit(solution)/shard_map/dot_general | solution.py:30
  78.7 2.9 %collective-permute-done.16 = bf16[160,576]{1,0:T(8,128)(2,1)S(1)} collective-permute-done((bf16[160,576]{1,0:T(8,128)(2,1)S(1)}, bf16[160,576]{1,0:T(8,128)(2,1)S(1)}, u32[]{:S(2)}, u32[]{:S(2)}) %collective-permute-start.16) | collective-permute-done | bytes 184352 | tf_op jit(solution)/shard_map/ppermute | solution.py:212
  81.6 0.8 convert_add_fusion
  (11 shorter events, 0.1 us)
Async XLA Ops:
  0.6 30.2 %copy-start.9 = (s32[16]{0:T(128)S(1)}, s32[16]{0:T(128)}, u32[]{:S(2)}) copy-start(s32[16]{0:T(128)} %param.13) | copy-start | bytes 196
  1.5 9.4 %collective-permute-start.2 = (bf16[40,640]{1,0:T(8,128)(2,1)S(1)}, bf16[40,640]{1,0:T(8,128)(2,1)S(1)}, u32[]{:S(2)}, u32[]{:S(2)}) collective-permute-start(bf16[40,640]{1,0:T(8,128)(2,1)S(1)} %pad_dynamic-slice_fusion), channel_id=1, source_target_pairs={{0,24},{4,28},{8,16},{12,20},{16,8},{20,12},{24,0},{28,4},{1,25},{... | collective-permute-start | bytes 153608 | tf_op jit(solution)/shard_map/ppermute | solution.py:212
  6.7 4.3 %collective-permute-start.1 = (bf16[40,640]{1,0:T(8,128)(2,1)S(1)}, bf16[40,640]{1,0:T(8,128)(2,1)S(1)}, u32[]{:S(2)}, u32[]{:S(2)}) collective-permute-start(bf16[40,640]{1,0:T(8,128)(2,1)S(1)} %pad_dynamic-slice_fusion), channel_id=1, source_target_pairs={{0,8},{4,12},{8,0},{12,4},{16,24},{20,28},{24,16},{28,20},{1,9},{5... | collective-permute-start | bytes 153608 | tf_op jit(solution)/shard_map/ppermute | solution.py:212
  6.7 5.3 %collective-permute-start = (bf16[40,640]{1,0:T(8,128)(2,1)S(1)}, bf16[40,640]{1,0:T(8,128)(2,1)S(1)}, u32[]{:S(2)}, u32[]{:S(2)}) collective-permute-start(bf16[40,640]{1,0:T(8,128)(2,1)S(1)} %pad_dynamic-slice_fusion), channel_id=1, source_target_pairs={{0,16},{4,20},{8,24},{12,28},{16,0},{20,4},{24,8},{28,12},{1,17},{... | collective-permute-start | bytes 153608 | tf_op jit(solution)/shard_map/ppermute | solution.py:212
  9.2 15.1 %collective-permute-start.5 = (bf16[160,1280]{1,0:T(8,128)(2,1)S(1)}, bf16[160,1280]{1,0:T(8,128)(2,1)S(1)}, u32[]{:S(2)}, u32[]{:S(2)}) collective-permute-start(bf16[160,1280]{1,0:T(8,128)(2,1)S(1)} %constant_dynamic-update-slice_fusion.refs_0_), channel_id=1, source_target_pairs={{0,4},{4,0},{8,12},{12,8},{16,20},{20,16},{24,28},{28,24},{1,5},{5... | collective-permute-start | bytes 1228808 | tf_op jit(solution)/shard_map/ppermute | solution.py:212
  12.0 13.1 %collective-permute-start.4 = (bf16[160,1280]{1,0:T(8,128)(2,1)S(1)}, bf16[160,1280]{1,0:T(8,128)(2,1)S(1)}, u32[]{:S(2)}, u32[]{:S(2)}) collective-permute-start(bf16[160,1280]{1,0:T(8,128)(2,1)S(1)} %constant_dynamic-update-slice_fusion.refs_0_), channel_id=1, source_target_pairs={{8,16},{12,20},{16,8},{20,12},{9,17},{13,21},{17,9},{21,13},{10,18... | collective-permute-start | bytes 1228808 | tf_op jit(solution)/shard_map/ppermute | solution.py:234
  12.7 12.4 %collective-permute-start.3 = (bf16[160,1280]{1,0:T(8,128)(2,1)S(1)}, bf16[160,1280]{1,0:T(8,128)(2,1)S(1)}, u32[]{:S(2)}, u32[]{:S(2)}) collective-permute-start(bf16[160,1280]{1,0:T(8,128)(2,1)S(1)} %constant_dynamic-update-slice_fusion.refs_0_), channel_id=1, source_target_pairs={{0,8},{4,12},{8,0},{12,4},{16,24},{20,28},{24,16},{28,20},{1,9},{5... | collective-permute-start | bytes 1228808 | tf_op jit(solution)/shard_map/ppermute | solution.py:212
  15.8 8.5 %collective-permute-start.6 = (bf16[160,640]{1,0:T(8,128)(2,1)S(1)}, bf16[160,640]{1,0:T(8,128)(2,1)S(1)}, u32[]{:S(2)}, u32[]{:S(2)}) collective-permute-start(bf16[160,640]{1,0:T(8,128)(2,1)S(1)} %pad_maximum_fusion.2), channel_id=1, source_target_pairs={{0,4},{4,0},{8,12},{12,8},{16,20},{20,16},{24,28},{28,24},{1,5},{5... | collective-permute-start | bytes 614408 | tf_op jit(solution)/shard_map/ppermute | solution.py:212
  24.3 0.8 copy-start.2
  25.1 15.4 %copy-start.4 = (bf16[160,1280]{1,0:T(8,128)(2,1)}, bf16[160,1280]{1,0:T(8,128)(2,1)S(1)}, u32[]{:S(2)}) copy-start(bf16[160,1280]{1,0:T(8,128)(2,1)S(1)} %collective-permute-done.3.refs_1_) | copy-start | bytes 1228804
  25.1 11.6 %collective-permute-start.8 = (bf16[160,1280]{1,0:T(8,128)(2,1)S(1)}, bf16[160,1280]{1,0:T(8,128)(2,1)S(1)}, u32[]{:S(2)}, u32[]{:S(2)}) collective-permute-start(bf16[160,1280]{1,0:T(8,128)(2,1)S(1)} %collective-permute-done.4), channel_id=1, source_target_pairs={{8,0},{12,4},{16,24},{20,28},{9,1},{13,5},{17,25},{21,29},{10,2},{... | collective-permute-start | bytes 1228808 | tf_op jit(solution)/shard_map/ppermute | solution.py:234
  26.4 10.3 %collective-permute-start.10 = (bf16[320,640]{1,0:T(8,128)(2,1)S(1)}, bf16[320,640]{1,0:T(8,128)(2,1)S(1)}, u32[]{:S(2)}, u32[]{:S(2)}) collective-permute-start(bf16[320,640]{1,0:T(8,128)(2,1)S(1)} %pad_maximum_fusion.1), channel_id=1, source_target_pairs={{0,2},{1,3},{2,0},{3,1},{4,6},{5,7},{6,4},{7,5},{8,10},{9,11},{10,... | collective-permute-start | bytes 1228808 | tf_op jit(solution)/shard_map/ppermute | solution.py:212
  27.9 9.5 %collective-permute-start.9 = (bf16[160,1280]{1,0:T(8,128)(2,1)S(1)}, bf16[160,1280]{1,0:T(8,128)(2,1)S(1)}, u32[]{:S(2)}, u32[]{:S(2)}) collective-permute-start(bf16[160,1280]{1,0:T(8,128)(2,1)S(1)} %collective-permute-done.3.refs_1_), channel_id=1, source_target_pairs={{0,4},{4,0},{8,12},{12,8},{16,20},{20,16},{24,28},{28,24},{1,5},{5... | collective-permute-start | bytes 1228808 | tf_op jit(solution)/shard_map/ppermute | solution.py:212
  29.5 8.0 %collective-permute-start.7 = (bf16[160,1280]{1,0:T(8,128)(2,1)S(1)}, bf16[160,1280]{1,0:T(8,128)(2,1)}, u32[]{:S(2)}, u32[]{:S(2)}) collective-permute-start(bf16[160,1280]{1,0:T(8,128)(2,1)S(1)} %collective-permute-done.3.refs_1_), channel_id=1, source_target_pairs={{8,16},{12,20},{16,8},{20,12},{9,17},{13,21},{17,9},{21,13},{10,18... | collective-permute-start | bytes 1228808 | tf_op jit(solution)/shard_map/ppermute | solution.py:234
  37.4 3.0 %copy-start.6 = (bf16[160,1280]{1,0:T(8,128)(2,1)}, bf16[160,1280]{1,0:T(8,128)(2,1)S(1)}, u32[]{:S(2)}) copy-start(bf16[160,1280]{1,0:T(8,128)(2,1)S(1)} %collective-permute-done.9.refs_5_) | copy-start | bytes 1228804
  37.5 8.6 %collective-permute-start.13 = (bf16[160,1280]{1,0:T(8,128)(2,1)S(1)}, bf16[160,1280]{1,0:T(8,128)(2,1)}, u32[]{:S(2)}, u32[]{:S(2)}) collective-permute-start(bf16[160,1280]{1,0:T(8,128)(2,1)S(1)} %broadcast_select_fusion.1.refs_2_), channel_id=1, source_target_pairs={{0,4},{4,0},{8,12},{12,8},{16,20},{20,16},{24,28},{28,24},{1,5},{5... | collective-permute-start | bytes 1228808 | tf_op jit(solution)/shard_map/ppermute | solution.py:212
  39.1 12.6 %collective-permute-start.12 = (bf16[160,1280]{1,0:T(8,128)(2,1)}, bf16[160,1280]{1,0:T(8,128)(2,1)}, u32[]{:S(2)}, u32[]{:S(2)}) collective-permute-start(bf16[160,1280]{1,0:T(8,128)(2,1)} %collective-permute-done.7), channel_id=1, source_target_pairs={{8,0},{12,4},{16,24},{20,28},{9,1},{13,5},{17,25},{21,29},{10,2},{... | collective-permute-start | bytes 1228808 | tf_op jit(solution)/shard_map/ppermute | solution.py:234
  40.5 13.8 %copy-start = (bf16[512,512]{1,0:T(8,128)(2,1)S(1)}, bf16[512,512]{1,0:T(8,128)(2,1)}, u32[]{:S(2)}) copy-start(bf16[512,512]{1,0:T(8,128)(2,1)} %refs_11_.1) | copy-start | bytes 1572868
  40.5 13.8 %copy-start.1 = (bf16[512,512]{1,0:T(8,128)(2,1)S(1)}, bf16[512,512]{1,0:T(8,128)(2,1)}, u32[]{:S(2)}) copy-start(bf16[512,512]{1,0:T(8,128)(2,1)} %refs_12_.1) | copy-start | bytes 1572868
  40.5 13.8 %copy-start.8 = (s32[16]{0:T(128)S(1)}, s32[16]{0:T(128)}, u32[]{:S(2)}) copy-start(s32[16]{0:T(128)} %order_ref.3) | copy-start | bytes 196
  40.6 13.7 %collective-permute-start.11 = (bf16[640,640]{1,0:T(8,128)(2,1)S(1)}, bf16[640,640]{1,0:T(8,128)(2,1)S(1)}, u32[]{:S(2)}, u32[]{:S(2)}) collective-permute-start(bf16[640,640]{1,0:T(8,128)(2,1)S(1)} %bitcast.17), channel_id=1, source_target_pairs={{0,1},{1,0},{2,3},{3,2},{4,5},{5,4},{6,7},{7,6},{8,9},{9,8},{10,11... | collective-permute-start | bytes 2457608 | tf_op jit(solution)/shard_map/ppermute | solution.py:212
  52.7 8.1 %copy-start.3 = (bf16[160,1280]{1,0:T(8,128)(2,1)S(1)}, bf16[160,1280]{1,0:T(8,128)(2,1)}, u32[]{:S(2)}) copy-start(bf16[160,1280]{1,0:T(8,128)(2,1)} %copy-done.2) | copy-start | bytes 1228804
  52.7 8.0 %copy-start.5 = (bf16[160,1280]{1,0:T(8,128)(2,1)S(1)}, bf16[160,1280]{1,0:T(8,128)(2,1)}, u32[]{:S(2)}) copy-start(bf16[160,1280]{1,0:T(8,128)(2,1)} %copy-done.4) | copy-start | bytes 1228804
  52.7 8.0 %copy-start.7 = (bf16[160,1280]{1,0:T(8,128)(2,1)S(1)}, bf16[160,1280]{1,0:T(8,128)(2,1)}, u32[]{:S(2)}) copy-start(bf16[160,1280]{1,0:T(8,128)(2,1)} %copy-done.6) | copy-start | bytes 1228804
  52.7 8.0 %collective-permute-start.14 = (bf16[160,1280]{1,0:T(8,128)(2,1)S(1)}, bf16[160,1280]{1,0:T(8,128)(2,1)S(1)}, u32[]{:S(2)}, u32[]{:S(2)}) collective-permute-start(bf16[160,1280]{1,0:T(8,128)(2,1)S(1)} %broadcast_select_fusion.refs_3_), channel_id=1, source_target_pairs={{0,4},{4,0},{8,12},{12,8},{16,20},{20,16},{24,28},{28,24},{1,5},{5... | collective-permute-start | bytes 1228808 | tf_op jit(solution)/shard_map/ppermute | solution.py:212
  72.8 1.5 %collective-permute-start.15 = (bf16[160,576]{1,0:T(8,128)(2,1)S(1)}, bf16[160,576]{1,0:T(8,128)(2,1)S(1)}, u32[]{:S(2)}, u32[]{:S(2)}) collective-permute-start(bf16[160,576]{1,0:T(8,128)(2,1)S(1)} %get-tuple-element.43), channel_id=1, source_target_pairs={{0,1},{1,0},{2,3},{3,2},{4,5},{5,4},{6,7},{7,6},{8,9},{9,8},{10,11... | collective-permute-start | bytes 552968 | tf_op jit(solution)/shard_map/ppermute | solution.py:212
  74.4 7.2 %collective-permute-start.16 = (bf16[160,576]{1,0:T(8,128)(2,1)S(1)}, bf16[160,576]{1,0:T(8,128)(2,1)S(1)}, u32[]{:S(2)}, u32[]{:S(2)}) collective-permute-start(bf16[160,576]{1,0:T(8,128)(2,1)S(1)} %convert_add_fusion.1), channel_id=1, source_target_pairs={{0,2},{1,3},{2,0},{3,1},{4,6},{5,7},{6,4},{7,5},{8,10},{9,11},{10,... | collective-permute-start | bytes 552968 | tf_op jit(solution)/shard_map/ppermute | solution.py:212
